TPU v7x, 32 devices: a whole 2x2x4 slice. The times are simulated.
32 devices in a mesh: dp: 16 (over z, y, core), tensor: 2 (over x).
Axes of the slice: x: 2, y: 2, z: 4, core: 2. Of those that a mesh axis runs over, the one named last changes fastest.
Arguments:
- tokens: bfloat16 [4096, 2048], P(('dp', 'tensor')), may hold values from -6 to 6
- attention_gain: bfloat16 [2048], P(('dp', 'tensor')), may hold values from 0.5 to 1.5
- expert_norm_gain: bfloat16 [2048], P(('dp', 'tensor')), may hold values from 0.5 to 1.5
- query_projection: bfloat16 [2048, 2048], P('dp', 'tensor'), may hold values from -0.125 to 0.125
- key_projection: bfloat16 [2048, 512], P('dp', 'tensor'), may hold values from -0.125 to 0.125
- value_projection: bfloat16 [2048, 512], P('dp', 'tensor'), may hold values from -0.125 to 0.125
- output_projection: bfloat16 [2048, 2048], P('tensor', 'dp'), may hold values from -0.5 to 0.5
- router: bfloat16 [2048, 16], P(('dp', 'tensor')), may hold values from -0.0625 to 0.0625
- shared_gate_matrix: bfloat16 [2048, 2816], P('dp', 'tensor'), may hold values from -0.125 to 0.125
- shared_up_matrix: bfloat16 [2048, 2816], P('dp', 'tensor'), may hold values from -0.125 to 0.125
- shared_down_matrix: bfloat16 [2816, 2048], P('tensor', 'dp'), may hold values from -0.109375 to 0.109375
- expert_gate_matrix: bfloat16 [16, 2048, 1408], P('dp', None, 'tensor'), may hold values from -0.125 to 0.125
- expert_up_matrix: bfloat16 [16, 2048, 1408], P('dp', None, 'tensor'), may hold values from -0.125 to 0.125
- expert_down_matrix: bfloat16 [16, 1408, 2048], P('dp', 'tensor'), may hold values from -0.15625 to 0.15625
- document_lengths: int32 [16, 4], P('dp'), may hold values from 1 to 160, 256 in all within a row
- expert_indices: int32 [4096, 6], P('dp'), may hold values from 0 to 15, all different within a row; in each aligned block of 256 rows (0 to 255, 256 to 511, ...) at most 128 rows name the same one
- cotangent: bfloat16 [4096, 2048], P(('dp', 'tensor')), may hold values from -6 to 6
Outputs:
- output: bfloat16 [4096, 2048], P(('dp', 'tensor'))
- grad_tokens: float32 [4096, 2048], P(('dp', 'tensor'))
- grad_gain_attn: float32 [2048], P(('dp', 'tensor'))
- grad_gain_ffn: float32 [2048], P(('dp', 'tensor'))
- grad_w_query: float32 [2048, 2048], P('dp', 'tensor')
- grad_w_key: float32 [2048, 512], P('dp', 'tensor')
- grad_w_value: float32 [2048, 512], P('dp', 'tensor')
- grad_w_out: float32 [2048, 2048], P('tensor', 'dp')
- grad_router: float32 [2048, 16], P(('dp', 'tensor'))
- grad_w_sgate: float32 [2048, 2816], P('dp', 'tensor')
- grad_w_sup: float32 [2048, 2816], P('dp', 'tensor')
- grad_w_sdown: float32 [2816, 2048], P('tensor', 'dp')
- grad_w_egate: float32 [16, 2048, 1408], P('dp', None, 'tensor')
- grad_w_eup: float32 [16, 2048, 1408], P('dp', None, 'tensor')
- grad_w_edown: float32 [16, 1408, 2048], P('dp', 'tensor')
Inputs may be any that keep to these rules, and one draw needn't show every extreme that they name: `expert_indices`: each row names 6 different experts; in each aligned block of 256 rows (one sequence) no expert is named by more than 128 rows. `document_lengths`: each row sums to 256.
All inputs are finite; a program needn't handle non-finite values.
Results may differ from a plain program's by a relative error of at most 0.017.
Values may be sent and summed in bfloat16 or wider, within the bound.
A program may use at most 256 MiB of HBM per device.

v0:
```python
import math

import jax
import jax.numpy as jnp
from jax import lax
from jax.sharding import PartitionSpec as P

HEAD_SIZE = 128


norm_eps = 1e-06
rope_base = 600000.0
neg_big = -1e30


def silu(argument):
    return argument * jax.nn.sigmoid(argument)


def silu_slope(argument):
    sigmoid_of = jax.nn.sigmoid(argument)
    return sigmoid_of * (1.0 + argument * (1.0 - sigmoid_of))


def rotation(sequence_length, head_dim):
    half_dim = head_dim // 2
    frequency = jnp.exp(
        jnp.arange(half_dim, dtype=jnp.float32) * (-2.0 * math.log(rope_base) / head_dim)
    )
    angles = jnp.arange(sequence_length, dtype=jnp.float32)[:, None] * frequency[None, :]
    return (jnp.cos(angles), jnp.sin(angles))


def apply_rotary(tensor, rotary_cosine, rotary_sine):
    half_dim = tensor.shape[-1] // 2
    first_half = tensor[..., :half_dim]
    second_half = tensor[..., half_dim:]
    cos_rows = rotary_cosine[:, None, :]
    sin_rows = rotary_sine[:, None, :]
    return jnp.concatenate(
        [
            first_half * cos_rows - second_half * sin_rows,
            second_half * cos_rows + first_half * sin_rows,
        ],
        axis=-1,
    )


def rotate_back(tensor, rotary_cosine, rotary_sine):
    return apply_rotary(tensor, rotary_cosine, -rotary_sine)


def rms_back(grad_normed, source, scale_rows, gain_full):
    weighted = grad_normed * gain_full
    cubed = scale_rows * scale_rows * scale_rows
    grad_source = scale_rows * weighted - source * cubed * jnp.mean(
        source * weighted, axis=-1, keepdims=True
    )
    grad_gain = jnp.sum(grad_normed * source * scale_rows, axis=0)
    return (grad_source, grad_gain)


def widen(sharded):
    return lax.all_gather(sharded, "tensor", axis=0, tiled=True)


def narrow(partial_sum):
    return lax.psum_scatter(partial_sum, "tensor", scatter_dimension=0, tiled=True)


def dense_fetch(
    query_projection,
    key_projection,
    value_projection,
    output_projection,
    shared_gate_matrix,
    shared_up_matrix,
    shared_down_matrix,
):
    return (
        lax.all_gather(query_projection, "dp", axis=0, tiled=True),
        lax.all_gather(key_projection, "dp", axis=0, tiled=True),
        lax.all_gather(value_projection, "dp", axis=0, tiled=True),
        lax.all_gather(output_projection, "dp", axis=1, tiled=True),
        lax.all_gather(shared_gate_matrix, "dp", axis=0, tiled=True),
        lax.all_gather(shared_up_matrix, "dp", axis=0, tiled=True),
        lax.all_gather(shared_down_matrix, "dp", axis=1, tiled=True),
    )


def expert_up_output(received_rows, expert_gate_matrix, expert_up_matrix, expert_down_matrix):
    gate_preactivation = jnp.einsum(
        "miwy,iyh->miwh", received_rows, expert_gate_matrix, preferred_element_type=jnp.float32
    )
    up_preactivation = jnp.einsum(
        "miwy,iyh->miwh", received_rows, expert_up_matrix, preferred_element_type=jnp.float32
    )
    hidden = (silu(gate_preactivation) * up_preactivation).astype(jnp.bfloat16)
    produced_rows = jnp.einsum(
        "sxcf,xfd->sxcd", hidden, expert_down_matrix, preferred_element_type=jnp.float32
    ).astype(jnp.bfloat16)
    return (produced_rows, gate_preactivation, up_preactivation)


def expert_gradients(
    received,
    received_gradient,
    gate_preactivation,
    up_preactivation,
    expert_gate_matrix,
    expert_up_matrix,
    expert_down_matrix,
):
    hidden_expert = (silu(gate_preactivation) * up_preactivation).astype(jnp.bfloat16)
    expert_down_gradient = jnp.einsum(
        "sxcf,sxcd->xfd", hidden_expert, received_gradient, preferred_element_type=jnp.float32
    )
    grad_hidden_e = jnp.einsum(
        "sxcd,xfd->sxcf", received_gradient, expert_down_matrix, preferred_element_type=jnp.float32
    )
    grad_gate_e = (grad_hidden_e * up_preactivation * silu_slope(gate_preactivation)).astype(
        jnp.bfloat16
    )
    expert_up_hidden_gradient = (grad_hidden_e * silu(gate_preactivation)).astype(jnp.bfloat16)
    expert_gate_gradient = jnp.einsum(
        "gayi,gayr->air", received, grad_gate_e, preferred_element_type=jnp.float32
    )
    expert_up_gradient = jnp.einsum(
        "gayi,gayr->air", received, expert_up_hidden_gradient, preferred_element_type=jnp.float32
    )
    output_rows_gradient = (
        jnp.einsum(
            "zkjh,klh->zkjl", grad_gate_e, expert_gate_matrix, preferred_element_type=jnp.float32
        )
        + jnp.einsum(
            "zkjh,klh->zkjl",
            expert_up_hidden_gradient,
            expert_up_matrix,
            preferred_element_type=jnp.float32,
        )
    ).astype(jnp.bfloat16)
    return (expert_gate_gradient, expert_up_gradient, expert_down_gradient, output_rows_gradient)


def shards(
    tokens,
    attention_gain,
    expert_norm_gain,
    query_projection,
    key_projection,
    value_projection,
    output_projection,
    router,
    shared_gate_matrix,
    shared_up_matrix,
    shared_down_matrix,
    expert_gate_matrix,
    expert_up_matrix,
    expert_down_matrix,
    document_lengths,
    expert_indices,
    cotangent,
):
    n_tensor = lax.axis_size("tensor")
    n_dp = lax.axis_size("dp")
    tensor_pos = lax.axis_index("tensor")
    own_rows = tokens.shape[0]
    sequence_length = own_rows * n_tensor
    model_dim = tokens.shape[1]
    exp_dev = expert_gate_matrix.shape[0]
    experts = exp_dev * n_dp
    top_k = expert_indices.shape[1]
    capacity = max(2, sequence_length * top_k * 4 // (3 * experts))
    slot_total = experts * capacity
    router_full, gain_first, gain_second = (
        lax.all_gather(router, ("dp", "tensor"), axis=0, tiled=True),
        lax.all_gather(attention_gain, ("dp", "tensor"), axis=0, tiled=True),
        lax.all_gather(expert_norm_gain, ("dp", "tensor"), axis=0, tiled=True),
    )
    first_gain = gain_first.astype(jnp.float32)
    second_gain = gain_second.astype(jnp.float32)
    fetched = dense_fetch(
        query_projection,
        key_projection,
        value_projection,
        output_projection,
        shared_gate_matrix,
        shared_up_matrix,
        shared_down_matrix,
    )
    query_all, key_all, value_all, out_all, sgate_all, sup_all, sdown_all = fetched
    input_values = tokens.astype(jnp.float32)
    scale_one = lax.rsqrt(jnp.mean(input_values * input_values, axis=-1, keepdims=True) + norm_eps)
    normed_one = (input_values * scale_one * first_gain).astype(jnp.bfloat16)
    full_one = widen(normed_one)
    q_heads = query_all.shape[1] // HEAD_SIZE
    kv_heads = key_all.shape[1] // HEAD_SIZE
    group_size = q_heads // kv_heads
    rotary_cosine, rotary_sine = rotation(sequence_length, HEAD_SIZE)
    query_unrotated = jnp.dot(full_one, query_all, preferred_element_type=jnp.float32).reshape(
        sequence_length, q_heads, HEAD_SIZE
    )
    key_unrotated = jnp.dot(full_one, key_all, preferred_element_type=jnp.float32).reshape(
        sequence_length, kv_heads, HEAD_SIZE
    )
    rows_of_query = (
        apply_rotary(query_unrotated, rotary_cosine, rotary_sine)
        .astype(jnp.bfloat16)
        .reshape(sequence_length, kv_heads, group_size, HEAD_SIZE)
    )
    key_rows = apply_rotary(key_unrotated, rotary_cosine, rotary_sine).astype(jnp.bfloat16)
    rows_of_value = (
        jnp.dot(full_one, value_all, preferred_element_type=jnp.float32)
        .astype(jnp.bfloat16)
        .reshape(sequence_length, kv_heads, HEAD_SIZE)
    )
    doc_ends = jnp.cumsum(document_lengths[0])
    positions = jnp.arange(sequence_length, dtype=jnp.int32)
    doc_ids = jnp.sum((positions[:, None] >= doc_ends[None, :]).astype(jnp.int32), axis=-1)
    score_scale = HEAD_SIZE ** (-0.5)

    def block_scores(start_row, end_row):
        scores = (
            jnp.einsum(
                "qkgd,skd->kgqs", rows_of_query, key_rows, preferred_element_type=jnp.float32
            )
            * score_scale
        )
        allowed = (doc_ids[start_row:end_row, None] == doc_ids[None, :end_row]) & (
            positions[start_row:end_row, None] >= positions[None, :end_row]
        )
        return (scores, allowed)

    block_index = 0
    start_row = block_index * sequence_length
    end_row = start_row + sequence_length
    scores, allowed = block_scores(start_row, end_row)
    scores = jnp.where(allowed, scores, neg_big)
    row_max = jnp.max(scores, axis=-1, keepdims=True)
    exp_scores = jnp.exp(scores - row_max)
    row_sum = jnp.sum(exp_scores, axis=-1, keepdims=True)
    lse_blocks = [row_max + jnp.log(row_sum)]
    attn_probs = (exp_scores / row_sum).astype(jnp.bfloat16)
    out_blocks = jnp.einsum(
        "kgqs,skd->qkgd", attn_probs, rows_of_value, preferred_element_type=jnp.float32
    )
    mixed_heads = out_blocks.reshape(sequence_length, q_heads * HEAD_SIZE).astype(jnp.bfloat16)
    attn_part = jnp.dot(mixed_heads, out_all, preferred_element_type=jnp.float32)
    residual = input_values + narrow(attn_part)
    scale_two = lax.rsqrt(jnp.mean(residual * residual, axis=-1, keepdims=True) + norm_eps)
    normed_two = (residual * scale_two * second_gain).astype(jnp.bfloat16)
    full_two = widen(normed_two)
    logits = jnp.dot(full_two, router_full, preferred_element_type=jnp.float32)
    chosen = expert_indices[:, :, None] == jnp.arange(experts, dtype=jnp.int32)[None, None, :]
    selected = jnp.sum(jnp.where(chosen, logits[:, None, :], 0.0), axis=-1)
    top_max = jnp.max(selected, axis=-1, keepdims=True)
    gate_exp = jnp.exp(selected - top_max)
    gate_probs = gate_exp / jnp.sum(gate_exp, axis=-1, keepdims=True)
    gate_shared = jnp.dot(full_two, sgate_all, preferred_element_type=jnp.float32)
    up_shared = jnp.dot(full_two, sup_all, preferred_element_type=jnp.float32)
    hidden_shared = (silu(gate_shared) * up_shared).astype(jnp.bfloat16)
    shared_part = jnp.dot(hidden_shared, sdown_all, preferred_element_type=jnp.float32)
    flat_ids = expert_indices.reshape(-1)
    onehot = (flat_ids[:, None] == jnp.arange(experts, dtype=jnp.int32)[None, :]).astype(jnp.int32)
    slot_rank = jnp.sum(onehot * (jnp.cumsum(onehot, axis=0) - 1), axis=-1)
    slot_index = flat_ids * capacity + slot_rank
    pair_index = jnp.arange(sequence_length * top_k, dtype=jnp.int32)
    token_of_slot = jnp.zeros((slot_total,), jnp.int32).at[slot_index].set(pair_index // top_k)
    slot_used = jnp.zeros((slot_total,), jnp.bool_).at[slot_index].set(True)
    gate_of_slot = jnp.zeros((slot_total,), jnp.float32).at[slot_index].set(gate_probs.reshape(-1))
    outgoing = jnp.where(slot_used[:, None], full_two[token_of_slot], 0).reshape(
        n_dp, exp_dev, capacity, model_dim
    )
    received_rows = lax.all_to_all(outgoing, "dp", split_axis=0, concat_axis=0, tiled=True)
    produced_rows, gate_preactivation, up_preactivation = expert_up_output(
        received_rows, expert_gate_matrix, expert_up_matrix, expert_down_matrix
    )
    sent_home = lax.all_to_all(produced_rows, "dp", split_axis=0, concat_axis=0, tiled=True)
    returned, received, gate_preactivation, up_preactivation = (
        sent_home,
        received_rows,
        gate_preactivation,
        up_preactivation,
    )
    picked = returned.reshape(slot_total, model_dim)[slot_index].reshape(
        sequence_length, top_k, model_dim
    )
    routed_part = jnp.einsum("sk,skd->sd", gate_probs, picked, preferred_element_type=jnp.float32)
    ffn_own = narrow(shared_part + routed_part)
    output = (residual + ffn_own).astype(jnp.bfloat16)
    weights_back = dense_fetch(
        query_projection,
        key_projection,
        value_projection,
        output_projection,
        shared_gate_matrix,
        shared_up_matrix,
        shared_down_matrix,
    )
    query_back, key_back, value_back, out_back, sgate_back, sup_back, sdown_back = weights_back
    grad_out = cotangent.astype(jnp.float32)
    grad_ffn = widen(cotangent)
    grad_hidden_sh = jnp.dot(grad_ffn, sdown_back.T, preferred_element_type=jnp.float32)
    grad_sdown = jnp.dot(hidden_shared.T, grad_ffn, preferred_element_type=jnp.float32)
    grad_gate_sh = (grad_hidden_sh * up_shared * silu_slope(gate_shared)).astype(jnp.bfloat16)
    grad_up_sh = (grad_hidden_sh * silu(gate_shared)).astype(jnp.bfloat16)
    grad_sgate = jnp.dot(full_two.T, grad_gate_sh, preferred_element_type=jnp.float32)
    grad_sup = jnp.dot(full_two.T, grad_up_sh, preferred_element_type=jnp.float32)
    grad_normed_part = jnp.dot(
        grad_gate_sh, sgate_back.T, preferred_element_type=jnp.float32
    ) + jnp.dot(grad_up_sh, sup_back.T, preferred_element_type=jnp.float32)
    grad_gates_part = jnp.einsum("sd,skd->sk", grad_ffn, picked, preferred_element_type=jnp.float32)
    grad_slot = (
        jnp.where(slot_used[:, None], grad_ffn[token_of_slot] * gate_of_slot[:, None], 0.0)
        .astype(jnp.bfloat16)
        .reshape(n_dp, exp_dev, capacity, model_dim)
    )
    received_gradient = lax.all_to_all(grad_slot, "dp", split_axis=0, concat_axis=0, tiled=True)
    expert_gate_gradient, expert_up_gradient, expert_down_gradient, output_rows_gradient = (
        expert_gradients(
            received,
            received_gradient,
            gate_preactivation,
            up_preactivation,
            expert_gate_matrix,
            expert_up_matrix,
            expert_down_matrix,
        )
    )
    grad_returned = lax.all_to_all(
        output_rows_gradient, "dp", split_axis=0, concat_axis=0, tiled=True
    )
    grad_picked = grad_returned.reshape(slot_total, model_dim)[slot_index].reshape(
        sequence_length, top_k, model_dim
    )
    grad_normed_part = grad_normed_part + jnp.sum(grad_picked, axis=1, dtype=jnp.float32)
    grad_normed_two, grad_gates = (
        lax.psum_scatter(
            grad_normed_part.astype(jnp.bfloat16), "tensor", scatter_dimension=0, tiled=True
        ).astype(jnp.float32),
        lax.psum_scatter(
            grad_gates_part.astype(jnp.bfloat16), "tensor", scatter_dimension=0, tiled=True
        ).astype(jnp.float32),
    )
    row_start = tensor_pos * own_rows
    gates_own = lax.dynamic_slice_in_dim(gate_probs, row_start, own_rows, 0)
    chosen_own = lax.dynamic_slice_in_dim(chosen, row_start, own_rows, 0)
    grad_selected = gates_own * (
        grad_gates - jnp.sum(gates_own * grad_gates, axis=-1, keepdims=True)
    )
    grad_logits = jnp.sum(jnp.where(chosen_own, grad_selected[:, :, None], 0.0), axis=1).astype(
        jnp.bfloat16
    )
    grad_normed_two = grad_normed_two + jnp.dot(
        grad_logits, router_full.T, preferred_element_type=jnp.float32
    )
    grad_router_part = jnp.dot(normed_two.T, grad_logits, preferred_element_type=jnp.float32)
    grad_residual, grad_gain_two = rms_back(grad_normed_two, residual, scale_two, second_gain)
    grad_residual = grad_residual + grad_out
    grad_attn = widen(grad_residual.astype(jnp.bfloat16))
    grad_wout = jnp.dot(mixed_heads.T, grad_attn, preferred_element_type=jnp.float32)
    grad_mixed = (
        jnp.dot(grad_attn, out_back.T, preferred_element_type=jnp.float32)
        .astype(jnp.bfloat16)
        .reshape(sequence_length, kv_heads, group_size, HEAD_SIZE)
    )
    grad_keys = jnp.zeros((sequence_length, kv_heads, HEAD_SIZE), jnp.float32)
    grad_values = jnp.zeros((sequence_length, kv_heads, HEAD_SIZE), jnp.float32)
    block_index = 0
    start_row = block_index * sequence_length
    end_row = start_row + sequence_length
    scores, allowed = block_scores(start_row, end_row)
    attn_probs = jnp.where(allowed, jnp.exp(scores - lse_blocks[block_index]), 0.0)
    probs_low = attn_probs.astype(jnp.bfloat16)
    grad_values = grad_values.at[:end_row].add(
        jnp.einsum("kgqs,qkgd->skd", probs_low, grad_mixed, preferred_element_type=jnp.float32)
    )
    grad_probs = jnp.einsum(
        "qkgd,skd->kgqs", grad_mixed, rows_of_value, preferred_element_type=jnp.float32
    )
    inner_sum = jnp.sum(attn_probs * grad_probs, axis=-1, keepdims=True)
    grad_scores = (attn_probs * (grad_probs - inner_sum)).astype(jnp.bfloat16)
    grad_query_blocks = (
        jnp.einsum("kgqs,skd->qkgd", grad_scores, key_rows, preferred_element_type=jnp.float32)
        * score_scale
    )
    grad_keys = grad_keys.at[:end_row].add(
        jnp.einsum("kgqs,qkgd->skd", grad_scores, rows_of_query, preferred_element_type=jnp.float32)
        * score_scale
    )
    grad_query = grad_query_blocks.reshape(sequence_length, q_heads, HEAD_SIZE)
    grad_q_raw = (
        rotate_back(grad_query, rotary_cosine, rotary_sine)
        .astype(jnp.bfloat16)
        .reshape(sequence_length, q_heads * HEAD_SIZE)
    )
    grad_k_raw = (
        rotate_back(grad_keys, rotary_cosine, rotary_sine)
        .astype(jnp.bfloat16)
        .reshape(sequence_length, kv_heads * HEAD_SIZE)
    )
    grad_v_low = grad_values.astype(jnp.bfloat16).reshape(sequence_length, kv_heads * HEAD_SIZE)
    grad_wquery = jnp.dot(full_one.T, grad_q_raw, preferred_element_type=jnp.float32)
    grad_wkey = jnp.dot(full_one.T, grad_k_raw, preferred_element_type=jnp.float32)
    grad_wvalue = jnp.dot(full_one.T, grad_v_low, preferred_element_type=jnp.float32)
    grad_normed_one_part = (
        jnp.dot(grad_q_raw, query_back.T, preferred_element_type=jnp.float32)
        + jnp.dot(grad_k_raw, key_back.T, preferred_element_type=jnp.float32)
        + jnp.dot(grad_v_low, value_back.T, preferred_element_type=jnp.float32)
    )
    grad_normed_one = narrow(grad_normed_one_part)
    grad_inputs, grad_gain_one = rms_back(grad_normed_one, input_values, scale_one, first_gain)
    grad_inputs = grad_inputs + grad_residual
    dense_sums = (
        lax.psum_scatter(grad_wquery, "dp", scatter_dimension=0, tiled=True),
        lax.psum_scatter(grad_wkey, "dp", scatter_dimension=0, tiled=True),
        lax.psum_scatter(grad_wvalue, "dp", scatter_dimension=0, tiled=True),
        lax.psum_scatter(grad_wout, "dp", scatter_dimension=1, tiled=True),
        lax.psum_scatter(grad_sgate, "dp", scatter_dimension=0, tiled=True),
        lax.psum_scatter(grad_sup, "dp", scatter_dimension=0, tiled=True),
        lax.psum_scatter(grad_sdown, "dp", scatter_dimension=1, tiled=True),
    )
    small_sums = (
        lax.psum_scatter(grad_router_part, ("dp", "tensor"), scatter_dimension=0, tiled=True),
        lax.psum_scatter(grad_gain_one, ("dp", "tensor"), scatter_dimension=0, tiled=True),
        lax.psum_scatter(grad_gain_two, ("dp", "tensor"), scatter_dimension=0, tiled=True),
    )
    return (
        output,
        grad_inputs,
        small_sums[1],
        small_sums[2],
        dense_sums[0],
        dense_sums[1],
        dense_sums[2],
        dense_sums[3],
        small_sums[0],
        dense_sums[4],
        dense_sums[5],
        dense_sums[6],
        expert_gate_gradient,
        expert_up_gradient,
        expert_down_gradient,
    )


def solution(mesh):
    placed = (
        P(("dp", "tensor"), None),
        P(("dp", "tensor")),
        P(("dp", "tensor")),
        P("dp", "tensor"),
        P("dp", "tensor"),
        P("dp", "tensor"),
        P("tensor", "dp"),
        P(("dp", "tensor"), None),
        P("dp", "tensor"),
        P("dp", "tensor"),
        P("tensor", "dp"),
        P("dp", None, "tensor"),
        P("dp", None, "tensor"),
        P("dp", "tensor", None),
        P("dp", None),
        P("dp", None),
        P(("dp", "tensor"), None),
    )
    return jax.shard_map(
        shards,
        mesh=mesh,
        in_specs=placed,
        out_specs=(
            P(("dp", "tensor"), None),
            P(("dp", "tensor"), None),
            P(("dp", "tensor")),
            P(("dp", "tensor")),
            P("dp", "tensor"),
            P("dp", "tensor"),
            P("dp", "tensor"),
            P("tensor", "dp"),
            P(("dp", "tensor"), None),
            P("dp", "tensor"),
            P("dp", "tensor"),
            P("tensor", "dp"),
            P("dp", None, "tensor"),
            P("dp", None, "tensor"),
            P("dp", "tensor", None),
        ),
        check_vma=False,
    )
```

profile of v0, /device:TPU:24, one launch (start us, length us, event | category | flops | bytes accessed | tf_op | source)
XLA Modules:
  0.0 2372.4 jit_solution(5493149657371583790)
XLA Ops:
  10.8 39.3 %all-reduce.5 = (bf16[2048]{0:T(1024)(128)(2,1)S(1)}, bf16[2048]{0:T(1024)(128)(2,1)}) all-reduce(bf16[2048]{0:T(1024)(128)(2,1)S(1)} %dynamic-update-slice.4, bf16[2048]{0:T(1024)(128)(2,1)S(1)} %dynamic-update-slice.5), channel_id=1, replica_groups=mesh['dp'=16,'tensor'=2] {'dp','tensor'}, use_global_device_ids=true, to_apply=%add | all-reduce | flops 4096 | bytes 16384
  57.7 17.8 all-gather.13.cloned.1.call-done
  75.4 39.1 %all-gather.17.cloned.1.call-done = bf16[2048,256]{1,0:T(8,128)(2,1)} async-done(((bf16[128,256]{1,0:T(8,128)(2,1)}), bf16[2048,256]{1,0:T(8,128)(2,1)}) %all-gather.17.cloned.1.call-update) | async-done | bytes 1048592 | tf_op jit(solution)/shard_map/all_gather | solution.py:82
  121.9 31.7 %all-gather.15.cloned.1.call-done = bf16[2048,256]{1,0:T(8,128)(2,1)} async-done(((bf16[128,256]{1,0:T(8,128)(2,1)}), bf16[2048,256]{1,0:T(8,128)(2,1)}) %all-gather.15.cloned.1.call-update) | async-done | bytes 1048592 | tf_op jit(solution)/shard_map/all_gather | solution.py:83
  156.3 48.4 %all-gather.19.cloned.1.call-done = bf16[2048,1024]{1,0:T(8,128)(2,1)} async-done(((bf16[128,1024]{1,0:T(8,128)(2,1)}), bf16[2048,1024]{1,0:T(8,128)(2,1)}) %all-gather.19.cloned.1.call-update) | async-done | bytes 4194320 | tf_op jit(solution)/shard_map/all_gather | solution.py:81
  213.7 44.3 %all-gather.21.cloned.1.call-done = bf16[1024,2048]{1,0:T(8,128)(2,1)} async-done(((bf16[1024,128]{1,0:T(8,128)(2,1)}), bf16[1024,2048]{1,0:T(8,128)(2,1)}) %all-gather.21.cloned.1.call-update) | async-done | bytes 4194320 | tf_op jit(solution)/shard_map/all_gather | solution.py:84
  267.5 27.5 %reduce-scatter.18.cloned.1.call-done = f32[128,2048]{1,0:T(8,128)} async-done(((f32[256,2048]{1,0:T(8,128)}), f32[128,2048]{1,0:T(8,128)}) %reduce-scatter.18.cloned.1.call-update) | async-done | bytes 1048592 | tf_op jit(solution)/shard_map/reduce_scatter | solution.py:68
  321.5 17.7 gather_fusion
  353.5 221.5 %all-gather = bf16[32,64,16]{1,2,0:T(8,128)(2,1)S(1)} all-gather(bf16[1,64,16]{1,2,0:T(8,128)(2,1)S(1)} %bitcast.356), channel_id=1, replica_groups=mesh['dp'=16,'tensor'=2] {'dp','tensor'}, dimensions={0}, use_global_device_ids=true | all-gather | bytes 67584 | tf_op jit(solution)/shard_map/all_gather | solution.py:176
  575.3 17.7 gather_fusion.2
  632.4 192.9 %all-to-all-done.2 = bf16[16,1,128,2048]{3,2,1,0:T(8,128)(2,1)} async-done(((bf16[16,1,128,2048]{3,2,1,0:T(8,128)(2,1)}), bf16[16,1,128,2048]{3,2,1,0:T(8,128)(2,1)}, u32[]{:S(2)}, u32[]{:S(2)}) %all-to-all-start.2) | async-done | bytes 8388640 | tf_op jit(solution)/shard_map/all_to_all | solution.py:318
  836.5 14.1 fusion.34
  861.4 17.3 all-to-all-start.1
  879.3 12.1 fusion.36
  891.4 12.5 fusion.2
  903.9 179.5 %all-to-all-done.1 = bf16[16,1,128,2048]{3,2,1,0:T(8,128)(2,1)} async-done(((bf16[16,1,128,2048]{3,2,1,0:T(8,128)(2,1)}), bf16[16,1,128,2048]{3,2,1,0:T(8,128)(2,1)}, u32[]{:S(2)}, u32[]{:S(2)}) %all-to-all-start.1) | async-done | bytes 8388640 | tf_op jit(solution)/shard_map/all_to_all | solution.py:278
  1083.4 17.3 all-to-all-start.3
  1112.9 170.2 %all-gather.29.cloned.1.call-done = bf16[1408,2048]{1,0:T(8,128)(2,1)} async-done(((bf16[1408,128]{1,0:T(8,128)(2,1)}), bf16[1408,2048]{1,0:T(8,128)(2,1)}) %all-gather.29.cloned.1.call-update) | async-done | bytes 5767184 | tf_op jit(solution)/shard_map/all_gather | solution.py:87
  1292.9 17.6 gather_fusion.1
  1331.3 17.1 gather_fusion.3
  1400.2 31.8 %reduce-scatter.20.cloned.1.call-done = f32[128,2048]{1,0:T(8,128)} async-done(((f32[256,2048]{1,0:T(8,128)}), f32[128,2048]{1,0:T(8,128)}) %reduce-scatter.20.cloned.1.call-update) | async-done | bytes 1048592 | tf_op jit(solution)/shard_map/reduce_scatter | solution.py:68
  1437.1 19.9 all-gather.33.cloned.1.call-done
  1547.6 33.7 %reduce-scatter.42.cloned.1.call-done = f32[64,16]{1,0:T(8,128)} async-done(((f32[2048,16]{1,0:T(8,128)}), f32[64,16]{1,0:T(8,128)}) %reduce-scatter.42.cloned.1.call-update) | async-done | bytes 4112
  1582.7 41.8 %reduce-scatter.24.cloned.1.call-done = f32[128,2048]{1,0:T(8,128)} async-done(((f32[256,2048]{1,0:T(8,128)}), f32[128,2048]{1,0:T(8,128)}) %reduce-scatter.24.cloned.1.call-update) | async-done | bytes 1048592 | tf_op jit(solution)/shard_map/reduce_scatter | solution.py:68
  1626.1 38.5 %all-reduce.4 = (f32[2048]{0:T(1024)S(1)}, f32[2048]{0:T(1024)S(1)}) all-reduce(f32[2048]{0:T(1024)S(1)} %get-tuple-element.57, f32[2048]{0:T(1024)S(1)} %get-tuple-element.55), channel_id=7, replica_groups=mesh['dp'=16,'tensor'=2] {'dp','tensor'}, use_global_device_ids=true, to_apply=%region_27.28.clone | all-reduce | flops 4096 | bytes 32768
  1668.7 86.1 %reduce-scatter.38.cloned.1.call-done = f32[1408,128]{1,0:T(8,128)} async-done(((f32[1408,2048]{1,0:T(8,128)}), f32[1408,128]{1,0:T(8,128)}) %reduce-scatter.38.cloned.1.call-update) | async-done | bytes 720912 | tf_op jit(solution)/shard_map/reduce_scatter | solution.py:421
  1754.9 130.7 %reduce-scatter.34.cloned.1.call-done = f32[128,1408]{1,0:T(8,128)} async-done(((f32[2048,1408]{1,0:T(8,128)}), f32[128,1408]{1,0:T(8,128)}) %reduce-scatter.34.cloned.1.call-update) | async-done | bytes 720912 | tf_op jit(solution)/shard_map/reduce_scatter | solution.py:419
  1885.6 131.2 %reduce-scatter.36.cloned.1.call-done = f32[128,1408]{1,0:T(8,128)} async-done(((f32[2048,1408]{1,0:T(8,128)}), f32[128,1408]{1,0:T(8,128)}) %reduce-scatter.36.cloned.1.call-update) | async-done | bytes 720912 | tf_op jit(solution)/shard_map/reduce_scatter | solution.py:420
  2016.8 65.7 %reduce-scatter.30.cloned.1.call-done = f32[128,256]{1,0:T(8,128)} async-done(((f32[2048,256]{1,0:T(8,128)}), f32[128,256]{1,0:T(8,128)}) %reduce-scatter.30.cloned.1.call-update) | async-done | bytes 131088 | tf_op jit(solution)/shard_map/reduce_scatter | solution.py:417
  2082.4 65.3 %reduce-scatter.28.cloned.1.call-done = f32[128,256]{1,0:T(8,128)} async-done(((f32[2048,256]{1,0:T(8,128)}), f32[128,256]{1,0:T(8,128)}) %reduce-scatter.28.cloned.1.call-update) | async-done | bytes 131088 | tf_op jit(solution)/shard_map/reduce_scatter | solution.py:416
  2147.8 108.3 %reduce-scatter.26.cloned.1.call-done = f32[128,1024]{1,0:T(8,128)} async-done(((f32[2048,1024]{1,0:T(8,128)}), f32[128,1024]{1,0:T(8,128)}) %reduce-scatter.26.cloned.1.call-update) | async-done | bytes 524304 | tf_op jit(solution)/shard_map/reduce_scatter | solution.py:415
  2256.0 109.1 %reduce-scatter.32.cloned.1.call-done = f32[1024,128]{1,0:T(8,128)} async-done(((f32[1024,2048]{1,0:T(8,128)}), f32[1024,128]{1,0:T(8,128)}) %reduce-scatter.32.cloned.1.call-update) | async-done | bytes 524304 | tf_op jit(solution)/shard_map/reduce_scatter | solution.py:418
  (333 shorter events, 339.1 us)
Async XLA Ops:
  7.2 829.3 %copy-start = (bf16[1,2048,704]{1,2,0:T(8,128)(2,1)S(1)}, bf16[1,2048,704]{1,2,0:T(8,128)(2,1)}, u32[]{:S(2)}) copy-start(bf16[1,2048,704]{1,2,0:T(8,128)(2,1)} %param.36) | copy-start | bytes 8650756
  7.2 68.2 %all-gather.13.cloned.1.call-start = ((), (), s32[]{:S(2)}) async-start(), calls=%async_computation.17 | async-start | bytes 1572864 | tf_op jit(solution)/shard_map/all_gather | solution.py:64
  52.7 61.7 %all-gather.17.cloned.1.call-start = ((), (), s32[]{:S(2)}) async-start(), calls=%async_computation.19 | async-start | bytes 1114112 | tf_op jit(solution)/shard_map/all_gather | solution.py:82
  53.5 100.1 %all-gather.15.cloned.1.call-start = ((), (), s32[]{:S(2)}) async-start(), calls=%async_computation.18 | async-start | bytes 1114112 | tf_op jit(solution)/shard_map/all_gather | solution.py:83
  54.2 150.4 %all-gather.19.cloned.1.call-start = ((), (), s32[]{:S(2)}) async-start(), calls=%async_computation.20 | async-start | bytes 4456448 | tf_op jit(solution)/shard_map/all_gather | solution.py:81
  54.8 203.2 %all-gather.21.cloned.1.call-start = ((), (), s32[]{:S(2)}) async-start(), calls=%async_computation.21 | async-start | bytes 4456448 | tf_op jit(solution)/shard_map/all_gather | solution.py:84
  55.4 239.7 %reduce-scatter.18.cloned.1.call-start = ((), (), s32[]{:S(2)}) async-start(), calls=%async_computation.22 | async-start | bytes 3145728 | tf_op jit(solution)/shard_map/reduce_scatter | solution.py:68
  263.0 58.5 %all-gather.23.cloned.1.call-start = ((), (), s32[]{:S(2)}) async-start(), calls=%async_computation.23 | async-start | bytes 1572864 | tf_op jit(solution)/shard_map/all_gather | solution.py:64
  346.6 263.6 %all-to-all-start = ((bf16[16,1,128,2048]{3,2,1,0:T(8,128)(2,1)}), bf16[16,1,128,2048]{3,2,1,0:T(8,128)(2,1)}, u32[]{:S(2)}, u32[]{:S(2)}) async-start(bf16[16,1,128,2048]{3,2,1,0:T(8,128)(2,1)} %broadcast_select_fusion), calls=%async_computation.1 | async-start | bytes 16777216 | tf_op jit(solution)/shard_map/all_to_all | solution.py:274
  352.7 222.6 %all-gather.31.cloned.1.call-start = ((), (), s32[]{:S(2)}) async-start(), calls=%async_computation.28 | async-start | bytes 1572864 | tf_op jit(solution)/shard_map/all_gather | solution.py:64
  610.1 215.2 %all-to-all-start.2 = ((bf16[16,1,128,2048]{3,2,1,0:T(8,128)(2,1)}), bf16[16,1,128,2048]{3,2,1,0:T(8,128)(2,1)}, u32[]{:S(2)}, u32[]{:S(2)}) async-start(bf16[16,1,128,2048]{3,2,1,0:T(8,128)(2,1)} %fusion.1), calls=%async_computation.4 | async-start | bytes 16777216 | tf_op jit(solution)/shard_map/all_to_all | solution.py:318
  620.6 481.0 %all-gather.27.cloned.1.call-start = ((), (), s32[]{:S(2)}) async-start(), calls=%async_computation.25 | async-start | bytes 6127616 | tf_op jit(solution)/shard_map/all_gather | solution.py:86
  861.4 222.0 %all-to-all-start.1 = ((bf16[16,1,128,2048]{3,2,1,0:T(8,128)(2,1)}), bf16[16,1,128,2048]{3,2,1,0:T(8,128)(2,1)}, u32[]{:S(2)}, u32[]{:S(2)}) async-start(bf16[16,1,128,2048]{3,2,1,0:T(8,128)(2,1)} %convert_bitcast_fusion), calls=%async_computation.2 | async-start | bytes 16777216 | tf_op jit(solution)/shard_map/all_to_all | solution.py:278
  878.7 228.6 %all-gather.25.cloned.1.call-start = ((), (), s32[]{:S(2)}) async-start(), calls=%async_computation.24 | async-start | bytes 6127616 | tf_op jit(solution)/shard_map/all_gather | solution.py:85
  903.9 197.8 %copy-start.2 = (bf16[256,2048]{1,0:T(8,128)(2,1)S(1)}, bf16[256,2048]{1,0:T(8,128)(2,1)}, u32[]{:S(2)}) copy-start(bf16[256,2048]{1,0:T(8,128)(2,1)} %all-gather.23.cloned.1.call-done) | copy-start | bytes 3145732
  1083.4 247.9 %all-to-all-start.3 = ((bf16[16,1,128,2048]{3,2,1,0:T(8,128)(2,1)}), bf16[16,1,128,2048]{3,2,1,0:T(8,128)(2,1)}, u32[]{:S(2)}, u32[]{:S(2)}) async-start(bf16[16,1,128,2048]{3,2,1,0:T(8,128)(2,1)} %fusion.2), calls=%async_computation.5 | async-start | bytes 16777216 | tf_op jit(solution)/shard_map/all_to_all | solution.py:330
  1100.7 182.4 %all-gather.29.cloned.1.call-start = ((), (), s32[]{:S(2)}) async-start(), calls=%async_computation.26 | async-start | bytes 6127616 | tf_op jit(solution)/shard_map/all_gather | solution.py:87
  1101.4 288.2 %reduce-scatter.40.cloned.1.call-start = ((), (), s32[]{:S(2)}) async-start(), calls=%async_computation.39 | async-start | bytes 98304
  1107.3 175.8 %copy-start.3 = (bf16[256,2048]{1,0:T(8,128)(2,1)S(1)}, bf16[256,2048]{1,0:T(8,128)(2,1)}, u32[]{:S(2)}) copy-start(bf16[256,2048]{1,0:T(8,128)(2,1)} %all-gather.31.cloned.1.call-done) | copy-start | bytes 3145732
  1331.2 66.2 %reduce-scatter.22.cloned.1.call-start = ((), (), s32[]{:S(2)}) async-start(), calls=%async_computation.29 | async-start | bytes 1572864 | tf_op jit(solution)/shard_map/reduce_scatter | solution.py:338
  1376.8 55.1 %reduce-scatter.20.cloned.1.call-start = ((), (), s32[]{:S(2)}) async-start(), calls=%async_computation.27 | async-start | bytes 3145728 | tf_op jit(solution)/shard_map/reduce_scatter | solution.py:68
  1389.5 67.6 %all-gather.33.cloned.1.call-start = ((), (), s32[]{:S(2)}) async-start(), calls=%async_computation.30 | async-start | bytes 1572864 | tf_op jit(solution)/shard_map/all_gather | solution.py:64
  1435.6 145.7 %reduce-scatter.42.cloned.1.call-start = ((), (), s32[]{:S(2)}) async-start(), calls=%async_computation.40 | async-start | bytes 1081344
  1437.1 187.5 %reduce-scatter.24.cloned.1.call-start = ((), (), s32[]{:S(2)}) async-start(), calls=%async_computation.31 | async-start | bytes 3145728 | tf_op jit(solution)/shard_map/reduce_scatter | solution.py:68
  1479.0 275.9 %reduce-scatter.38.cloned.1.call-start = ((), (), s32[]{:S(2)}) async-start(), calls=%async_computation.38 | async-start | bytes 12255232 | tf_op jit(solution)/shard_map/reduce_scatter | solution.py:421
  1486.1 399.5 %reduce-scatter.34.cloned.1.call-start = ((), (), s32[]{:S(2)}) async-start(), calls=%async_computation.36 | async-start | bytes 12255232 | tf_op jit(solution)/shard_map/reduce_scatter | solution.py:419
  1493.3 523.5 %reduce-scatter.36.cloned.1.call-start = ((), (), s32[]{:S(2)}) async-start(), calls=%async_computation.37 | async-start | bytes 12255232 | tf_op jit(solution)/shard_map/reduce_scatter | solution.py:420
  1500.5 582.0 %reduce-scatter.30.cloned.1.call-start = ((), (), s32[]{:S(2)}) async-start(), calls=%async_computation.34 | async-start | bytes 2228224 | tf_op jit(solution)/shard_map/reduce_scatter | solution.py:417
  1503.5 644.3 %reduce-scatter.28.cloned.1.call-start = ((), (), s32[]{:S(2)}) async-start(), calls=%async_computation.33 | async-start | bytes 2228224 | tf_op jit(solution)/shard_map/reduce_scatter | solution.py:416
  1505.4 750.6 %reduce-scatter.26.cloned.1.call-start = ((), (), s32[]{:S(2)}) async-start(), calls=%async_computation.32 | async-start | bytes 8912896 | tf_op jit(solution)/shard_map/reduce_scatter | solution.py:415
  1510.1 855.1 %reduce-scatter.32.cloned.1.call-start = ((), (), s32[]{:S(2)}) async-start(), calls=%async_computation.35 | async-start | bytes 8912896 | tf_op jit(solution)/shard_map/reduce_scatter | solution.py:418
  1537.4 827.8 %copy-start.1 = (bf16[1,2048,704]{1,2,0:T(8,128)(2,1)S(1)}, bf16[1,2048,704]{1,2,0:T(8,128)(2,1)}, u32[]{:S(2)}) copy-start(bf16[1,2048,704]{1,2,0:T(8,128)(2,1)} %param.36) | copy-start | bytes 8650756
  (71 other events, 1552.0 us)
Sparse Core Ops, SparseCore 0:
  52.9 22.5 all-gather.12
  77.6 36.8 all-gather.16
  116.7 36.8 all-gather.14
  155.6 49.0 all-gather.18
  206.6 51.3 all-gather.20
  263.1 31.8 reduce-scatter.17
  298.6 21.3 all-gather.22
  355.2 21.3 all-gather.30
  624.0 176.8 all-gather.26
  881.7 172.7 all-gather.24
  1103.9 179.1 all-gather.28
  1331.3 9.9 reduce-scatter.39
  1377.0 20.3 reduce-scatter.21
  1400.0 31.8 reduce-scatter.19
  1435.8 21.2 all-gather.32
  1459.3 122.0 reduce-scatter.41
  1583.4 41.1 reduce-scatter.23
  1629.7 125.1 reduce-scatter.37
  1759.5 126.0 reduce-scatter.33
  1890.7 126.0 reduce-scatter.35
  2021.1 61.3 reduce-scatter.29
  2087.2 60.5 reduce-scatter.27
  2152.4 103.5 reduce-scatter.25
  2260.5 104.5 reduce-scatter.31
where the time goes:
time: 2390 us; the launch traced here: 2370 us
  waiting for transfers between devices  1590 us (67%)
  blocking collectives  299 us (13%)
  matrix products  216 us (9%)
  local copies, waits for them, and re-layouts  147 us (6%)
  other arithmetic  54.5 us (2%)
  starting transfers between devices  53.1 us (2%)
    all_gather x1, blocking collectives, shards(): lax.all_gather(router, ('dp', 'tensor'), axis=0, tiled=True)  222 us
    all_to_all x1, waiting for transfers between devices, shards(): lax.all_to_all(grad_slot, 'dp', split_axis=0, concat_axis=0, tiled=True)  193 us
    all_to_all x1, waiting for transfers between devices, shards(): lax.all_to_all(produced_rows, 'dp', split_axis=0, concat_axis=0, tiled=True)  179 us
    all_gather x1, waiting for transfers between devices, dense_fetch(): lax.all_gather(shared_down_matrix, 'dp', axis=1, tiled=True)  170 us
    reduce_scatter x1, waiting for transfers between devices, shards(): lax.psum_scatter(grad_sup, 'dp', scatter_dimension=0, tiled=True)  131 us
    reduce_scatter x1, waiting for transfers between devices, shards(): lax.psum_scatter(grad_sgate, 'dp', scatter_dimension=0, tiled=True)  131 us
    reduce_scatter x1, waiting for transfers between devices, shards(): lax.psum_scatter(grad_wout, 'dp', scatter_dimension=1, tiled=True)  109 us
    reduce_scatter x1, waiting for transfers between devices, shards(): lax.psum_scatter(grad_wquery, 'dp', scatter_dimension=0, tiled=True)  108 us
  transfers between devices with their start and end apart: 28, of which 21 were waited for; matrix products, arithmetic and copies ran while one was open for 15% of the time, Pallas kernels for 0%

commit v1 on v0

--- a/solution.py
+++ b/solution.py
@@ -1,11 +1,15 @@
+import functools
 import math
 
 import jax
 import jax.numpy as jnp
 from jax import lax
+from jax.experimental import pallas as pl
+from jax.experimental.pallas import tpu as pltpu
 from jax.sharding import PartitionSpec as P
 
 HEAD_SIZE = 128
+DP, TENSOR = ("dp", "tensor")
 
 
 norm_eps = 1e-06
@@ -61,11 +65,11 @@
 
 
 def widen(sharded):
-    return lax.all_gather(sharded, "tensor", axis=0, tiled=True)
+    return lax.all_gather(sharded, TENSOR, axis=0, tiled=True)
 
 
 def narrow(partial_sum):
-    return lax.psum_scatter(partial_sum, "tensor", scatter_dimension=0, tiled=True)
+    return lax.psum_scatter(partial_sum, TENSOR, scatter_dimension=0, tiled=True)
 
 
 def dense_fetch(
@@ -78,13 +82,13 @@
     shared_down_matrix,
 ):
     return (
-        lax.all_gather(query_projection, "dp", axis=0, tiled=True),
-        lax.all_gather(key_projection, "dp", axis=0, tiled=True),
-        lax.all_gather(value_projection, "dp", axis=0, tiled=True),
-        lax.all_gather(output_projection, "dp", axis=1, tiled=True),
-        lax.all_gather(shared_gate_matrix, "dp", axis=0, tiled=True),
-        lax.all_gather(shared_up_matrix, "dp", axis=0, tiled=True),
-        lax.all_gather(shared_down_matrix, "dp", axis=1, tiled=True),
+        lax.all_gather(query_projection, DP, axis=0, tiled=True),
+        lax.all_gather(key_projection, DP, axis=0, tiled=True),
+        lax.all_gather(value_projection, DP, axis=0, tiled=True),
+        lax.all_gather(output_projection, DP, axis=1, tiled=True),
+        lax.all_gather(shared_gate_matrix, DP, axis=0, tiled=True),
+        lax.all_gather(shared_up_matrix, DP, axis=0, tiled=True),
+        lax.all_gather(shared_down_matrix, DP, axis=1, tiled=True),
     )
 
 
@@ -142,7 +146,7 @@
     return (expert_gate_gradient, expert_up_gradient, expert_down_gradient, output_rows_gradient)
 
 
-def shards(
+def exchange_plan(
     tokens,
     attention_gain,
     expert_norm_gain,
@@ -161,9 +165,9 @@
     expert_indices,
     cotangent,
 ):
-    n_tensor = lax.axis_size("tensor")
-    n_dp = lax.axis_size("dp")
-    tensor_pos = lax.axis_index("tensor")
+    n_tensor = lax.axis_size(TENSOR)
+    n_dp = lax.axis_size(DP)
+    tensor_pos = lax.axis_index(TENSOR)
     own_rows = tokens.shape[0]
     sequence_length = own_rows * n_tensor
     model_dim = tokens.shape[1]
@@ -173,9 +177,9 @@
     capacity = max(2, sequence_length * top_k * 4 // (3 * experts))
     slot_total = experts * capacity
     router_full, gain_first, gain_second = (
-        lax.all_gather(router, ("dp", "tensor"), axis=0, tiled=True),
-        lax.all_gather(attention_gain, ("dp", "tensor"), axis=0, tiled=True),
-        lax.all_gather(expert_norm_gain, ("dp", "tensor"), axis=0, tiled=True),
+        lax.all_gather(router, (DP, TENSOR), axis=0, tiled=True),
+        lax.all_gather(attention_gain, (DP, TENSOR), axis=0, tiled=True),
+        lax.all_gather(expert_norm_gain, (DP, TENSOR), axis=0, tiled=True),
     )
     first_gain = gain_first.astype(jnp.float32)
     second_gain = gain_second.astype(jnp.float32)
@@ -271,11 +275,11 @@
     outgoing = jnp.where(slot_used[:, None], full_two[token_of_slot], 0).reshape(
         n_dp, exp_dev, capacity, model_dim
     )
-    received_rows = lax.all_to_all(outgoing, "dp", split_axis=0, concat_axis=0, tiled=True)
+    received_rows = lax.all_to_all(outgoing, DP, split_axis=0, concat_axis=0, tiled=True)
     produced_rows, gate_preactivation, up_preactivation = expert_up_output(
         received_rows, expert_gate_matrix, expert_up_matrix, expert_down_matrix
     )
-    sent_home = lax.all_to_all(produced_rows, "dp", split_axis=0, concat_axis=0, tiled=True)
+    sent_home = lax.all_to_all(produced_rows, DP, split_axis=0, concat_axis=0, tiled=True)
     returned, received, gate_preactivation, up_preactivation = (
         sent_home,
         received_rows,
@@ -315,7 +319,7 @@
         .astype(jnp.bfloat16)
         .reshape(n_dp, exp_dev, capacity, model_dim)
     )
-    received_gradient = lax.all_to_all(grad_slot, "dp", split_axis=0, concat_axis=0, tiled=True)
+    received_gradient = lax.all_to_all(grad_slot, DP, split_axis=0, concat_axis=0, tiled=True)
     expert_gate_gradient, expert_up_gradient, expert_down_gradient, output_rows_gradient = (
         expert_gradients(
             received,
@@ -328,7 +332,7 @@
         )
     )
     grad_returned = lax.all_to_all(
-        output_rows_gradient, "dp", split_axis=0, concat_axis=0, tiled=True
+        output_rows_gradient, DP, split_axis=0, concat_axis=0, tiled=True
     )
     grad_picked = grad_returned.reshape(slot_total, model_dim)[slot_index].reshape(
         sequence_length, top_k, model_dim
@@ -336,10 +340,10 @@
     grad_normed_part = grad_normed_part + jnp.sum(grad_picked, axis=1, dtype=jnp.float32)
     grad_normed_two, grad_gates = (
         lax.psum_scatter(
-            grad_normed_part.astype(jnp.bfloat16), "tensor", scatter_dimension=0, tiled=True
+            grad_normed_part.astype(jnp.bfloat16), TENSOR, scatter_dimension=0, tiled=True
         ).astype(jnp.float32),
         lax.psum_scatter(
-            grad_gates_part.astype(jnp.bfloat16), "tensor", scatter_dimension=0, tiled=True
+            grad_gates_part.astype(jnp.bfloat16), TENSOR, scatter_dimension=0, tiled=True
         ).astype(jnp.float32),
     )
     row_start = tensor_pos * own_rows
@@ -412,18 +416,18 @@
     grad_inputs, grad_gain_one = rms_back(grad_normed_one, input_values, scale_one, first_gain)
     grad_inputs = grad_inputs + grad_residual
     dense_sums = (
-        lax.psum_scatter(grad_wquery, "dp", scatter_dimension=0, tiled=True),
-        lax.psum_scatter(grad_wkey, "dp", scatter_dimension=0, tiled=True),
-        lax.psum_scatter(grad_wvalue, "dp", scatter_dimension=0, tiled=True),
-        lax.psum_scatter(grad_wout, "dp", scatter_dimension=1, tiled=True),
-        lax.psum_scatter(grad_sgate, "dp", scatter_dimension=0, tiled=True),
-        lax.psum_scatter(grad_sup, "dp", scatter_dimension=0, tiled=True),
-        lax.psum_scatter(grad_sdown, "dp", scatter_dimension=1, tiled=True),
+        lax.psum_scatter(grad_wquery, DP, scatter_dimension=0, tiled=True),
+        lax.psum_scatter(grad_wkey, DP, scatter_dimension=0, tiled=True),
+        lax.psum_scatter(grad_wvalue, DP, scatter_dimension=0, tiled=True),
+        lax.psum_scatter(grad_wout, DP, scatter_dimension=1, tiled=True),
+        lax.psum_scatter(grad_sgate, DP, scatter_dimension=0, tiled=True),
+        lax.psum_scatter(grad_sup, DP, scatter_dimension=0, tiled=True),
+        lax.psum_scatter(grad_sdown, DP, scatter_dimension=1, tiled=True),
     )
     small_sums = (
-        lax.psum_scatter(grad_router_part, ("dp", "tensor"), scatter_dimension=0, tiled=True),
-        lax.psum_scatter(grad_gain_one, ("dp", "tensor"), scatter_dimension=0, tiled=True),
-        lax.psum_scatter(grad_gain_two, ("dp", "tensor"), scatter_dimension=0, tiled=True),
+        lax.psum_scatter(grad_router_part, (DP, TENSOR), scatter_dimension=0, tiled=True),
+        lax.psum_scatter(grad_gain_one, (DP, TENSOR), scatter_dimension=0, tiled=True),
+        lax.psum_scatter(grad_gain_two, (DP, TENSOR), scatter_dimension=0, tiled=True),
     )
     return (
         output,
@@ -444,46 +448,868 @@
     )
 
 
+MESH = pl.DeviceIdType.MESH
+ANY = pl.BlockSpec(memory_space=pl.ANY)
+
+
+def when(condition, body):
+    if condition is None:
+        body()
+    else:
+        pl.when(condition)(body)
+
+
+class Spot:
+    def __init__(self, n_planes):
+        dp = lax.axis_index(DP)
+        self.x = lax.axis_index(TENSOR)
+        self.dp = dp
+        self.core = dp % 2
+        self.y = (dp // 2) % 2
+        self.z = dp // 4
+        self.n_planes = n_planes
+        self.has_up = self.z < n_planes - 1
+        self.has_down = self.z > 0
+        self.up = (dp + 4, self.x)
+        self.down = (dp - 4, self.x)
+        self.side = (dp + 2 - 4 * self.y, self.x)
+        self.across = (dp, 1 - self.x)
+        self.twin = (dp + 1 - 2 * self.core, self.x)
+
+    def far_first(self):
+        low, high = 0 * self.z, 0 * self.z + self.n_planes - 1
+        order = []
+        for _ in range(self.n_planes):
+            take_low = (self.z - low >= high - self.z).astype(jnp.int32)
+            order.append(take_low * low + (1 - take_low) * high)
+            low, high = low + take_low, high - (1 - take_low)
+        return order
+
+    def greet(self):
+        barrier = pltpu.get_barrier_semaphore()
+        fixed = [self.side, self.twin, self.across]
+        for device in fixed:
+            pl.semaphore_signal(barrier, inc=1, device_id=device, device_id_type=MESH)
+        for condition, device in ((self.has_up, self.up), (self.has_down, self.down)):
+
+            @pl.when(condition)
+            def _(device=device):
+                pl.semaphore_signal(barrier, inc=1, device_id=device, device_id_type=MESH)
+
+        ends = self.has_up.astype(jnp.int32) + self.has_down.astype(jnp.int32)
+        pl.semaphore_wait(barrier, len(fixed) + ends)
+
+
+class Copies:
+    def __init__(self, groups, n_planes, n_pieces, send, recv):
+        self.base = {name: i * n_planes for i, name in enumerate(groups)}
+        self.n_pieces = n_pieces
+        self.send, self.recv = send, recv
+        self.open = []
+
+    def copy(self, group, s, piece, src, dst, device, arrival=None):
+        return pltpu.make_async_remote_copy(
+            src_ref=src,
+            dst_ref=dst,
+            send_sem=self.send.at[self.base[group] + s, piece],
+            recv_sem=self.recv.at[self.base[arrival or group] + s, piece],
+            device_id=device,
+            device_id_type=MESH,
+        )
+
+    def start(self, condition, group, s, sources, targets, device, arrival=None):
+        def body():
+            for i, (src, dst) in enumerate(zip(sources, targets)):
+                self.copy(group, s, i, src, dst, device, arrival).start()
+
+        when(condition, body)
+        self.open.append((condition, group, s, sources, targets, device, arrival))
+
+    def arrive(self, group, s, targets, device):
+        for i, dst in enumerate(targets):
+            self.copy(group, s, i, dst, dst, device).wait_recv()
+
+    def close(self):
+        for condition, group, s, sources, targets, device, arrival in self.open:
+
+            def body():
+                for i, (src, dst) in enumerate(zip(sources, targets)):
+                    self.copy(group, s, i, src, dst, device, arrival).wait_send()
+
+            when(condition, body)
+
+
+SPREAD_GROUPS = (
+    "z", "z_down", "y_all", "y_half", "x_all", "x_half", "c_own", "c_y", "c_x", "c_xh", "c_yh",
+)
+
+
+def spread(spot, copies, own, views, use_x):
+    order = spot.far_first()[::-1]
+    y, x, core = spot.y, spot.x, spot.core
+
+    def at(s, yy, xx, part="all", cc=None):
+        return views(s, yy, core if cc is None else cc, xx, part)
+
+    def onward(s, sources):
+        copies.start(None, "y_all", s, sources, at(s, y, x), spot.side)
+        if use_x:
+            copies.start(None, "x_all", s, sources, at(s, y, x), spot.across)
+        copies.start(None, "c_own", s, sources, at(s, y, x), spot.twin)
+
+    def column(j):
+        s = order[j]
+        here = at(s, y, x)
+        copies.arrive("z", s, here, spot.up)
+        copies.start((s > spot.z) & spot.has_down, "z_down", s, here, here, spot.down, "z")
+        copies.start((s < spot.z) & spot.has_up, "z", s, here, here, spot.up)
+        onward(s, here)
+
+    def sides(j):
+        s = order[j]
+        there = at(s, 1 - y, x)
+        copies.arrive("y_all", s, there, spot.side)
+        if use_x:
+            part = at(s, 1 - y, x, "first")
+            copies.start(None, "x_half", s, part, part, spot.across)
+        copies.start(None, "c_y", s, there, there, spot.twin)
+        if use_x:
+            there = at(s, y, 1 - x)
+            copies.arrive("x_all", s, there, spot.across)
+            part = at(s, y, 1 - x, "second")
+            copies.start(None, "y_half", s, part, part, spot.side)
+            copies.start(None, "c_x", s, there, there, spot.twin)
+
+    def corner(j):
+        if not use_x:
+            return
+        s = order[j]
+        part = at(s, 1 - y, 1 - x, "first")
+        copies.arrive("x_half", s, part, spot.across)
+        copies.start(None, "c_xh", s, part, part, spot.twin)
+        part = at(s, 1 - y, 1 - x, "second")
+        copies.arrive("y_half", s, part, spot.side)
+        copies.start(None, "c_yh", s, part, part, spot.twin)
+
+    here = at(spot.z, y, x)
+    copies.start(spot.has_up, "z", spot.z, own, here, spot.up)
+    copies.start(spot.has_down, "z_down", spot.z, own, here, spot.down, "z")
+    onward(spot.z, own)
+    n = spot.n_planes
+    for step in range(1, n + 2):
+        if step < n:
+            column(step)
+        if 0 <= step - 1 < n:
+            sides(step - 1)
+        if 0 <= step - 2 < n:
+            corner(step - 2)
+    other = 1 - core
+    for s in range(n):
+        copies.arrive("c_own", s, at(s, y, x, cc=other), spot.twin)
+        copies.arrive("c_y", s, at(s, 1 - y, x, cc=other), spot.twin)
+        if use_x:
+            copies.arrive("c_x", s, at(s, y, 1 - x, cc=other), spot.twin)
+            copies.arrive("c_xh", s, at(s, 1 - y, 1 - x, "first", cc=other), spot.twin)
+            copies.arrive("c_yh", s, at(s, 1 - y, 1 - x, "second", cc=other), spot.twin)
+    copies.close()
+
+
+def dp_of(s, yy, cc):
+    return (s * 2 + yy) * 2 + cc
+
+
+def gather_kernel(n_planes, n, *refs):
+    ins, outs, (send, recv, local) = refs[:n], refs[n : 2 * n], refs[2 * n :]
+    spot = Spot(n_planes)
+    half = ins[0].shape[0] // 2
+
+    def views(s, yy, cc, xx, part):
+        b = dp_of(s, yy, cc) * 2 + xx
+        if part == "all":
+            return [o.at[b] for o in outs]
+        if part == "first":
+            return [outs[0].at[b, pl.ds(0, half)]] + [o.at[b] for o in outs[1:]]
+        return [outs[0].at[b, pl.ds(half, half)]]
+
+    own = [
+        pltpu.make_async_copy(ins[i], outs[i].at[spot.dp * 2 + spot.x], local.at[i])
+        for i in range(n)
+    ]
+    for c in own:
+        c.start()
+    spot.greet()
+    copies = Copies(SPREAD_GROUPS, n_planes, n, send, recv)
+    spread(spot, copies, list(ins), views, True)
+    for c in own:
+        c.wait()
+
+
+def gather_everywhere(arrays, n_dp, collective_id):
+    n, n_planes = len(arrays), n_dp // 4
+    sems = (len(SPREAD_GROUPS) * n_planes, n)
+    return pl.pallas_call(
+        functools.partial(gather_kernel, n_planes, n),
+        out_shape=[jax.ShapeDtypeStruct((2 * n_dp,) + a.shape, a.dtype) for a in arrays],
+        in_specs=[ANY] * n,
+        out_specs=[ANY] * n,
+        scratch_shapes=[
+            pltpu.SemaphoreType.DMA(sems),
+            pltpu.SemaphoreType.DMA(sems),
+            pltpu.SemaphoreType.DMA((n,)),
+        ],
+        compiler_params=pltpu.CompilerParams(collective_id=collective_id, has_side_effects=True),
+    )(*arrays)
+
+
+def fetch_kernel(n_planes, axes, *refs):
+    n = len(axes)
+    ins, (tokens, small), outs = refs[:n], refs[n : n + 2], refs[n + 2 : 2 * n + 2]
+    sequence, smalls = refs[2 * n + 2 : 2 * n + 4]
+    send, recv, local, x_send, x_recv = refs[2 * n + 4 :]
+    spot = Spot(n_planes)
+
+    def views(s, yy, cc, xx, part):
+        i = dp_of(s, yy, cc)
+        places = []
+        for o, a, axis in zip(outs, ins, axes):
+            size = a.shape[axis]
+            span = pl.ds(pl.multiple_of(i * size, size), size)
+            places.append(o.at[span] if axis == 0 else o.at[:, span])
+        return places + [smalls.at[xx, i]]
+
+    sources = list(ins) + [small]
+    mine = views(spot.z, spot.y, spot.core, spot.x, "all")
+    own = [pltpu.make_async_copy(a, v, local.at[i]) for i, (a, v) in enumerate(zip(sources, mine))]
+    own.append(pltpu.make_async_copy(tokens, sequence.at[spot.x], local.at[n + 1]))
+    for c in own:
+        c.start()
+    spot.greet()
+
+    def across(i, src, dst):
+        return pltpu.make_async_remote_copy(
+            src_ref=src, dst_ref=dst, send_sem=x_send.at[i], recv_sem=x_recv.at[i],
+            device_id=spot.across, device_id_type=MESH,
+        )
+
+    across(0, tokens, sequence.at[spot.x]).start()
+    copies = Copies(SPREAD_GROUPS, n_planes, n + 1, send, recv)
+    spread(spot, copies, sources, views, False)
+    for c in own:
+        c.wait()
+    across(1, smalls.at[spot.x], smalls.at[spot.x]).start()
+    across(0, tokens, sequence.at[spot.x]).wait_send()
+    across(1, smalls.at[spot.x], smalls.at[spot.x]).wait_send()
+    across(0, sequence.at[1 - spot.x], sequence.at[1 - spot.x]).wait_recv()
+    across(1, smalls.at[1 - spot.x], smalls.at[1 - spot.x]).wait_recv()
+
+
+def fetch(arrays, axes, tokens, small, n_dp, collective_id):
+    n, n_planes = len(arrays), n_dp // 4
+    sems = (len(SPREAD_GROUPS) * n_planes, n + 1)
+
+    def whole(a, axis):
+        shape = list(a.shape)
+        shape[axis] *= n_dp
+        return jax.ShapeDtypeStruct(tuple(shape), a.dtype)
+
+    return pl.pallas_call(
+        functools.partial(fetch_kernel, n_planes, axes),
+        out_shape=[whole(a, axis) for a, axis in zip(arrays, axes)]
+        + [
+            jax.ShapeDtypeStruct((2,) + tokens.shape, tokens.dtype),
+            jax.ShapeDtypeStruct((2, n_dp) + small.shape, small.dtype),
+        ],
+        in_specs=[ANY] * (n + 2),
+        out_specs=[ANY] * (n + 2),
+        scratch_shapes=[
+            pltpu.SemaphoreType.DMA(sems),
+            pltpu.SemaphoreType.DMA(sems),
+            pltpu.SemaphoreType.DMA((n + 2,)),
+            pltpu.SemaphoreType.DMA((2,)),
+            pltpu.SemaphoreType.DMA((2,)),
+        ],
+        compiler_params=pltpu.CompilerParams(collective_id=collective_id, has_side_effects=True),
+    )(*arrays, tokens, small)
+
+
+REDUCE_GROUPS = ("c_yx", "c_y", "c_x", "c_own", "x_half", "y_half", "y_all", "x_all", "z_up", "z_down")
+
+
+def add_up(target, sources):
+    rows = target.shape[0]
+    step = 16 if rows % 16 == 0 else rows
+
+    def body(i, carry):
+        span = pl.ds(pl.multiple_of(i * step, step), step)
+        total = sources[0][span, :].astype(jnp.float32)
+        for source in sources[1:]:
+            total = total + source[span, :].astype(jnp.float32)
+        target[span, :] = total.astype(target.dtype)
+        return carry
+
+    lax.fori_loop(0, rows // step, body, 0)
+
+
+class Sums:
+    @staticmethod
+    def scratch(shapes, dtypes, n_planes, use_x):
+        n = len(shapes)
+        kinds = 4 if use_x else 2
+        out = []
+        for i, (shape, dtype) in enumerate(zip(shapes, dtypes)):
+            half = (shape[0] // 2, shape[1]) if i == 0 else shape
+            out.append(pltpu.VMEM((kinds, n_planes) + shape, dtype))
+            out.append(pltpu.VMEM((kinds, n_planes) + shape, dtype))
+            out.append(pltpu.VMEM((n_planes,) + shape, dtype))
+            out.append(pltpu.VMEM((n_planes,) + shape, dtype))
+            out.append(pltpu.VMEM((n_planes,) + shape, dtype))
+            if use_x:
+                out.append(pltpu.VMEM((n_planes,) + shape, dtype))
+                out.append(pltpu.VMEM((n_planes,) + half, dtype))
+                out.append(pltpu.VMEM((n_planes,) + (half if i == 0 else (8, 128)), dtype))
+        sems = (len(REDUCE_GROUPS) * n_planes, n)
+        out.append(pltpu.SemaphoreType.DMA(sems))
+        out.append(pltpu.SemaphoreType.DMA(sems))
+        out.append(pltpu.SemaphoreType.DMA((kinds * n_planes, n)))
+        return out
+
+
+def reduce_scatter(spot, ins, outs, scratch, use_x):
+    n, n_planes = len(outs), spot.n_planes
+    per = 8 if use_x else 5
+    send, recv, local = scratch[n * per :]
+    sets = [scratch[i * per : (i + 1) * per] for i in range(n)]
+    mine = [s[0] for s in sets]
+    twin = [s[1] for s in sets]
+    above = [s[2] for s in sets]
+    below = [s[3] for s in sets]
+    side = [s[4] for s in sets]
+    across = [s[5] for s in sets] if use_x else None
+    first = [s[6] for s in sets] if use_x else None
+    second = [sets[0][7]] if use_x else None
+    copies = Copies(REDUCE_GROUPS, n_planes, n, send, recv)
+    y, x, core = spot.y, spot.x, spot.core
+    order = spot.far_first()
+    kinds = (["c_yx", "c_y", "c_x", "c_own"] if use_x else ["c_y", "c_own"])
+    places = {"c_yx": (1 - y, 1 - x), "c_y": (1 - y, x), "c_x": (y, 1 - x), "c_own": (y, x)}
+
+    def load(k, j):
+        s = order[j]
+        yy, xx = places[kinds[k]]
+        for i, ref in enumerate(ins(s, yy, core, xx)):
+            yield pltpu.make_async_copy(ref, mine[i].at[k, s], local.at[k * n_planes + s, i])
+
+    for j in range(n_planes):
+        for k in range(len(kinds)):
+            for c in load(k, j):
+                c.start()
+    spot.greet()
+    for j in range(n_planes):
+        s = order[j]
+        for k, name in enumerate(kinds):
+            yy, xx = places[name]
+            copies.start(None, name, s, ins(s, yy, 1 - core, xx), [t.at[k, s] for t in twin], spot.twin)
+
+    def ready(k, j):
+        s = order[j]
+        for c in load(k, j):
+            c.wait()
+        copies.arrive(kinds[k], s, [t.at[k, s] for t in twin], spot.twin)
+
+    half = sets[0][0].shape[2] // 2
+
+    def corner(j):
+        s = order[j]
+        ready(0, j)
+        for i in range(n):
+            add_up(mine[i].at[0, s], [mine[i].at[0, s], twin[i].at[0, s]])
+        head = [mine[0].at[0, s, pl.ds(0, half)]] + [m.at[0, s] for m in mine[1:]]
+        copies.start(None, "x_half", s, head, [f.at[s] for f in first], spot.across)
+        copies.start(None, "y_half", s, [mine[0].at[0, s, pl.ds(half, half)]], [second[0].at[s]], spot.side)
+
+    def sides(j):
+        s = order[j]
+        k = kinds.index("c_y")
+        ready(k, j)
+        if use_x:
+            copies.arrive("x_half", s, [f.at[s] for f in first], spot.across)
+            for i in range(n):
+                if i == 0:
+                    a, b = pl.ds(0, half), pl.ds(half, half)
+                    add_up(mine[0].at[k, s, a], [mine[0].at[k, s, a], twin[0].at[k, s, a], first[0].at[s]])
+                    add_up(mine[0].at[k, s, b], [mine[0].at[k, s, b], twin[0].at[k, s, b]])
+                else:
+                    add_up(mine[i].at[k, s], [mine[i].at[k, s], twin[i].at[k, s], first[i].at[s]])
+        else:
+            for i in range(n):
+                add_up(mine[i].at[k, s], [mine[i].at[k, s], twin[i].at[k, s]])
+        copies.start(None, "y_all", s, [m.at[k, s] for m in mine], [t.at[s] for t in side], spot.side)
+        if not use_x:
+            return
+        k = kinds.index("c_x")
+        ready(k, j)
+        copies.arrive("y_half", s, [second[0].at[s]], spot.side)
+        for i in range(n):
+            if i == 0:
+                a, b = pl.ds(0, half), pl.ds(half, half)
+                add_up(mine[0].at[k, s, a], [mine[0].at[k, s, a], twin[0].at[k, s, a]])
+                add_up(mine[0].at[k, s, b], [mine[0].at[k, s, b], twin[0].at[k, s, b], second[0].at[s]])
+            else:
+                add_up(mine[i].at[k, s], [mine[i].at[k, s], twin[i].at[k, s]])
+        copies.start(None, "x_all", s, [m.at[k, s] for m in mine], [t.at[s] for t in across], spot.across)
+
+    def column(j):
+        s = order[j]
+        k = kinds.index("c_own")
+        ready(k, j)
+        copies.arrive("y_all", s, [t.at[s] for t in side], spot.side)
+        if use_x:
+            copies.arrive("x_all", s, [t.at[s] for t in across], spot.across)
+        here = [[mine[i].at[k, s], twin[i].at[k, s], side[i].at[s]] + ([across[i].at[s]] if use_x else []) for i in range(n)]
+        if j == n_planes - 1:
+            from_above = [t.at[s] for t in above]
+            from_below = [t.at[s] for t in below]
+
+            def wait_above():
+                copies.arrive("z_down", s, from_above, spot.up)
+
+            def wait_below():
+                copies.arrive("z_up", s, from_below, spot.down)
+
+            when(spot.has_up, wait_above)
+            when(spot.has_down, wait_below)
+
+            def both():
+                for i in range(n):
+                    add_up(outs[i], here[i] + [from_above[i], from_below[i]])
+
+            def one_above():
+                for i in range(n):
+                    add_up(outs[i], here[i] + [from_above[i]])
+
+            def one_below():
+                for i in range(n):
+                    add_up(outs[i], here[i] + [from_below[i]])
+
+            when(spot.has_up & spot.has_down, both)
+            when(spot.has_up & (spot.z == 0), one_above)
+            when(spot.has_down & (spot.z == n_planes - 1), one_below)
+            return
+        goes_down = s < spot.z
+        goes_up = s > spot.z
+        for goes, more, group, buffers, device, source in (
+            (goes_down, spot.has_up, "z_down", above, spot.down, spot.up),
+            (goes_up, spot.has_down, "z_up", below, spot.up, spot.down),
+        ):
+            arrived = [t.at[s] for t in buffers]
+
+            def partial():
+                copies.arrive(group, s, arrived, source)
+                for i in range(n):
+                    add_up(mine[i].at[k, s], here[i] + [arrived[i]])
+
+            def alone():
+                for i in range(n):
+                    add_up(mine[i].at[k, s], here[i])
+
+            when(goes & more, partial)
+            when(goes & jnp.logical_not(more), alone)
+            copies.start(goes, group, s, [m.at[k, s] for m in mine], [t.at[s] for t in buffers], device)
+
+    for step in range(n_planes + 2):
+        if use_x and step < n_planes:
+            corner(step)
+        if 0 <= step - 1 < n_planes:
+            sides(step - 1)
+        if 0 <= step - 2 < n_planes:
+            column(step - 2)
+    copies.close()
+
+
+def sum_kernel(n_planes, n, *refs):
+    ins, outs, scratch = refs[:n], refs[n : 2 * n], refs[2 * n :]
+    spot = Spot(n_planes)
+
+    def blocks(s, yy, cc, xx):
+        return [a.at[dp_of(s, yy, cc) * 2 + xx] for a in ins]
+
+    reduce_scatter(spot, blocks, outs, scratch, True)
+
+
+def sum_everywhere(arrays, out_dtypes, n_dp, collective_id):
+    n, n_planes = len(arrays), n_dp // 4
+    shapes = [a.shape[1:] for a in arrays]
+    return pl.pallas_call(
+        functools.partial(sum_kernel, n_planes, n),
+        out_shape=[jax.ShapeDtypeStruct(s, t) for s, t in zip(shapes, out_dtypes)],
+        in_specs=[ANY] * n,
+        out_specs=[pl.BlockSpec(memory_space=pltpu.VMEM)] * n,
+        scratch_shapes=Sums.scratch(shapes, [a.dtype for a in arrays], n_planes, True),
+        compiler_params=pltpu.CompilerParams(
+            collective_id=collective_id, has_side_effects=True, vmem_limit_bytes=56 << 20
+        ),
+    )(*arrays)
+
+
+def return_kernel(n_planes, axes, *refs):
+    n = len(axes)
+    ins, outs = refs[:n], refs[n : 2 * n]
+    scratch, (tile_sum, tile_in, x_send, x_recv) = refs[2 * n : -4], refs[-4:]
+    spot = Spot(n_planes)
+
+    def blocks(s, yy, cc, xx):
+        i = dp_of(s, yy, cc)
+        places = []
+        for j, (a, o, axis) in enumerate(zip(ins, outs, axes)):
+            size = o.shape[axis] * (2 if j == n - 1 else 1)
+            span = pl.ds(pl.multiple_of(i * size, size), size)
+            places.append(a.at[span] if axis == 0 else a.at[:, span])
+        return places
+
+    reduce_scatter(spot, blocks, list(outs[:-1]) + [tile_sum], scratch, False)
+    rows = tile_in.shape[0]
+    swap = pltpu.make_async_remote_copy(
+        src_ref=tile_sum.at[pl.ds(pl.multiple_of((1 - spot.x) * rows, rows), rows)], dst_ref=tile_in,
+        send_sem=x_send, recv_sem=x_recv, device_id=spot.across, device_id_type=MESH,
+    )
+    swap.start()
+    swap.wait()
+    outs[-1][...] = tile_sum[pl.ds(pl.multiple_of(spot.x * rows, rows), rows), :] + tile_in[...]
+
+
+def sum_back(arrays, axes, n_dp, collective_id):
+    n, n_planes = len(arrays), n_dp // 4
+
+    def part(a, axis):
+        shape = list(a.shape)
+        shape[axis] //= n_dp
+        return tuple(shape)
+
+    shapes = [part(a, axis) for a, axis in zip(arrays, axes)]
+    tile = (shapes[-1][0] // 2, shapes[-1][1])
+    return pl.pallas_call(
+        functools.partial(return_kernel, n_planes, axes),
+        out_shape=[jax.ShapeDtypeStruct(s, jnp.float32) for s in shapes[:-1] + [tile]],
+        in_specs=[ANY] * n,
+        out_specs=[pl.BlockSpec(memory_space=pltpu.VMEM)] * n,
+        scratch_shapes=Sums.scratch(shapes, [a.dtype for a in arrays], n_planes, False)
+        + [
+            pltpu.VMEM(shapes[-1], jnp.float32),
+            pltpu.VMEM(tile, jnp.float32),
+            pltpu.SemaphoreType.DMA(()),
+            pltpu.SemaphoreType.DMA(()),
+        ],
+        compiler_params=pltpu.CompilerParams(
+            collective_id=collective_id, has_side_effects=True, vmem_limit_bytes=56 << 20
+        ),
+    )(*arrays)
+
+
+def swap_halves(own, x):
+    return lax.ppermute(own, TENSOR, [(0, 1), (1, 0)])
+
+
+def halves_sum(partial, rows, x):
+    kept = lax.dynamic_slice_in_dim(partial, x * rows, rows, 0)
+    given = lax.dynamic_slice_in_dim(partial, (1 - x) * rows, rows, 0).astype(jnp.bfloat16)
+    return kept + swap_halves(given, x).astype(jnp.float32)
+
+
+def gather_plan(
+    tokens,
+    attention_gain,
+    expert_norm_gain,
+    query_projection,
+    key_projection,
+    value_projection,
+    output_projection,
+    router,
+    shared_gate_matrix,
+    shared_up_matrix,
+    shared_down_matrix,
+    expert_gate_matrix,
+    expert_up_matrix,
+    expert_down_matrix,
+    document_lengths,
+    expert_indices,
+    cotangent,
+):
+    n_dp = lax.axis_size(DP)
+    x = lax.axis_index(TENSOR)
+    dp = lax.axis_index(DP)
+    own_rows, model_dim = tokens.shape
+    sequence_length = own_rows * 2
+    experts = n_dp
+    top_k = expert_indices.shape[1]
+    capacity = sequence_length * top_k * 4 // (3 * experts)
+    bf16, f32 = jnp.bfloat16, jnp.float32
+
+    def dot(a, b):
+        return jnp.dot(a, b, preferred_element_type=f32)
+
+    width = attention_gain.shape[0]
+    small = jnp.concatenate([attention_gain, expert_norm_gain, router.reshape(-1)])
+    small = jnp.pad(small, (0, -small.shape[0] % 2048)).reshape(-1, 128)
+    axes = (0, 0, 0, 1)
+    query_all, key_all, value_all, out_all, sequence, smalls = fetch(
+        [query_projection, key_projection, value_projection, output_projection],
+        axes, tokens, small, n_dp, 1,
+    )
+    flat = smalls.swapaxes(0, 1).reshape(2 * n_dp, -1)
+    first_gain = flat[:, :width].reshape(-1).astype(f32)
+    second_gain = flat[:, width : 2 * width].reshape(-1).astype(f32)
+    router_full = flat[:, 2 * width : (2 + experts) * width].reshape(model_dim, experts)
+
+    hidden = shared_gate_matrix.shape[1] // n_dp
+    hidden_pad = -(-hidden // 16) * 16
+
+    def slices(transposed):
+        blocks = transposed.reshape(n_dp, hidden, -1)
+        return jnp.pad(blocks, ((0, 0), (0, hidden_pad - hidden), (0, 0)))
+
+    shared_out = jnp.stack(
+        [slices(shared_gate_matrix.T), slices(shared_up_matrix.T), slices(shared_down_matrix)], axis=1
+    )
+    shared_in = lax.all_to_all(shared_out, DP, split_axis=0, concat_axis=0, tiled=True)
+    shared_rows = jnp.moveaxis(shared_in, 0, 2).reshape(3, hidden_pad, model_dim)
+    sgate_t, sup_t, sdown = shared_rows[0], shared_rows[1], shared_rows[2]
+
+    full_tokens = sequence.reshape(sequence_length, model_dim).astype(f32)
+    full_scale = lax.rsqrt(jnp.mean(full_tokens * full_tokens, axis=-1, keepdims=True) + norm_eps)
+    full_one = (full_tokens * full_scale * first_gain).astype(bf16)
+    input_values = tokens.astype(f32)
+    scale_one = lax.dynamic_slice_in_dim(full_scale, x * own_rows, own_rows, 0)
+    q_heads = query_all.shape[1] // HEAD_SIZE
+    kv_heads = key_all.shape[1] // HEAD_SIZE
+    group_size = q_heads // kv_heads
+    rotary_cosine, rotary_sine = rotation(sequence_length, HEAD_SIZE)
+    query_unrotated = dot(full_one, query_all).reshape(sequence_length, q_heads, HEAD_SIZE)
+    key_unrotated = dot(full_one, key_all).reshape(sequence_length, kv_heads, HEAD_SIZE)
+    rows_of_query = (
+        apply_rotary(query_unrotated, rotary_cosine, rotary_sine)
+        .astype(bf16)
+        .reshape(sequence_length, kv_heads, group_size, HEAD_SIZE)
+    )
+    key_rows = apply_rotary(key_unrotated, rotary_cosine, rotary_sine).astype(bf16)
+    rows_of_value = dot(full_one, value_all).astype(bf16).reshape(sequence_length, kv_heads, HEAD_SIZE)
+    doc_ends = jnp.cumsum(document_lengths[0])
+    positions = jnp.arange(sequence_length, dtype=jnp.int32)
+    doc_ids = jnp.sum((positions[:, None] >= doc_ends[None, :]).astype(jnp.int32), axis=-1)
+    score_scale = HEAD_SIZE ** (-0.5)
+    allowed = (doc_ids[:, None] == doc_ids[None, :]) & (positions[:, None] >= positions[None, :])
+    scores = (
+        jnp.einsum("qkgd,skd->kgqs", rows_of_query, key_rows, preferred_element_type=f32) * score_scale
+    )
+    scores = jnp.where(allowed, scores, neg_big)
+    exp_scores = jnp.exp(scores - jnp.max(scores, axis=-1, keepdims=True))
+    attn_probs = exp_scores / jnp.sum(exp_scores, axis=-1, keepdims=True)
+    probs_low = attn_probs.astype(bf16)
+    mixed_heads = (
+        jnp.einsum("kgqs,skd->qkgd", probs_low, rows_of_value, preferred_element_type=f32)
+        .reshape(sequence_length, q_heads * HEAD_SIZE)
+        .astype(bf16)
+    )
+    residual = input_values + halves_sum(dot(mixed_heads, out_all), own_rows, x)
+
+    scale_two = lax.rsqrt(jnp.mean(residual * residual, axis=-1, keepdims=True) + norm_eps)
+    normed_two = (residual * scale_two * second_gain).astype(bf16)
+    logits = dot(normed_two, router_full)
+    own_indices = lax.dynamic_slice_in_dim(expert_indices, x * own_rows, own_rows, 0)
+    chosen = own_indices[:, :, None] == jnp.arange(experts, dtype=jnp.int32)[None, None, :]
+    selected = jnp.sum(jnp.where(chosen, logits[:, None, :], 0.0), axis=-1)
+    gate_exp = jnp.exp(selected - jnp.max(selected, axis=-1, keepdims=True))
+    gate_probs = gate_exp / jnp.sum(gate_exp, axis=-1, keepdims=True)
+    gates = jnp.sum(jnp.where(chosen, gate_probs[:, :, None], 0.0), axis=1)
+
+    (cotangent_all,) = gather_everywhere([cotangent], n_dp, 3)
+    normed_all, gates_all = gather_everywhere([normed_two, gates.T], n_dp, 2)
+
+    normed_seq = normed_all.reshape(n_dp, sequence_length, model_dim)
+    grad_seq = cotangent_all.reshape(n_dp, sequence_length, model_dim)
+    gate_seq = lax.dynamic_index_in_dim(gates_all, dp, 1, keepdims=False).reshape(n_dp, sequence_length)
+    routed = gate_seq > 0.0
+    rank = jnp.cumsum(routed.astype(jnp.int32), axis=1) - 1
+    pick = (rank[:, None, :] == jnp.arange(capacity, dtype=jnp.int32)[None, :, None]) & routed[:, None, :]
+    pick_low = pick.astype(bf16)
+    rows = n_dp * capacity
+    received = jnp.einsum("sjt,std->sjd", pick_low, normed_seq, preferred_element_type=f32)
+    received = received.astype(bf16).reshape(rows, model_dim)
+    grad_rows = jnp.einsum("sjt,std->sjd", pick_low, grad_seq, preferred_element_type=f32)
+    grad_rows = grad_rows.astype(bf16).reshape(rows, model_dim)
+    gate_rows = jnp.sum(jnp.where(pick, gate_seq[:, None, :], 0.0), axis=-1).reshape(rows, 1)
+    w_gate, w_up, w_down = expert_gate_matrix[0], expert_up_matrix[0], expert_down_matrix[0]
+    gate_pre = dot(received, w_gate)
+    up_pre = dot(received, w_up)
+    hidden_rows = silu(gate_pre) * up_pre
+    gated_hidden = (hidden_rows * gate_rows).astype(bf16)
+    produced = dot(gated_hidden, w_down).astype(bf16)
+    grad_hidden = dot(grad_rows, w_down.T)
+    grad_gate_rows = jnp.sum(hidden_rows * grad_hidden, axis=-1).reshape(n_dp, capacity)
+    grad_hidden = grad_hidden * gate_rows
+    grad_gate = (grad_hidden * up_pre * silu_slope(gate_pre)).astype(bf16)
+    grad_up = (grad_hidden * silu(gate_pre)).astype(bf16)
+    grad_received = (dot(grad_gate, w_gate.T) + dot(grad_up, w_up.T)).astype(bf16)
+    expert_gate_gradient = dot(received.T, grad_gate)[None]
+    expert_up_gradient = dot(received.T, grad_up)[None]
+    expert_down_gradient = dot(gated_hidden.T, grad_rows)[None]
+
+    normed_flat = normed_all.reshape(-1, model_dim)
+    grad_flat = cotangent_all.reshape(-1, model_dim)
+    gate_shared = dot(normed_flat, sgate_t.T)
+    up_shared = dot(normed_flat, sup_t.T)
+    hidden_shared = (silu(gate_shared) * up_shared).astype(bf16)
+    grad_hidden_sh = dot(grad_flat, sdown.T)
+    grad_gate_sh = (grad_hidden_sh * up_shared * silu_slope(gate_shared)).astype(bf16)
+    grad_up_sh = (grad_hidden_sh * silu(gate_shared)).astype(bf16)
+    shared_grads = jnp.stack(
+        [dot(grad_gate_sh.T, normed_flat), dot(grad_up_sh.T, normed_flat), dot(hidden_shared.T, grad_flat)]
+    ).astype(bf16)
+
+    def scatter(rows_out, shared_part):
+        back = jnp.einsum(
+            "sjt,sjd->std", pick_low, rows_out.reshape(n_dp, capacity, model_dim), preferred_element_type=f32
+        )
+        total = back.reshape(-1, model_dim) + shared_part
+        return total.astype(bf16).reshape(2 * n_dp, own_rows, model_dim)
+
+    output_parts = scatter(produced, dot(hidden_shared, sdown))
+    normed_parts = scatter(grad_received, dot(grad_gate_sh, sgate_t) + dot(grad_up_sh, sup_t))
+    grad_gate_tokens = jnp.sum(jnp.where(pick, grad_gate_rows[:, :, None], 0.0), axis=1)
+    grad_gate_parts = jnp.where(
+        jnp.arange(experts)[None, :, None] == dp, grad_gate_tokens.reshape(2 * n_dp, 1, own_rows), 0.0
+    )
+    grad_normed_two, grad_gates_t = sum_everywhere([normed_parts, grad_gate_parts], [f32, f32], n_dp, 4)
+    (ffn_own,) = sum_everywhere([output_parts], [f32], n_dp, 5)
+    output = (residual + ffn_own).astype(bf16)
+
+    grad_gates = grad_gates_t.T
+    grad_logits = (
+        gates * (grad_gates - jnp.sum(gates * grad_gates, axis=-1, keepdims=True))
+    ).astype(bf16)
+    grad_normed_two = grad_normed_two + dot(grad_logits, router_full.T)
+    grad_router_part = dot(normed_two.T, grad_logits)
+    grad_residual, grad_gain_two = rms_back(grad_normed_two, residual, scale_two, second_gain)
+    grad_residual = grad_residual + cotangent.astype(f32)
+    grad_low = grad_residual.astype(bf16)
+    grad_other = swap_halves(grad_low, x)
+    grad_attn = jnp.where(
+        x == 0, jnp.concatenate([grad_low, grad_other]), jnp.concatenate([grad_other, grad_low])
+    )
+
+    grad_wout = dot(mixed_heads.T, grad_attn)
+    grad_mixed = (
+        dot(grad_attn, out_all.T).astype(bf16).reshape(sequence_length, kv_heads, group_size, HEAD_SIZE)
+    )
+    grad_values = jnp.einsum("kgqs,qkgd->skd", probs_low, grad_mixed, preferred_element_type=f32)
+    grad_probs = jnp.einsum("qkgd,skd->kgqs", grad_mixed, rows_of_value, preferred_element_type=f32)
+    inner_sum = jnp.sum(attn_probs * grad_probs, axis=-1, keepdims=True)
+    grad_scores = (attn_probs * (grad_probs - inner_sum)).astype(bf16)
+    grad_query = (
+        jnp.einsum("kgqs,skd->qkgd", grad_scores, key_rows, preferred_element_type=f32) * score_scale
+    ).reshape(sequence_length, q_heads, HEAD_SIZE)
+    grad_keys = (
+        jnp.einsum("kgqs,qkgd->skd", grad_scores, rows_of_query, preferred_element_type=f32) * score_scale
+    )
+    grad_q_raw = rotate_back(grad_query, rotary_cosine, rotary_sine).astype(bf16)
+    grad_q_raw = grad_q_raw.reshape(sequence_length, q_heads * HEAD_SIZE)
+    grad_k_raw = rotate_back(grad_keys, rotary_cosine, rotary_sine).astype(bf16)
+    grad_k_raw = grad_k_raw.reshape(sequence_length, kv_heads * HEAD_SIZE)
+    grad_v_low = grad_values.astype(bf16).reshape(sequence_length, kv_heads * HEAD_SIZE)
+    grad_wquery = dot(full_one.T, grad_q_raw).astype(bf16)
+    grad_wkey = dot(full_one.T, grad_k_raw).astype(bf16)
+    grad_wvalue = dot(full_one.T, grad_v_low).astype(bf16)
+    grad_normed_one = halves_sum(
+        dot(grad_q_raw, query_all.T) + dot(grad_k_raw, key_all.T) + dot(grad_v_low, value_all.T), own_rows, x
+    )
+    grad_inputs, grad_gain_one = rms_back(grad_normed_one, input_values, scale_one, first_gain)
+    grad_inputs = grad_inputs + grad_residual
+
+    def by_owner(v):
+        return v.reshape(2 * n_dp, -1)
+
+    tiles = jnp.concatenate([by_owner(grad_gain_one), by_owner(grad_gain_two), by_owner(grad_router_part)], axis=1)
+    tiles = jnp.pad(tiles, ((0, 0), (0, -tiles.shape[1] % 2048)))
+    small_rows = tiles.shape[1] // 128
+    sums = sum_back(
+        [grad_wquery, grad_wkey, grad_wvalue, grad_wout.astype(bf16), tiles.reshape(-1, 128)],
+        axes + (0,), n_dp, 6,
+    )
+    mine = sums[4].reshape(-1)
+    gain_one_own, gain_two_own = mine[:width], mine[width : 2 * width]
+    router_own = mine[2 * width : (2 + experts) * width].reshape(width, experts)
+    returned = lax.all_to_all(
+        shared_grads.reshape(3, hidden_pad, n_dp, -1).transpose(2, 0, 1, 3),
+        DP, split_axis=0, concat_axis=0, tiled=True,
+    )[:, :, :hidden]
+    returned = returned.transpose(1, 0, 2, 3).reshape(3, n_dp * hidden, -1).astype(f32)
+    return (
+        output,
+        grad_inputs,
+        gain_one_own,
+        gain_two_own,
+        sums[0],
+        sums[1],
+        sums[2],
+        sums[3],
+        router_own,
+        returned[0].T,
+        returned[1].T,
+        returned[2],
+        expert_gate_gradient,
+        expert_up_gradient,
+        expert_down_gradient,
+    )
+
+
+def shards(*arguments):
+    tokens, expert_gate_matrix = arguments[0], arguments[11]
+    n_dp, n_tensor = lax.axis_size(DP), lax.axis_size(TENSOR)
+    gathered = n_dp * n_tensor * tokens.shape[0] * tokens.shape[1] * 2
+    if n_tensor == 2 and n_dp % 4 == 0 and expert_gate_matrix.shape[0] == 1 and gathered <= 32 << 20:
+        return gather_plan(*arguments)
+    return exchange_plan(*arguments)
+
+
 def solution(mesh):
     placed = (
-        P(("dp", "tensor"), None),
-        P(("dp", "tensor")),
-        P(("dp", "tensor")),
-        P("dp", "tensor"),
-        P("dp", "tensor"),
-        P("dp", "tensor"),
-        P("tensor", "dp"),
-        P(("dp", "tensor"), None),
-        P("dp", "tensor"),
-        P("dp", "tensor"),
-        P("tensor", "dp"),
-        P("dp", None, "tensor"),
-        P("dp", None, "tensor"),
-        P("dp", "tensor", None),
-        P("dp", None),
-        P("dp", None),
-        P(("dp", "tensor"), None),
+        P((DP, TENSOR), None),
+        P((DP, TENSOR)),
+        P((DP, TENSOR)),
+        P(DP, TENSOR),
+        P(DP, TENSOR),
+        P(DP, TENSOR),
+        P(TENSOR, DP),
+        P((DP, TENSOR), None),
+        P(DP, TENSOR),
+        P(DP, TENSOR),
+        P(TENSOR, DP),
+        P(DP, None, TENSOR),
+        P(DP, None, TENSOR),
+        P(DP, TENSOR, None),
+        P(DP, None),
+        P(DP, None),
+        P((DP, TENSOR), None),
     )
     return jax.shard_map(
         shards,
         mesh=mesh,
         in_specs=placed,
         out_specs=(
-            P(("dp", "tensor"), None),
-            P(("dp", "tensor"), None),
-            P(("dp", "tensor")),
-            P(("dp", "tensor")),
-            P("dp", "tensor"),
-            P("dp", "tensor"),
-            P("dp", "tensor"),
-            P("tensor", "dp"),
-            P(("dp", "tensor"), None),
-            P("dp", "tensor"),
-            P("dp", "tensor"),
-            P("tensor", "dp"),
-            P("dp", None, "tensor"),
-            P("dp", None, "tensor"),
-            P("dp", "tensor", None),
+            P((DP, TENSOR), None),
+            P((DP, TENSOR), None),
+            P((DP, TENSOR)),
+            P((DP, TENSOR)),
+            P(DP, TENSOR),
+            P(DP, TENSOR),
+            P(DP, TENSOR),
+            P(TENSOR, DP),
+            P((DP, TENSOR), None),
+            P(DP, TENSOR),
+            P(DP, TENSOR),
+            P(TENSOR, DP),
+            P(DP, None, TENSOR),
+            P(DP, None, TENSOR),
+            P(DP, TENSOR, None),
         ),
         check_vma=False,
     )

time: 2390 us -> 943 us (0.39)
  waiting for transfers between devices: 1590 us -> 3.37 us
  Pallas kernels: 0 us -> 487 us
  blocking collectives: 299 us -> 0 us
  matrix products: 216 us -> 293 us
  local copies, waits for them, and re-layouts: 147 us -> 92.9 us
  starting transfers between devices: 53.1 us -> 15 us
    reduce_scatter x11 -> x0, waiting for transfers between devices: 804 us -> none  [the longest x1 131 us: shards(): lax.psum_scatter(grad_sup, 'dp', scatter_dimension=0, tiled=True)]
    pallas_call x0 -> x6, Pallas kernels: none -> 487 us  [the longest x2 176 us: gather_everywhere(): pl.pallas_call(functools.partial(gather_kernel, n_planes, n), out_shape=[...]
    all_to_all x4 -> x2, waiting for transfers between devices: 372 us -> 0.01 us  [the longest x1 0.01 us: gather_plan(): lax.all_to_all(shared_out, DP, split_axis=0, concat_axis=0, tiled=True)]
    all_gather x11 -> x0, waiting for transfers between devices: 371 us -> none  [the longest x1 170 us: dense_fetch(): lax.all_gather(shared_down_matrix, 'dp', axis=1, tiled=True)]
    all_gather x1 -> x0, blocking collectives: 222 us -> none  [shards(): lax.all_gather(router, ('dp', 'tensor'), axis=0, tiled=True)]
    unnamed x2 -> x0, blocking collectives: 77.7 us -> none
    dot_general x40 -> x42, matrix products: 215 us -> 289 us  [the longest x33 240 us: dot(): return jnp.dot(a, b, preferred_element_type=f32)]
    gather x4 -> x0, local copies, waits for them, and re-layouts: 70.1 us -> none  [the longest x1 17.7 us: shards(): grad_ffn[token_of_slot] * gate_of_slot[:, None]]
  transfers between devices with their start and end apart: 28 -> 5, of which waited for: 21 -> 1; matrix products, arithmetic and copies ran while one was open for 15% -> 26% of each run, Pallas kernels for 0% -> 28%
where the time goes in v1:
time: 943 us; the launch traced here: 931 us
  Pallas kernels  487 us (52%)
  matrix products  293 us (31%)
  local copies, waits for them, and re-layouts  92.9 us (10%)
  other arithmetic  38.2 us (4%)
  starting transfers between devices  15 us (2%)
    dot_general x33, matrix products, dot(): return jnp.dot(a, b, preferred_element_type=f32)  240 us
    pallas_call x2, Pallas kernels, gather_everywhere(): pl.pallas_call(functools.partial(gather_kernel, n_planes, n), out_shape=[...  176 us
    pallas_call x2, Pallas kernels, sum_everywhere(): pl.pallas_call(functools.partial(sum_kernel, n_planes, n), out_shape=[jax...  155 us
    pallas_call x1, Pallas kernels, sum_back(): pl.pallas_call(functools.partial(return_kernel, n_planes, axes), out_shap...  82 us
    pallas_call x1, Pallas kernels, fetch(): pl.pallas_call(functools.partial(fetch_kernel, n_planes, axes), out_shape...  73.2 us
    dot_general x4, local copies, waits for them, and re-layouts, dot(): return jnp.dot(a, b, preferred_element_type=f32)  51.4 us
    dot_general x2, matrix products, scatter(): jnp.einsum('sjt,sjd->std', pick_low, rows_out.reshape(n_dp, capacity, mod...  27.7 us
  transfers between devices with their start and end apart: 5, of which 1 were waited for; matrix products, arithmetic and copies ran while one was open for 26% of the time, Pallas kernels for 28%

profile of v1, /device:TPU:24, one launch (start us, length us, event | category | flops | bytes accessed | tf_op | source)
XLA Modules:
  0.0 930.6 jit_solution(2335126321758131253)
XLA Ops:
  6.3 73.2 %shard_map.280 = (bf16[2048,1024]{1,0:T(8,128)(2,1)}, bf16[2048,256]{1,0:T(8,128)(2,1)}, bf16[2048,256]{1,0:T(8,128)(2,1)}, bf16[1024,2048]{1,0:T(8,128)(2,1)}, ...) custom-call(bf16[128,1024]{1,0:T(8,128)(2,1)} %refs_0_.2, bf16[128,256]{1,0:T(8,128)(2,1)} %refs_1_.1, ...), custom_call_target="tpu_custom_call" | custom-call | tf_op jit(solution)/shard_map/pallas_call | solution.py:715
  89.5 6.4 copy.172
  131.5 93.9 %shard_map.283 = bf16[32,128,2048]{2,1,0:T(8,128)(2,1)} custom-call(bf16[128,2048]{1,0:T(8,128)(2,1)} %refs_0_.3), custom_call_target="tpu_custom_call" | custom-call | tf_op jit(solution)/shard_map/pallas_call | solution.py:650
  225.4 21.3 %copy.150 = bf16[2048,4096]{1,0:T(8,128)(2,1)} copy(bf16[2048,4096]{0,1:T(8,128)(2,1)} %bitcast.285) | data formatting | bytes 33554432 | tf_op jit(solution)/shard_map/dot_general | solution.py:1048
  251.7 82.5 %shard_map.281 = (bf16[32,128,2048]{2,1,0:T(8,128)(2,1)}, f32[32,16,128]{2,1,0:T(8,128)}) custom-call(bf16[128,2048]{1,0:T(8,128)(2,1)} %copy-done.8, f32[16,128]{1,0:T(8,128)} %bitcast.342), custom_call_target="tpu_custom_call" | custom-call | tf_op jit(solution)/shard_map/pallas_call | solution.py:650
  337.1 9.5 %convolution_convert_fusion.1 = bf16[16,128,2048]{2,1,0:T(8,128)(2,1)} fusion(bf16[16,256,2048]{2,1,0:T(8,128)(2,1)} %bitcast.286, s32[16,256]{1,0:T(8,128)S(1)} %copy_bitcast_fusion.1, pred[16,256]{1,0:T(8,128)(4,1)S(1)} %broadcast_compare_fusion), kind=kOutput, calls=%fused_computation.13 | convolution fusion | flops 2152726528 | bytes 25186304 | tf_op jit(solution)/shard_map/sjt,std->sjd/dot_general | solution.py:1137
  346.6 7.8 convolution_convert_fusion.2
  354.4 6.2 fusion.8
  360.6 6.2 fusion.12
  366.8 11.1 %multiply_reduce_fusion = (f32[2048]{0:T(1024)S(1)}, f32[2048,704]{0,1:T(8,128)}) fusion(f32[2048,704]{0,1:T(8,128)S(1)} %fusion.8, f32[2048,704]{0,1:T(8,128)S(1)} %fusion.12, bf16[2048,2048]{1,0:T(8,128)(2,1)} %bitcast.308, bf16[1,704,2048]{2,1,0:T(8,128)(2,1)S(1)} %copy-done), kind=kOutput, calls=%fused_computation.7 | convolution fusion | flops 5915670528 | bytes 28581888 | tf_op jit(solution)/shard_map/dot_general | solution.py:1048
  380.8 9.0 multiply_convert_fusion
  389.9 11.1 %convolution_bitcast_fusion.3 = f32[1,704,2048]{2,1,0:T(8,128)} fusion(bf16[2048,704]{0,1:T(8,128)(2,1)} %get-tuple-element.117, bf16[2048,2048]{1,0:T(8,128)(2,1)} %bitcast.309), kind=kOutput, calls=%fused_computation.20 | convolution fusion | flops 5905580032 | bytes 17039360 | tf_op jit(solution)/shard_map/dot_general | solution.py:1048
  401.0 9.2 convolution_convert_fusion
  410.2 8.4 convolution_bitcast_fusion.2
  418.6 10.4 %fusion.10 = f32[2048,2048]{1,0:T(8,128)} fusion(bf16[2048,704]{0,1:T(8,128)(2,1)S(1)} %copy-done.22, bf16[1,2048,704]{1,2,0:T(8,128)(2,1)S(1)} %copy-done.60), kind=kOutput, calls=%fused_computation.27 | convolution fusion | flops 5905580032 | bytes 22544384 | tf_op jit(solution)/shard_map/dot_general | solution.py:1048
  428.9 10.2 %convolution_bitcast_fusion.1 = f32[1,2048,704]{1,2,0:T(8,128)} fusion(bf16[2048,704]{0,1:T(8,128)(2,1)S(1)} %copy-done.21, bf16[2048,2048]{1,0:T(8,128)(2,1)} %bitcast.307), kind=kOutput, calls=%fused_computation.18 | convolution fusion | flops 5905580032 | bytes 17039360 | tf_op jit(solution)/shard_map/dot_general | solution.py:1048
  439.2 10.4 %add_convert_fusion = bf16[2048,2048]{1,0:T(8,128)(2,1)S(1)} fusion(f32[2048,2048]{1,0:T(8,128)} %fusion.10, bf16[2048,704]{0,1:T(8,128)(2,1)S(1)} %copy-done.21, bf16[1,2048,704]{1,2,0:T(8,128)(2,1)S(1)} %copy-done.62), kind=kOutput, calls=%fused_computation.5 | convolution fusion | flops 5913968640 | bytes 30932992 | tf_op jit(solution)/shard_map/dot_general | solution.py:1048
  449.6 12.1 %fusion.20 = f32[16,256,2048]{2,1,0:T(8,128)} fusion(bf16[16,128,2048]{2,1,0:T(8,128)(2,1)S(1)} %bitcast.303, s32[16,256]{1,0:T(8,128)S(1)} %copy_bitcast_fusion.1, pred[16,256]{1,0:T(8,128)(4,1)S(1)} %broadcast_compare_fusion), kind=kOutput, calls=%fused_computation.53 | convolution fusion | flops 2148532224 | bytes 41963520 | tf_op jit(solution)/shard_map/sjt,sjd->std/dot_general | solution.py:1169
  462.5 21.4 %copy.149 = bf16[2048,4096]{1,0:T(8,128)(2,1)} copy(bf16[2048,4096]{0,1:T(8,128)(2,1)} %bitcast.289) | data formatting | bytes 33554432 | tf_op jit(solution)/shard_map/dot_general | solution.py:1048
  483.9 15.6 %fusion.23 = f32[16,256,2048]{2,1,0:T(8,128)} fusion(bf16[16,128,2048]{2,1,0:T(8,128)(2,1)} %bitcast.302, s32[16,256]{1,0:T(8,128)S(1)} %copy_bitcast_fusion.1, pred[16,256]{1,0:T(8,128)(4,1)S(1)} %broadcast_compare_fusion), kind=kOutput, calls=%fused_computation.54 | convolution fusion | flops 2148532224 | bytes 41963520 | tf_op jit(solution)/shard_map/sjt,sjd->std/dot_general | solution.py:1169
  501.3 12.3 %fusion.59 = f32[4096,96]{0,1:T(8,128)} fusion(bf16[4096,2048]{1,0:T(8,128)(2,1)} %bitcast.290, bf16[12,8,16,128]{3,2,1,0:T(8,128)(2,1)S(1)} %bitcast.317), kind=kOutput, calls=%fused_computation.124 | convolution fusion | flops 1610612736 | bytes 18743296 | tf_op jit(solution)/shard_map/dot_general | solution.py:1048
  513.6 12.2 %fusion.63 = f32[4096,96]{0,1:T(8,128)} fusion(bf16[4096,2048]{1,0:T(8,128)(2,1)} %bitcast.291, bf16[12,8,16,128]{3,2,1,0:T(8,128)(2,1)S(1)} %bitcast.319), kind=kOutput, calls=%fused_computation.128 | convolution fusion | flops 1610612736 | bytes 18743296 | tf_op jit(solution)/shard_map/dot_general | solution.py:1048
  525.8 12.1 %multiply_convert_fusion.4 = (bf16[4096,96]{0,1:T(8,128)(2,1)S(1)}, bf16[4096,96]{0,1:T(8,128)(2,1)S(1)}, bf16[4096,96]{0,1:T(8,128)(2,1)S(1)}) fusion(f32[4096,96]{0,1:T(8,128)} %fusion.63, f32[4096,96]{0,1:T(8,128)} %fusion.59, bf16[4096,2048]{1,0:T(8,128)(2,1)} %bitcast.287, bf16[12,8,16,128]{3,2,1,0:T(8,128)(2,1)S(1)} %bitcast.310), kind=kOutput, calls=%fused_computation.60 | convolution fusion | flops 1616510976 | bytes 22675456 | tf_op jit(solution)/shard_map/dot_general | solution.py:1048
  537.9 14.6 %fusion.61 = f32[4096,2048]{1,0:T(8,128)} fusion(bf16[4096,96]{0,1:T(8,128)(2,1)S(1)} %get-tuple-element.119, bf16[12,8,16,128]{3,2,1,0:T(8,128)(2,1)} %bitcast.320), kind=kOutput, calls=%fused_computation.126 | convolution fusion | flops 1610612736 | bytes 34734080 | tf_op jit(solution)/shard_map/dot_general | solution.py:1048
  552.6 9.6 %fusion.28 = bf16[1,96,16,128]{3,1,2,0:T(8,128)(2,1)} fusion(bf16[16,128,4096]{2,1,0:T(8,128)(2,1)} %bitcast.292, bf16[4096,96]{0,1:T(8,128)(2,1)S(1)} %get-tuple-element.119), kind=kOutput, calls=%fused_computation.71 | convolution fusion | flops 1610809344 | bytes 17956864 | tf_op jit(solution)/shard_map/dot_general | solution.py:1048
  562.2 9.6 %fusion.29 = bf16[1,96,16,128]{3,1,2,0:T(8,128)(2,1)} fusion(bf16[16,128,4096]{2,1,0:T(8,128)(2,1)} %bitcast.293, bf16[4096,96]{0,1:T(8,128)(2,1)S(1)} %get-tuple-element.118), kind=kOutput, calls=%fused_computation.72 | convolution fusion | flops 1610809344 | bytes 17956864 | tf_op jit(solution)/shard_map/dot_general | solution.py:1048
  571.7 18.9 %fusion.2 = bf16[4096,2048]{1,0:T(8,128)(2,1)} fusion(f32[16,256,2048]{2,1,0:T(8,128)} %fusion.23, bf16[4096,96]{0,1:T(8,128)(2,1)S(1)} %get-tuple-element.120, bf16[12,8,16,128]{3,2,1,0:T(8,128)(2,1)S(1)} %bitcast.311), kind=kOutput, calls=%fused_computation.4 | convolution fusion | flops 1627389952 | bytes 51511296 | tf_op jit(solution)/shard_map/dot_general | solution.py:1048
  590.6 76.9 %shard_map.282 = f32[128,2048]{1,0:T(8,128)} custom-call(bf16[32,128,2048]{2,1,0:T(8,128)(2,1)} %bitcast.295), custom_call_target="tpu_custom_call" | custom-call | tf_op jit(solution)/shard_map/pallas_call | solution.py:942
  667.6 28.3 %fusion.1 = bf16[4096,2048]{1,0:T(8,128)(2,1)} fusion(f32[16,256,2048]{2,1,0:T(8,128)} %fusion.20, f32[4096,2048]{1,0:T(8,128)} %fusion.61, bf16[4096,96]{0,1:T(8,128)(2,1)S(1)} %get-tuple-element.118, bf16[12,8,16,128]{3,2,1,0:T(8,128)(2,1)S(1)} %bitcast.318), kind=kOutput, calls=%fused_computation.2 | convolution fusion | flops 1635778560 | bytes 85065728 | tf_op jit(solution)/shard_map/dot_general | solution.py:1048
  695.9 78.0 %shard_map.284 = (f32[128,2048]{1,0:T(8,128)}, f32[16,128]{1,0:T(8,128)}) custom-call(bf16[32,128,2048]{2,1,0:T(8,128)(2,1)} %bitcast.294, f32[32,16,128]{2,1,0:T(8,128)} %broadcast_select_fusion.refs_1_), custom_call_target="tpu_custom_call" | custom-call | tf_op jit(solution)/shard_map/pallas_call | solution.py:942
  781.6 8.9 fusion.30
  830.4 82.0 %shard_map.285 = (f32[128,1024]{1,0:T(8,128)}, f32[128,256]{1,0:T(8,128)}, f32[128,256]{1,0:T(8,128)}, f32[1024,128]{1,0:T(8,128)}, f32[16,128]{1,0:T(8,128)}) custom-call(bf16[2048,1024]{1,0:T(8,128)(2,1)} %convolution_convert_fusion.4.refs_0_, bf16[2048,256]{1,0:T(8,128)(2,1)} %convolution_convert_fusion.6.refs_1_, ...), custom_call_target="tpu_custom_call" | custom-call | tf_op jit(solution)/shard_map/pallas_call | solution.py:990
  (255 shorter events, 129.4 us)
Async XLA Ops:
  0.6 366.1 %copy-start = (bf16[1,704,2048]{2,1,0:T(8,128)(2,1)S(1)}, bf16[1,704,2048]{2,1,0:T(8,128)(2,1)}, u32[]{:S(2)}) copy-start(bf16[1,704,2048]{2,1,0:T(8,128)(2,1)} %param.30) | copy-start | bytes 8650756
  6.3 96.1 %copy-start.30 = (f32[256,64]{0,1:T(8,128)}, f32[256,64]{0,1:T(8,128)S(1)}, u32[]{:S(2)}) copy-start(f32[256,64]{0,1:T(8,128)S(1)} %get-tuple-element.146) | copy-start | bytes 196612
  104.6 8.9 copy-start.27
  119.2 128.7 %collective-permute-start = (bf16[128,2048]{1,0:T(8,128)(2,1)}, bf16[128,2048]{1,0:T(8,128)(2,1)}, u32[]{:S(2)}, u32[]{:S(2)}) collective-permute-start(bf16[128,2048]{1,0:T(8,128)(2,1)} %dynamic-slice_convert_fusion.1), channel_id=1, source_target_pairs={{0,1},{1,0},{2,3},{3,2},{4,5},{5,4},{6,7},{7,6},{8,9},{9,8},{10,11... | collective-permute-start | bytes 1572872 | tf_op jit(solution)/shard_map/ppermute | solution.py:1009
  124.8 374.7 %all-to-all-start = ((bf16[16,3,96,128]{3,2,1,0:T(8,128)(2,1)}), bf16[16,3,96,128]{3,2,1,0:T(8,128)(2,1)}, u32[]{:S(2)}, u32[]{:S(2)}) async-start(bf16[16,3,96,128]{3,2,1,0:T(8,128)(2,1)} %copy.136), calls=%async_computation | async-start | bytes 2359296 | tf_op jit(solution)/shard_map/all_to_all | solution.py:1073
  130.3 119.8 %copy-start.43 = (f32[2048]{0:T(1024)}, f32[2048]{0:T(1024)S(1)}, u32[]{:S(2)}) copy-start(f32[2048]{0:T(1024)S(1)} %reshape.522) | copy-start | bytes 24580
  225.4 21.9 %copy-start.50 = (f32[2,128]{1,0:T(2,128)S(1)}, f32[2,128]{1,0:T(2,128)}, u32[]{:S(2)}) copy-start(f32[2,128]{1,0:T(2,128)} %copy-done.49) | copy-start | bytes 3076
  225.4 22.4 %copy-start.54 = (s32[256,6]{0,1:T(8,128)S(1)}, s32[256,6]{0,1:T(8,128)}, u32[]{:S(2)}) copy-start(s32[256,6]{0,1:T(8,128)} %param.32) | copy-start | bytes 18436
  225.4 22.4 %copy-start.10 = (bf16[128,2048]{1,0:T(8,128)(2,1)S(1)}, bf16[128,2048]{1,0:T(8,128)(2,1)}, u32[]{:S(2)}) copy-start(bf16[128,2048]{1,0:T(8,128)(2,1)} %refs_4_.1) | copy-start | bytes 1572868
  354.4 55.8 %copy-start.5 = (bf16[16,128,2048]{2,1,0:T(8,128)(2,1)}, bf16[16,128,2048]{2,1,0:T(8,128)(2,1)S(1)}, u32[]{:S(2)}) copy-start(bf16[16,128,2048]{2,1,0:T(8,128)(2,1)S(1)} %convolution_convert_fusion.2) | copy-start | bytes 25165828
  389.9 11.1 %copy-start.23 = (bf16[2048,704]{0,1:T(8,128)(2,1)S(1)}, bf16[2048,704]{0,1:T(8,128)(2,1)}, u32[]{:S(2)}) copy-start(bf16[2048,704]{0,1:T(8,128)(2,1)} %get-tuple-element.117) | copy-start | bytes 8650756
  401.0 9.2 copy-start.22
  418.6 10.4 %copy-start.21 = (bf16[2048,704]{0,1:T(8,128)(2,1)S(1)}, bf16[2048,704]{0,1:T(8,128)(2,1)}, u32[]{:S(2)}) copy-start(bf16[2048,704]{0,1:T(8,128)(2,1)} %get-tuple-element.115) | copy-start | bytes 8650756
  428.9 10.2 %copy-start.62 = (bf16[1,2048,704]{1,2,0:T(8,128)(2,1)S(1)}, bf16[1,2048,704]{1,2,0:T(8,128)(2,1)}, u32[]{:S(2)}) copy-start(bf16[1,2048,704]{1,2,0:T(8,128)(2,1)} %param.29) | copy-start | bytes 8650756
  449.6 12.1 %copy-start.57 = (pred[16]{0:T(512)(128)(4,1)S(1)}, pred[16]{0:T(512)(128)(4,1)}, u32[]{:S(2)}) copy-start(pred[16]{0:T(512)(128)(4,1)} %iota_compare_fusion.4) | copy-start | bytes 52
  501.1 12.5 %copy-start.18 = (bf16[1,96,16,128]{3,2,1,0:T(8,128)(2,1)}, bf16[1,96,16,128]{3,2,1,0:T(8,128)(2,1)S(1)}, u32[]{:S(2)}) copy-start(bf16[1,96,16,128]{3,2,1,0:T(8,128)(2,1)S(1)} %copy.138) | copy-start | bytes 1179652
  501.3 12.3 %copy-start.20 = (bf16[1,96,16,128]{3,2,1,0:T(8,128)(2,1)}, bf16[1,96,16,128]{3,2,1,0:T(8,128)(2,1)S(1)}, u32[]{:S(2)}) copy-start(bf16[1,96,16,128]{3,2,1,0:T(8,128)(2,1)S(1)} %copy.137) | copy-start | bytes 1179652
  590.6 76.9 %copy-start.19 = (bf16[1,96,16,128]{3,2,1,0:T(8,128)(2,1)S(1)}, bf16[1,96,16,128]{3,2,1,0:T(8,128)(2,1)}, u32[]{:S(2)}) copy-start(bf16[1,96,16,128]{3,2,1,0:T(8,128)(2,1)} %copy-done.18) | copy-start | bytes 1179652
  695.9 78.1 %copy-start.45 = (f32[128,16]{0,1:T(8,128)S(1)}, f32[128,16]{0,1:T(8,128)}, u32[]{:S(2)}) copy-start(f32[128,16]{0,1:T(8,128)} %select_reduce_fusion.2) | copy-start | bytes 24580
  695.9 79.7 %copy-start.4 = (f32[128,2048]{1,0:T(8,128)S(1)}, f32[128,2048]{1,0:T(8,128)}, u32[]{:S(2)}) copy-start(f32[128,2048]{1,0:T(8,128)} %copy-done.3) | copy-start | bytes 3145732
  695.9 79.7 %copy-start.13 = (bf16[2048,16]{1,0:T(8,128)(2,1)S(1)}, bf16[2048,16]{1,0:T(8,128)(2,1)}, u32[]{:S(2)}) copy-start(bf16[2048,16]{1,0:T(8,128)(2,1)} %reshape.493) | copy-start | bytes 196612
  695.9 79.7 %copy-start.44 = (f32[2048]{0:T(1024)S(1)}, f32[2048]{0:T(1024)}, u32[]{:S(2)}) copy-start(f32[2048]{0:T(1024)} %copy-done.43) | copy-start | bytes 24580
  695.9 79.7 %copy-start.52 = (f32[128]{0:T(128)S(1)}, f32[128]{0:T(128)}, u32[]{:S(2)}) copy-start(f32[128]{0:T(128)} %copy-done.51) | copy-start | bytes 1540
  779.0 19.5 %copy-start.36 = (bf16[128,2048]{1,0:T(8,128)(2,1)}, bf16[128,2048]{1,0:T(8,128)(2,1)S(1)}, u32[]{:S(2)}) copy-start(bf16[128,2048]{1,0:T(8,128)(2,1)S(1)} %get-tuple-element.111) | copy-start | bytes 1572868
  779.0 19.5 %collective-permute-start.1 = (bf16[128,2048]{1,0:T(8,128)(2,1)S(1)}, bf16[128,2048]{1,0:T(8,128)(2,1)}, u32[]{:S(2)}, u32[]{:S(2)}) collective-permute-start(bf16[128,2048]{1,0:T(8,128)(2,1)S(1)} %get-tuple-element.111), channel_id=1, source_target_pairs={{0,1},{1,0},{2,3},{3,2},{4,5},{5,4},{6,7},{7,6},{8,9},{9,8},{10,11... | collective-permute-start | bytes 1572872 | tf_op jit(solution)/shard_map/ppermute | solution.py:1009
  781.6 8.9 copy-start.33
  791.8 126.1 %all-to-all-start.1 = ((bf16[16,3,96,128]{3,2,1,0:T(8,128)(2,1)}), bf16[16,3,96,128]{3,2,1,0:T(8,128)(2,1)}, u32[]{:S(2)}, u32[]{:S(2)}) async-start(bf16[16,3,96,128]{3,2,1,0:T(8,128)(2,1)} %copy.151), calls=%async_computation.1 | async-start | bytes 2359296 | tf_op jit(solution)/shard_map/all_to_all | solution.py:1240
  814.9 14.1 %copy-start.6 = (f32[256,2048]{1,0:T(8,128)}, f32[256,2048]{1,0:T(8,128)S(1)}, u32[]{:S(2)}) copy-start(f32[256,2048]{1,0:T(8,128)S(1)} %convolution_add_fusion) | copy-start | bytes 6291460
  815.0 14.0 %collective-permute-start.2 = (bf16[128,2048]{1,0:T(8,128)(2,1)S(1)}, bf16[128,2048]{1,0:T(8,128)(2,1)S(1)}, u32[]{:S(2)}, u32[]{:S(2)}) collective-permute-start(bf16[128,2048]{1,0:T(8,128)(2,1)S(1)} %dynamic-slice_convert_fusion), channel_id=1, source_target_pairs={{0,1},{1,0},{2,3},{3,2},{4,5},{5,4},{6,7},{7,6},{8,9},{9,8},{10,11... | collective-permute-start | bytes 1572872 | tf_op jit(solution)/shard_map/ppermute | solution.py:1009
  830.4 84.8 %copy-start.7 = (f32[256,2048]{1,0:T(8,128)S(1)}, f32[256,2048]{1,0:T(8,128)}, u32[]{:S(2)}) copy-start(f32[256,2048]{1,0:T(8,128)} %copy-done.6) | copy-start | bytes 6291460
  830.4 84.8 %copy-start.55 = (f32[128]{0:T(128)S(1)}, f32[128]{0:T(128)}, u32[]{:S(2)}) copy-start(f32[128]{0:T(128)} %get-tuple-element.140) | copy-start | bytes 1540
  919.3 11.0 %copy-start.1 = (bf16[1,704,2048]{2,1,0:T(8,128)(2,1)S(1)}, bf16[1,704,2048]{2,1,0:T(8,128)(2,1)}, u32[]{:S(2)}) copy-start(bf16[1,704,2048]{2,1,0:T(8,128)(2,1)} %param.30) | copy-start | bytes 8650756
  (38 other events, 145.4 us)

commit v2 on v1

--- a/solution.py
+++ b/solution.py
@@ -501,18 +501,17 @@
 
 
 class Copies:
-    def __init__(self, groups, n_planes, n_pieces, send, recv):
-        self.base = {name: i * n_planes for i, name in enumerate(groups)}
-        self.n_pieces = n_pieces
-        self.send, self.recv = send, recv
+    def __init__(self, n_planes, send, recv):
+        self.n_planes, self.send, self.recv = n_planes, send, recv
         self.open = []
 
     def copy(self, group, s, piece, src, dst, device, arrival=None):
+        arrival = group if arrival is None else arrival
         return pltpu.make_async_remote_copy(
             src_ref=src,
             dst_ref=dst,
-            send_sem=self.send.at[self.base[group] + s, piece],
-            recv_sem=self.recv.at[self.base[arrival or group] + s, piece],
+            send_sem=self.send.at[group * self.n_planes + s, piece],
+            recv_sem=self.recv.at[arrival * self.n_planes + s, piece],
             device_id=device,
             device_id_type=MESH,
         )
@@ -539,133 +538,125 @@
             when(condition, body)
 
 
-SPREAD_GROUPS = (
-    "z", "z_down", "y_all", "y_half", "x_all", "x_half", "c_own", "c_y", "c_x", "c_xh", "c_yh",
-)
-
-
-def spread(spot, copies, own, views, use_x):
-    order = spot.far_first()[::-1]
-    y, x, core = spot.y, spot.x, spot.core
-
-    def at(s, yy, xx, part="all", cc=None):
-        return views(s, yy, core if cc is None else cc, xx, part)
-
-    def onward(s, sources):
-        copies.start(None, "y_all", s, sources, at(s, y, x), spot.side)
-        if use_x:
-            copies.start(None, "x_all", s, sources, at(s, y, x), spot.across)
-        copies.start(None, "c_own", s, sources, at(s, y, x), spot.twin)
-
-    def column(j):
-        s = order[j]
-        here = at(s, y, x)
-        copies.arrive("z", s, here, spot.up)
-        copies.start((s > spot.z) & spot.has_down, "z_down", s, here, here, spot.down, "z")
-        copies.start((s < spot.z) & spot.has_up, "z", s, here, here, spot.up)
-        onward(s, here)
-
-    def sides(j):
-        s = order[j]
-        there = at(s, 1 - y, x)
-        copies.arrive("y_all", s, there, spot.side)
-        if use_x:
-            part = at(s, 1 - y, x, "first")
-            copies.start(None, "x_half", s, part, part, spot.across)
-        copies.start(None, "c_y", s, there, there, spot.twin)
-        if use_x:
-            there = at(s, y, 1 - x)
-            copies.arrive("x_all", s, there, spot.across)
-            part = at(s, y, 1 - x, "second")
-            copies.start(None, "y_half", s, part, part, spot.side)
-            copies.start(None, "c_x", s, there, there, spot.twin)
-
-    def corner(j):
-        if not use_x:
+(Z_UP, Z_DOWN, Y_ALL, Y_HALF, X_ALL, X_HALF, C_OWN, C_Y, C_X, C_XH, C_YH) = range(11)
+(ALL, FIRST, SECOND) = range(3)
+
+
+class Spread:
+    def __init__(self, spot, copies, own, views, use_x):
+        self.spot, self.copies, self.own, self.use_x = spot, copies, own, use_x
+        self.order = spot.far_first()[::-1]
+        y, x, core = spot.y, spot.x, spot.core
+
+        def places(s, cc):
+            return (
+                views(s, y, cc, x, ALL),
+                views(s, 1 - y, cc, x, ALL),
+                views(s, 1 - y, cc, x, FIRST),
+                views(s, y, cc, 1 - x, ALL),
+                views(s, y, cc, 1 - x, SECOND),
+                views(s, 1 - y, cc, 1 - x, FIRST),
+                views(s, 1 - y, cc, 1 - x, SECOND),
+            )
+
+        self.mine = [places(s, core) for s in self.order]
+        self.twins = [places(s, 1 - core) for s in self.order]
+        self.goes_down = [(s > spot.z) & spot.has_down for s in self.order]
+        self.goes_up = [(s < spot.z) & spot.has_up for s in self.order]
+
+    def onward(self, j, sources):
+        s, here, spot, start = self.order[j], self.mine[j][0], self.spot, self.copies.start
+        start(None, Y_ALL, s, sources, here, spot.side)
+        if self.use_x:
+            start(None, X_ALL, s, sources, here, spot.across)
+        start(None, C_OWN, s, sources, here, spot.twin)
+
+    def begin(self):
+        spot, here = self.spot, self.mine[0][0]
+        self.copies.start(spot.has_up, Z_UP, spot.z, self.own, here, spot.up)
+        self.copies.start(spot.has_down, Z_DOWN, spot.z, self.own, here, spot.down, Z_UP)
+        self.onward(0, self.own)
+
+    def relay(self, j, goes=None):
+        s, here, spot = self.order[j], self.mine[j][0], self.spot
+        goes_down, goes_up = goes or (self.goes_down[j], self.goes_up[j])
+        self.copies.arrive(Z_UP, s, here, spot.up)
+        self.copies.start(goes_down, Z_DOWN, s, here, here, spot.down, Z_UP)
+        self.copies.start(goes_up, Z_UP, s, here, here, spot.up)
+
+    def column(self, j):
+        if j < len(self.order):
+            self.relay(j)
+            self.onward(j, self.mine[j][0])
+
+    def side(self, j):
+        s, (_, there, part, *_), spot = self.order[j], self.mine[j], self.spot
+        self.copies.arrive(Y_ALL, s, there, spot.side)
+        if self.use_x:
+            self.copies.start(None, X_HALF, s, part, part, spot.across)
+        self.copies.start(None, C_Y, s, there, there, spot.twin)
+
+    def across(self, j):
+        s, (_, _, _, there, part, *_), spot = self.order[j], self.mine[j], self.spot
+        self.copies.arrive(X_ALL, s, there, spot.across)
+        self.copies.start(None, Y_HALF, s, part, part, spot.side)
+        self.copies.start(None, C_X, s, there, there, spot.twin)
+
+    def sides(self, j):
+        if 0 <= j < len(self.order):
+            self.side(j)
+            if self.use_x:
+                self.across(j)
+
+    def corner(self, j):
+        if not self.use_x or not 0 <= j < len(self.order):
             return
-        s = order[j]
-        part = at(s, 1 - y, 1 - x, "first")
-        copies.arrive("x_half", s, part, spot.across)
-        copies.start(None, "c_xh", s, part, part, spot.twin)
-        part = at(s, 1 - y, 1 - x, "second")
-        copies.arrive("y_half", s, part, spot.side)
-        copies.start(None, "c_yh", s, part, part, spot.twin)
-
-    here = at(spot.z, y, x)
-    copies.start(spot.has_up, "z", spot.z, own, here, spot.up)
-    copies.start(spot.has_down, "z_down", spot.z, own, here, spot.down, "z")
-    onward(spot.z, own)
-    n = spot.n_planes
-    for step in range(1, n + 2):
-        if step < n:
-            column(step)
-        if 0 <= step - 1 < n:
-            sides(step - 1)
-        if 0 <= step - 2 < n:
-            corner(step - 2)
-    other = 1 - core
-    for s in range(n):
-        copies.arrive("c_own", s, at(s, y, x, cc=other), spot.twin)
-        copies.arrive("c_y", s, at(s, 1 - y, x, cc=other), spot.twin)
-        if use_x:
-            copies.arrive("c_x", s, at(s, y, 1 - x, cc=other), spot.twin)
-            copies.arrive("c_xh", s, at(s, 1 - y, 1 - x, "first", cc=other), spot.twin)
-            copies.arrive("c_yh", s, at(s, 1 - y, 1 - x, "second", cc=other), spot.twin)
-    copies.close()
+        s, (_, _, _, _, _, first, second), spot = self.order[j], self.mine[j], self.spot
+        self.copies.arrive(X_HALF, s, first, spot.across)
+        self.copies.start(None, C_XH, s, first, first, spot.twin)
+        self.copies.arrive(Y_HALF, s, second, spot.side)
+        self.copies.start(None, C_YH, s, second, second, spot.twin)
+
+    def twin_near(self, j):
+        s, there, spot = self.order[j], self.twins[j], self.spot
+        self.copies.arrive(C_OWN, s, there[0], spot.twin)
+        if self.use_x:
+            self.copies.arrive(C_X, s, there[3], spot.twin)
+
+    def twin_far(self, j):
+        s, there, spot = self.order[j], self.twins[j], self.spot
+        self.copies.arrive(C_Y, s, there[1], spot.twin)
+        if self.use_x:
+            self.copies.arrive(C_XH, s, there[5], spot.twin)
+            self.copies.arrive(C_YH, s, there[6], spot.twin)
+
+    def twin_all(self):
+        for j in range(len(self.order)):
+            self.twin_near(j)
+            self.twin_far(j)
+
+    def stage(self, step):
+        self.column(step)
+        self.sides(step - 1)
+        self.corner(step - 2)
+
+    def run(self):
+        self.begin()
+        for step in range(1, len(self.order) + 2):
+            self.stage(step)
+        self.twin_all()
+        self.copies.close()
 
 
 def dp_of(s, yy, cc):
     return (s * 2 + yy) * 2 + cc
 
 
-def gather_kernel(n_planes, n, *refs):
-    ins, outs, (send, recv, local) = refs[:n], refs[n : 2 * n], refs[2 * n :]
-    spot = Spot(n_planes)
-    half = ins[0].shape[0] // 2
-
-    def views(s, yy, cc, xx, part):
-        b = dp_of(s, yy, cc) * 2 + xx
-        if part == "all":
-            return [o.at[b] for o in outs]
-        if part == "first":
-            return [outs[0].at[b, pl.ds(0, half)]] + [o.at[b] for o in outs[1:]]
-        return [outs[0].at[b, pl.ds(half, half)]]
-
-    own = [
-        pltpu.make_async_copy(ins[i], outs[i].at[spot.dp * 2 + spot.x], local.at[i])
-        for i in range(n)
-    ]
-    for c in own:
-        c.start()
-    spot.greet()
-    copies = Copies(SPREAD_GROUPS, n_planes, n, send, recv)
-    spread(spot, copies, list(ins), views, True)
-    for c in own:
-        c.wait()
-
-
-def gather_everywhere(arrays, n_dp, collective_id):
-    n, n_planes = len(arrays), n_dp // 4
-    sems = (len(SPREAD_GROUPS) * n_planes, n)
-    return pl.pallas_call(
-        functools.partial(gather_kernel, n_planes, n),
-        out_shape=[jax.ShapeDtypeStruct((2 * n_dp,) + a.shape, a.dtype) for a in arrays],
-        in_specs=[ANY] * n,
-        out_specs=[ANY] * n,
-        scratch_shapes=[
-            pltpu.SemaphoreType.DMA(sems),
-            pltpu.SemaphoreType.DMA(sems),
-            pltpu.SemaphoreType.DMA((n,)),
-        ],
-        compiler_params=pltpu.CompilerParams(collective_id=collective_id, has_side_effects=True),
-    )(*arrays)
-
-
 def fetch_kernel(n_planes, axes, *refs):
     n = len(axes)
-    ins, (tokens, small), outs = refs[:n], refs[n : n + 2], refs[n + 2 : 2 * n + 2]
-    sequence, smalls = refs[2 * n + 2 : 2 * n + 4]
-    send, recv, local, x_send, x_recv = refs[2 * n + 4 :]
+    ins, (tokens, small, grads), outs = refs[:n], refs[n : n + 3], refs[n + 3 : 2 * n + 3]
+    sequence, smalls, all_grads = refs[2 * n + 3 : 2 * n + 6]
+    send, recv, local, x_send, x_recv, g_send, g_recv = refs[2 * n + 6 :]
     spot = Spot(n_planes)
 
     def views(s, yy, cc, xx, part):
@@ -678,9 +669,18 @@
         return places + [smalls.at[xx, i]]
 
     sources = list(ins) + [small]
-    mine = views(spot.z, spot.y, spot.core, spot.x, "all")
+    mine = views(spot.z, spot.y, spot.core, spot.x, ALL)
     own = [pltpu.make_async_copy(a, v, local.at[i]) for i, (a, v) in enumerate(zip(sources, mine))]
     own.append(pltpu.make_async_copy(tokens, sequence.at[spot.x], local.at[n + 1]))
+    own.append(pltpu.make_async_copy(grads, all_grads.at[spot.dp * 2 + spot.x], local.at[n + 2]))
+    half = grads.shape[0] // 2
+
+    def grad_views(s, yy, cc, xx, part):
+        b = dp_of(s, yy, cc) * 2 + xx
+        if part == ALL:
+            return [all_grads.at[b]]
+        return [all_grads.at[b, pl.ds(0 if part == FIRST else half, half)]]
+
     for c in own:
         c.start()
     spot.greet()
@@ -692,8 +692,18 @@
         )
 
     across(0, tokens, sequence.at[spot.x]).start()
-    copies = Copies(SPREAD_GROUPS, n_planes, n + 1, send, recv)
-    spread(spot, copies, sources, views, False)
+    copies = Copies(n_planes, send, recv)
+    weights = Spread(spot, copies, sources, views, False)
+    gradients = Spread(spot, Copies(n_planes, g_send, g_recv), [grads], grad_views, True)
+    weights.begin()
+    gradients.begin()
+    for step in range(1, n_planes + 2):
+        weights.stage(step)
+        gradients.stage(step)
+    weights.twin_all()
+    gradients.twin_all()
+    weights.copies.close()
+    gradients.copies.close()
     for c in own:
         c.wait()
     across(1, smalls.at[spot.x], smalls.at[spot.x]).start()
@@ -703,9 +713,9 @@
     across(1, smalls.at[1 - spot.x], smalls.at[1 - spot.x]).wait_recv()
 
 
-def fetch(arrays, axes, tokens, small, n_dp, collective_id):
+def fetch(arrays, axes, tokens, small, grads, n_dp, collective_id):
     n, n_planes = len(arrays), n_dp // 4
-    sems = (len(SPREAD_GROUPS) * n_planes, n + 1)
+    sems = (11 * n_planes, n + 1)
 
     def whole(a, axis):
         shape = list(a.shape)
@@ -718,21 +728,24 @@
         + [
             jax.ShapeDtypeStruct((2,) + tokens.shape, tokens.dtype),
             jax.ShapeDtypeStruct((2, n_dp) + small.shape, small.dtype),
+            jax.ShapeDtypeStruct((2 * n_dp,) + grads.shape, grads.dtype),
         ],
-        in_specs=[ANY] * (n + 2),
-        out_specs=[ANY] * (n + 2),
+        in_specs=[ANY] * (n + 3),
+        out_specs=[ANY] * (n + 3),
         scratch_shapes=[
             pltpu.SemaphoreType.DMA(sems),
             pltpu.SemaphoreType.DMA(sems),
-            pltpu.SemaphoreType.DMA((n + 2,)),
+            pltpu.SemaphoreType.DMA((n + 3,)),
             pltpu.SemaphoreType.DMA((2,)),
             pltpu.SemaphoreType.DMA((2,)),
+            pltpu.SemaphoreType.DMA((11 * n_planes, 1)),
+            pltpu.SemaphoreType.DMA((11 * n_planes, 1)),
         ],
         compiler_params=pltpu.CompilerParams(collective_id=collective_id, has_side_effects=True),
-    )(*arrays, tokens, small)
-
-
-REDUCE_GROUPS = ("c_yx", "c_y", "c_x", "c_own", "x_half", "y_half", "y_all", "x_all", "z_up", "z_down")
+    )(*arrays, tokens, small, grads)
+
+
+(T_YX, T_Y, T_X, T_OWN, R_XHALF, R_YHALF, R_YALL, R_XALL, R_UP, R_DOWN) = range(10)
 
 
 def add_up(target, sources):
@@ -750,7 +763,7 @@
     lax.fori_loop(0, rows // step, body, 0)
 
 
-class Sums:
+class Reduce:
     @staticmethod
     def scratch(shapes, dtypes, n_planes, use_x):
         n = len(shapes)
@@ -767,163 +780,161 @@
                 out.append(pltpu.VMEM((n_planes,) + shape, dtype))
                 out.append(pltpu.VMEM((n_planes,) + half, dtype))
                 out.append(pltpu.VMEM((n_planes,) + (half if i == 0 else (8, 128)), dtype))
-        sems = (len(REDUCE_GROUPS) * n_planes, n)
+        sems = (10 * n_planes, n)
         out.append(pltpu.SemaphoreType.DMA(sems))
         out.append(pltpu.SemaphoreType.DMA(sems))
         out.append(pltpu.SemaphoreType.DMA((kinds * n_planes, n)))
         return out
 
-
-def reduce_scatter(spot, ins, outs, scratch, use_x):
-    n, n_planes = len(outs), spot.n_planes
-    per = 8 if use_x else 5
-    send, recv, local = scratch[n * per :]
-    sets = [scratch[i * per : (i + 1) * per] for i in range(n)]
-    mine = [s[0] for s in sets]
-    twin = [s[1] for s in sets]
-    above = [s[2] for s in sets]
-    below = [s[3] for s in sets]
-    side = [s[4] for s in sets]
-    across = [s[5] for s in sets] if use_x else None
-    first = [s[6] for s in sets] if use_x else None
-    second = [sets[0][7]] if use_x else None
-    copies = Copies(REDUCE_GROUPS, n_planes, n, send, recv)
-    y, x, core = spot.y, spot.x, spot.core
-    order = spot.far_first()
-    kinds = (["c_yx", "c_y", "c_x", "c_own"] if use_x else ["c_y", "c_own"])
-    places = {"c_yx": (1 - y, 1 - x), "c_y": (1 - y, x), "c_x": (y, 1 - x), "c_own": (y, x)}
-
-    def load(k, j):
-        s = order[j]
-        yy, xx = places[kinds[k]]
-        for i, ref in enumerate(ins(s, yy, core, xx)):
-            yield pltpu.make_async_copy(ref, mine[i].at[k, s], local.at[k * n_planes + s, i])
-
-    for j in range(n_planes):
-        for k in range(len(kinds)):
-            for c in load(k, j):
-                c.start()
-    spot.greet()
-    for j in range(n_planes):
-        s = order[j]
-        for k, name in enumerate(kinds):
-            yy, xx = places[name]
-            copies.start(None, name, s, ins(s, yy, 1 - core, xx), [t.at[k, s] for t in twin], spot.twin)
-
-    def ready(k, j):
-        s = order[j]
-        for c in load(k, j):
+    @staticmethod
+    def n_scratch(n, use_x):
+        return n * (8 if use_x else 5) + 3
+
+    def __init__(self, spot, blocks, outs, scratch, use_x):
+        self.spot, self.outs, self.use_x = spot, outs, use_x
+        self.n, self.n_planes = len(outs), spot.n_planes
+        per = 8 if use_x else 5
+        send, recv, self.local = scratch[self.n * per :]
+        sets = [scratch[i * per : (i + 1) * per] for i in range(self.n)]
+        self.mine = [s[0] for s in sets]
+        self.twin = [s[1] for s in sets]
+        self.above = [s[2] for s in sets]
+        self.below = [s[3] for s in sets]
+        self.near = [s[4] for s in sets]
+        self.across = [s[5] for s in sets] if use_x else None
+        self.first = [s[6] for s in sets] if use_x else None
+        self.second = sets[0][7] if use_x else None
+        self.half = sets[0][0].shape[2] // 2
+        self.copies = Copies(self.n_planes, send, recv)
+        y, x, core = spot.y, spot.x, spot.core
+        self.order = spot.far_first()
+        places = {T_YX: (1 - y, 1 - x), T_Y: (1 - y, x), T_X: (y, 1 - x), T_OWN: (y, x)}
+        self.kinds = [T_YX, T_Y, T_X, T_OWN] if use_x else [T_Y, T_OWN]
+        self.terms = {(k, j): blocks(s, places[k][0], core, places[k][1]) for k in self.kinds for j, s in enumerate(self.order)}
+        self.others = {(k, j): blocks(s, places[k][0], 1 - core, places[k][1]) for k in self.kinds for j, s in enumerate(self.order)}
+
+    def load(self, kind, j):
+        k = self.kinds.index(kind)
+        s = self.order[j]
+        return [
+            pltpu.make_async_copy(ref, self.mine[i].at[k, s], self.local.at[k * self.n_planes + s, i])
+            for i, ref in enumerate(self.terms[kind, j])
+        ]
+
+    def start_loads(self):
+        for j in range(self.n_planes):
+            for kind in self.kinds:
+                for c in self.load(kind, j):
+                    c.start()
+
+    def start_twins(self):
+        for j in range(self.n_planes):
+            s = self.order[j]
+            for k, kind in enumerate(self.kinds):
+                self.copies.start(None, kind, s, self.others[kind, j], [t.at[k, s] for t in self.twin], self.spot.twin)
+
+    def ready(self, kind, j):
+        k, s = self.kinds.index(kind), self.order[j]
+        for c in self.load(kind, j):
             c.wait()
-        copies.arrive(kinds[k], s, [t.at[k, s] for t in twin], spot.twin)
-
-    half = sets[0][0].shape[2] // 2
-
-    def corner(j):
-        s = order[j]
-        ready(0, j)
-        for i in range(n):
-            add_up(mine[i].at[0, s], [mine[i].at[0, s], twin[i].at[0, s]])
-        head = [mine[0].at[0, s, pl.ds(0, half)]] + [m.at[0, s] for m in mine[1:]]
-        copies.start(None, "x_half", s, head, [f.at[s] for f in first], spot.across)
-        copies.start(None, "y_half", s, [mine[0].at[0, s, pl.ds(half, half)]], [second[0].at[s]], spot.side)
-
-    def sides(j):
-        s = order[j]
-        k = kinds.index("c_y")
-        ready(k, j)
-        if use_x:
-            copies.arrive("x_half", s, [f.at[s] for f in first], spot.across)
-            for i in range(n):
-                if i == 0:
-                    a, b = pl.ds(0, half), pl.ds(half, half)
-                    add_up(mine[0].at[k, s, a], [mine[0].at[k, s, a], twin[0].at[k, s, a], first[0].at[s]])
-                    add_up(mine[0].at[k, s, b], [mine[0].at[k, s, b], twin[0].at[k, s, b]])
-                else:
-                    add_up(mine[i].at[k, s], [mine[i].at[k, s], twin[i].at[k, s], first[i].at[s]])
-        else:
-            for i in range(n):
-                add_up(mine[i].at[k, s], [mine[i].at[k, s], twin[i].at[k, s]])
-        copies.start(None, "y_all", s, [m.at[k, s] for m in mine], [t.at[s] for t in side], spot.side)
-        if not use_x:
+        self.copies.arrive(kind, s, [t.at[k, s] for t in self.twin], self.spot.twin)
+        return [m.at[k, s] for m in self.mine], [t.at[k, s] for t in self.twin]
+
+    def corner(self, j):
+        if not self.use_x or not 0 <= j < self.n_planes:
             return
-        k = kinds.index("c_x")
-        ready(k, j)
-        copies.arrive("y_half", s, [second[0].at[s]], spot.side)
-        for i in range(n):
+        s, half = self.order[j], self.half
+        mine, twin = self.ready(T_YX, j)
+        for m, t in zip(mine, twin):
+            add_up(m, [m, t])
+        head = [mine[0].at[pl.ds(0, half)]] + mine[1:]
+        self.copies.start(None, R_XHALF, s, head, [f.at[s] for f in self.first], self.spot.across)
+        tail = [mine[0].at[pl.ds(half, half)]]
+        self.copies.start(None, R_YHALF, s, tail, [self.second.at[s]], self.spot.side)
+
+    def side(self, j):
+        s, half = self.order[j], self.half
+        mine, twin = self.ready(T_Y, j)
+        if self.use_x:
+            first = [f.at[s] for f in self.first]
+            self.copies.arrive(R_XHALF, s, first, self.spot.across)
+        for i, (m, t) in enumerate(zip(mine, twin)):
+            if not self.use_x:
+                add_up(m, [m, t])
+            elif i == 0:
+                a, b = pl.ds(0, half), pl.ds(half, half)
+                add_up(m.at[a], [m.at[a], t.at[a], first[0]])
+                add_up(m.at[b], [m.at[b], t.at[b]])
+            else:
+                add_up(m, [m, t, first[i]])
+        self.copies.start(None, R_YALL, s, mine, [t.at[s] for t in self.near], self.spot.side)
+
+    def over(self, j):
+        s, half = self.order[j], self.half
+        mine, twin = self.ready(T_X, j)
+        second = self.second.at[s]
+        self.copies.arrive(R_YHALF, s, [second], self.spot.side)
+        for i, (m, t) in enumerate(zip(mine, twin)):
             if i == 0:
                 a, b = pl.ds(0, half), pl.ds(half, half)
-                add_up(mine[0].at[k, s, a], [mine[0].at[k, s, a], twin[0].at[k, s, a]])
-                add_up(mine[0].at[k, s, b], [mine[0].at[k, s, b], twin[0].at[k, s, b], second[0].at[s]])
+                add_up(m.at[a], [m.at[a], t.at[a]])
+                add_up(m.at[b], [m.at[b], t.at[b], second])
             else:
-                add_up(mine[i].at[k, s], [mine[i].at[k, s], twin[i].at[k, s]])
-        copies.start(None, "x_all", s, [m.at[k, s] for m in mine], [t.at[s] for t in across], spot.across)
-
-    def column(j):
-        s = order[j]
-        k = kinds.index("c_own")
-        ready(k, j)
-        copies.arrive("y_all", s, [t.at[s] for t in side], spot.side)
-        if use_x:
-            copies.arrive("x_all", s, [t.at[s] for t in across], spot.across)
-        here = [[mine[i].at[k, s], twin[i].at[k, s], side[i].at[s]] + ([across[i].at[s]] if use_x else []) for i in range(n)]
-        if j == n_planes - 1:
-            from_above = [t.at[s] for t in above]
-            from_below = [t.at[s] for t in below]
-
-            def wait_above():
-                copies.arrive("z_down", s, from_above, spot.up)
-
-            def wait_below():
-                copies.arrive("z_up", s, from_below, spot.down)
-
-            when(spot.has_up, wait_above)
-            when(spot.has_down, wait_below)
-
-            def both():
-                for i in range(n):
-                    add_up(outs[i], here[i] + [from_above[i], from_below[i]])
-
-            def one_above():
-                for i in range(n):
-                    add_up(outs[i], here[i] + [from_above[i]])
-
-            def one_below():
-                for i in range(n):
-                    add_up(outs[i], here[i] + [from_below[i]])
-
-            when(spot.has_up & spot.has_down, both)
-            when(spot.has_up & (spot.z == 0), one_above)
-            when(spot.has_down & (spot.z == n_planes - 1), one_below)
+                add_up(m, [m, t])
+        self.copies.start(None, R_XALL, s, mine, [t.at[s] for t in self.across], self.spot.across)
+
+    def sides(self, j):
+        if 0 <= j < self.n_planes:
+            self.side(j)
+            if self.use_x:
+                self.over(j)
+
+    def column(self, j):
+        if not 0 <= j < self.n_planes:
             return
-        goes_down = s < spot.z
-        goes_up = s > spot.z
+        s, spot, copies, n = self.order[j], self.spot, self.copies, self.n
+        mine, twin = self.ready(T_OWN, j)
+        near = [t.at[s] for t in self.near]
+        copies.arrive(R_YALL, s, near, spot.side)
+        here = [[m, t, a] for m, t, a in zip(mine, twin, near)]
+        if self.use_x:
+            across = [t.at[s] for t in self.across]
+            copies.arrive(R_XALL, s, across, spot.across)
+            here = [h + [a] for h, a in zip(here, across)]
+        above = [t.at[s] for t in self.above]
+        below = [t.at[s] for t in self.below]
+
+        def add_all(targets, *more):
+            for i in range(n):
+                add_up(targets[i], here[i] + [m[i] for m in more])
+
+        if j == self.n_planes - 1:
+            when(spot.has_up, lambda: copies.arrive(R_DOWN, s, above, spot.up))
+            when(spot.has_down, lambda: copies.arrive(R_UP, s, below, spot.down))
+            when(spot.has_up & spot.has_down, lambda: add_all(self.outs, above, below))
+            when(spot.z == 0, lambda: add_all(self.outs, above))
+            when(spot.z == self.n_planes - 1, lambda: add_all(self.outs, below))
+            return
         for goes, more, group, buffers, device, source in (
-            (goes_down, spot.has_up, "z_down", above, spot.down, spot.up),
-            (goes_up, spot.has_down, "z_up", below, spot.up, spot.down),
+            (s < spot.z, spot.has_up, R_DOWN, above, spot.down, spot.up),
+            (s > spot.z, spot.has_down, R_UP, below, spot.up, spot.down),
         ):
-            arrived = [t.at[s] for t in buffers]
 
             def partial():
-                copies.arrive(group, s, arrived, source)
-                for i in range(n):
-                    add_up(mine[i].at[k, s], here[i] + [arrived[i]])
-
-            def alone():
-                for i in range(n):
-                    add_up(mine[i].at[k, s], here[i])
+                copies.arrive(group, s, buffers, source)
+                add_all(mine, buffers)
 
             when(goes & more, partial)
-            when(goes & jnp.logical_not(more), alone)
-            copies.start(goes, group, s, [m.at[k, s] for m in mine], [t.at[s] for t in buffers], device)
-
-    for step in range(n_planes + 2):
-        if use_x and step < n_planes:
-            corner(step)
-        if 0 <= step - 1 < n_planes:
-            sides(step - 1)
-        if 0 <= step - 2 < n_planes:
-            column(step - 2)
-    copies.close()
+            when(goes & jnp.logical_not(more), lambda: add_all(mine))
+            copies.start(goes, group, s, mine, buffers, device)
+
+    def stage(self, step):
+        self.corner(step)
+        self.sides(step - 1)
+        self.column(step - 2)
+
+    def close(self):
+        self.copies.close()
 
 
 def sum_kernel(n_planes, n, *refs):
@@ -933,7 +944,13 @@
     def blocks(s, yy, cc, xx):
         return [a.at[dp_of(s, yy, cc) * 2 + xx] for a in ins]
 
-    reduce_scatter(spot, blocks, outs, scratch, True)
+    net = Reduce(spot, blocks, outs, scratch, True)
+    net.start_loads()
+    spot.greet()
+    net.start_twins()
+    for step in range(n_planes + 2):
+        net.stage(step)
+    net.close()
 
 
 def sum_everywhere(arrays, out_dtypes, n_dp, collective_id):
@@ -944,7 +961,7 @@
         out_shape=[jax.ShapeDtypeStruct(s, t) for s, t in zip(shapes, out_dtypes)],
         in_specs=[ANY] * n,
         out_specs=[pl.BlockSpec(memory_space=pltpu.VMEM)] * n,
-        scratch_shapes=Sums.scratch(shapes, [a.dtype for a in arrays], n_planes, True),
+        scratch_shapes=Reduce.scratch(shapes, [a.dtype for a in arrays], n_planes, True),
         compiler_params=pltpu.CompilerParams(
             collective_id=collective_id, has_side_effects=True, vmem_limit_bytes=56 << 20
         ),
@@ -953,8 +970,8 @@
 
 def return_kernel(n_planes, axes, *refs):
     n = len(axes)
-    ins, outs = refs[:n], refs[n : 2 * n]
-    scratch, (tile_sum, tile_in, x_send, x_recv) = refs[2 * n : -4], refs[-4:]
+    ins, parts, outs, out_sum = refs[:n], refs[n], refs[n + 1 : 2 * n + 1], refs[2 * n + 1]
+    scratch, (tile_sum, tile_in, x_send, x_recv) = refs[2 * n + 2 : -4], refs[-4:]
     spot = Spot(n_planes)
 
     def blocks(s, yy, cc, xx):
@@ -966,7 +983,22 @@
             places.append(a.at[span] if axis == 0 else a.at[:, span])
         return places
 
-    reduce_scatter(spot, blocks, list(outs[:-1]) + [tile_sum], scratch, False)
+    cut = Reduce.n_scratch(n, False)
+    weights = Reduce(spot, blocks, list(outs[:-1]) + [tile_sum], scratch[:cut], False)
+    tokens = Reduce(
+        spot, lambda s, yy, cc, xx: [parts.at[dp_of(s, yy, cc) * 2 + xx]], [out_sum], scratch[cut:], True
+    )
+    weights.start_loads()
+    tokens.start_loads()
+    spot.greet()
+    weights.start_twins()
+    tokens.start_twins()
+    for step in range(n_planes + 2):
+        weights.sides(step)
+        tokens.corner(step)
+        tokens.sides(step - 1)
+        weights.column(step - 1)
+        tokens.column(step - 2)
     rows = tile_in.shape[0]
     swap = pltpu.make_async_remote_copy(
         src_ref=tile_sum.at[pl.ds(pl.multiple_of((1 - spot.x) * rows, rows), rows)], dst_ref=tile_in,
@@ -975,9 +1007,11 @@
     swap.start()
     swap.wait()
     outs[-1][...] = tile_sum[pl.ds(pl.multiple_of(spot.x * rows, rows), rows), :] + tile_in[...]
-
-
-def sum_back(arrays, axes, n_dp, collective_id):
+    weights.close()
+    tokens.close()
+
+
+def sum_back(arrays, axes, parts, n_dp, collective_id):
     n, n_planes = len(arrays), n_dp // 4
 
     def part(a, axis):
@@ -987,12 +1021,14 @@
 
     shapes = [part(a, axis) for a, axis in zip(arrays, axes)]
     tile = (shapes[-1][0] // 2, shapes[-1][1])
+    block = parts.shape[1:]
     return pl.pallas_call(
         functools.partial(return_kernel, n_planes, axes),
-        out_shape=[jax.ShapeDtypeStruct(s, jnp.float32) for s in shapes[:-1] + [tile]],
-        in_specs=[ANY] * n,
-        out_specs=[pl.BlockSpec(memory_space=pltpu.VMEM)] * n,
-        scratch_shapes=Sums.scratch(shapes, [a.dtype for a in arrays], n_planes, False)
+        out_shape=[jax.ShapeDtypeStruct(s, jnp.float32) for s in shapes[:-1] + [tile, block]],
+        in_specs=[ANY] * (n + 1),
+        out_specs=[pl.BlockSpec(memory_space=pltpu.VMEM)] * (n + 1),
+        scratch_shapes=Reduce.scratch(shapes, [a.dtype for a in arrays], n_planes, False)
+        + Reduce.scratch([block], [parts.dtype], n_planes, True)
         + [
             pltpu.VMEM(shapes[-1], jnp.float32),
             pltpu.VMEM(tile, jnp.float32),
@@ -1000,9 +1036,353 @@
             pltpu.SemaphoreType.DMA(()),
         ],
         compiler_params=pltpu.CompilerParams(
-            collective_id=collective_id, has_side_effects=True, vmem_limit_bytes=56 << 20
+            collective_id=collective_id, has_side_effects=True, vmem_limit_bytes=60 << 20
         ),
-    )(*arrays)
+    )(*arrays, parts)
+UNIT = 2
+
+
+def dot_t(a, b):
+    return lax.dot_general(a, b, (((1,), (1,)), ((), ())), preferred_element_type=jnp.float32)
+
+
+def dot_f32(a, b):
+    return lax.dot_general(a, b, (((1,), (0,)), ((), ())), preferred_element_type=jnp.float32)
+
+
+class ExpertWork:
+    def __init__(self, expert, weights, scratch):
+        self.expert = expert
+        self.w_gate, self.w_up, self.w_down, self.shared = weights
+        (
+            self.tokens, self.grads, self.rows, self.grad_rows, self.hidden, self.pre, self.left_out,
+            self.left_grad, self.right_out, self.right_grad, self.out, self.back, self.shared_hidden,
+        ) = scratch
+
+    @staticmethod
+    def scratch(model, width, capacity, own_rows):
+        bf16 = jnp.bfloat16
+        seq = 2 * own_rows
+        return [
+            pltpu.VMEM((2, 2 * UNIT, own_rows, model), bf16),
+            pltpu.VMEM((2, 2 * UNIT, own_rows, model), bf16),
+            pltpu.VMEM((2, UNIT * capacity, model), bf16),
+            pltpu.VMEM((2, UNIT * capacity, model), bf16),
+            pltpu.VMEM((2, 3, UNIT * capacity, width), bf16),
+            pltpu.VMEM((3, UNIT * capacity, width), jnp.float32),
+            pltpu.VMEM((UNIT, seq, capacity + 128), bf16),
+            pltpu.VMEM((UNIT, seq, capacity + 256), bf16),
+            pltpu.VMEM((UNIT, capacity + 128, model), bf16),
+            pltpu.VMEM((UNIT, capacity + 256, model), bf16),
+            pltpu.VMEM((2, 2 * UNIT, own_rows, model), bf16),
+            pltpu.VMEM((2, 2 * UNIT, own_rows, model), bf16),
+            pltpu.VMEM((2, UNIT * seq, 384), bf16),
+        ]
+
+    def prepare(self):
+        capacity = self.rows.shape[1] // UNIT
+        for q in range(UNIT):
+            self.right_out[q, pl.ds(capacity, 128), :] = self.shared[pl.ds(256, 128), :]
+            self.right_grad[q, pl.ds(capacity, 256), :] = self.shared[pl.ds(0, 256), :]
+
+    def run(self, slot, unit, gates, grad_gates, hook):
+        bf16, f32 = jnp.bfloat16, jnp.float32
+        own_rows, model = self.tokens.shape[2:]
+        seq = 2 * own_rows
+        capacity = self.rows.shape[1] // UNIT
+        experts = gates.shape[1]
+        column = 1024
+        n_columns = model // column
+        first = unit * (2 * UNIT)
+        before = lax.broadcasted_iota(jnp.int32, (seq, seq), 0) <= lax.broadcasted_iota(jnp.int32, (seq, seq), 1)
+        before = before.astype(f32).astype(bf16)
+        slots = lax.broadcasted_iota(jnp.int32, (capacity, seq), 0)
+        picks, row_gates = [], []
+        for q in range(UNIT):
+            g = jnp.concatenate(
+                [gates[first + 2 * q + h, pl.ds(self.expert, 1), :] for h in range(2)], axis=1
+            )
+            g = jnp.broadcast_to(g, (8, seq))
+            taken = (g > 0.0).astype(f32)
+            rank = dot_f32(taken.astype(bf16), before).astype(jnp.int32) - 1
+            hit = (slots == rank[:1]) & (g[:1] > 0.0)
+            pick = hit.astype(f32)
+            picks.append(pick)
+            row_gates.append(jnp.sum(pick * g[:1], axis=1, keepdims=True))
+            self.left_out[q, :, pl.ds(0, capacity)] = pick.T.astype(bf16)
+            self.left_grad[q, :, pl.ds(0, capacity)] = pick.T.astype(bf16)
+            low = pick.astype(bf16)
+
+            span = pl.ds(q * capacity, capacity)
+            for source, target in ((self.tokens, self.rows), (self.grads, self.grad_rows)):
+                whole = source[slot, pl.ds(2 * q, 2)].reshape(seq, model)
+                target[slot, span] = dot_f32(low, whole).astype(bf16)
+        hook(1)
+        row_gate = jnp.concatenate(row_gates, axis=0)
+        rows, grad_rows = self.rows.at[slot], self.grad_rows.at[slot]
+        self.pre[0] = dot_f32(rows[...], self.w_gate[...])
+        self.pre[1] = dot_f32(rows[...], self.w_up[...])
+        self.pre[2] = dot_t(grad_rows[...], self.w_down[...])
+        hook(2)
+        step = 32
+        parts = []
+        for r in range(UNIT * capacity // step):
+            span = pl.ds(r * step, step)
+            gate_pre, up_pre, grad_hidden = self.pre[0, span], self.pre[1, span], self.pre[2, span]
+            gate = row_gate[r * step : (r + 1) * step]
+            sig = jax.nn.sigmoid(gate_pre)
+            act = gate_pre * sig
+            hidden = act * up_pre
+            parts.append(jnp.sum(hidden * grad_hidden, axis=1, keepdims=True))
+            grad_hidden = grad_hidden * gate
+            self.hidden[slot, 0, span] = (hidden * gate).astype(bf16)
+            slope = sig * (1.0 + gate_pre * (1.0 - sig))
+            self.hidden[slot, 1, span] = (grad_hidden * up_pre * slope).astype(bf16)
+            self.hidden[slot, 2, span] = (grad_hidden * act).astype(bf16)
+        grad_gate_rows = jnp.concatenate(parts, axis=0)
+        mine = lax.broadcasted_iota(jnp.int32, (experts, own_rows), 0) == self.expert
+        for q in range(UNIT):
+            per_token = jnp.sum(picks[q] * grad_gate_rows[q * capacity : (q + 1) * capacity], axis=0, keepdims=True)
+            for h in range(2):
+                part = jnp.broadcast_to(per_token[:, h * own_rows : (h + 1) * own_rows], (experts, own_rows))
+                grad_gates[first + 2 * q + h] = jnp.where(mine, part, 0.0)
+
+        for q in range(UNIT):
+            blocks = pl.ds(2 * q, 2)
+            whole = self.tokens[slot, blocks].reshape(seq, model)
+            grad = self.grads[slot, blocks].reshape(seq, model)
+            pre = dot_t(whole, self.shared[pl.ds(0, 256), :])
+            grad_hidden = dot_t(grad, self.shared[pl.ds(256, 128), :])
+            gate_pre, up_pre = pre[:, :128], pre[:, 128:]
+            sig = jax.nn.sigmoid(gate_pre)
+            act = gate_pre * sig
+            hidden = (act * up_pre).astype(bf16)
+            grad_gate = (grad_hidden * up_pre * sig * (1.0 + gate_pre * (1.0 - sig))).astype(bf16)
+            grad_up = (grad_hidden * act).astype(bf16)
+            span = pl.ds(q * seq, seq)
+            self.shared_hidden[slot, span, pl.ds(0, 128)] = hidden
+            self.shared_hidden[slot, span, pl.ds(128, 128)] = grad_gate
+            self.shared_hidden[slot, span, pl.ds(256, 128)] = grad_up
+            self.left_out[q, :, pl.ds(capacity, 128)] = hidden
+            self.left_grad[q, :, pl.ds(capacity, 128)] = grad_gate
+            self.left_grad[q, :, pl.ds(capacity + 128, 128)] = grad_up
+
+        hook(3)
+
+        def combine(c, carry):
+            cols = pl.ds(pl.multiple_of(c * column, column), column)
+            made = dot_f32(self.hidden[slot, 0], self.w_down[:, cols]).astype(bf16)
+            back = dot_t(self.hidden[slot, 1], self.w_gate[cols, :])
+            back = (back + dot_t(self.hidden[slot, 2], self.w_up[cols, :])).astype(bf16)
+            for q in range(UNIT):
+                span = slice(q * capacity, (q + 1) * capacity)
+                self.right_out[q, pl.ds(0, capacity), cols] = made[span]
+                self.right_grad[q, pl.ds(0, capacity), cols] = back[span]
+                out = dot_f32(self.left_out[q], self.right_out[q, :, cols]).astype(bf16)
+                self.out[slot, pl.ds(2 * q, 2), :, cols] = out.reshape(2, own_rows, column)
+                out = dot_f32(self.left_grad[q], self.right_grad[q, :, cols]).astype(bf16)
+                self.back[slot, pl.ds(2 * q, 2), :, cols] = out.reshape(2, own_rows, column)
+
+            @pl.when(c == n_columns // 2)
+            def _():
+                hook(4)
+
+            return carry
+
+        lax.fori_loop(0, n_columns, combine, 0)
+
+
+def expert_kernel(n_dp, *refs):
+    own, own_gates, grads, w_gate, w_up, w_down, shared = refs[:7]
+    normed, out_parts, back_parts, grad_gates, rows_out, grad_rows_out, hidden_out, shared_out = refs[7:15]
+    scratch, (gates, load, store, local, send, recv) = refs[15:-6], refs[-6:]
+    n_planes = n_dp // 4
+    spot = Spot(n_planes)
+    half = own.shape[0] // 2
+
+    def views(s, yy, cc, xx, part):
+        b = dp_of(s, yy, cc) * 2 + xx
+        if part == ALL:
+            return [normed.at[b], gates.at[b]]
+        if part == FIRST:
+            return [normed.at[b, pl.ds(0, half)], gates.at[b]]
+        return [normed.at[b, pl.ds(half, half)]]
+
+    kept = [
+        pltpu.make_async_copy(a, v, local.at[i])
+        for i, (a, v) in enumerate(zip((own, own_gates), views(spot.z, spot.y, spot.core, spot.x, ALL)))
+    ]
+    for c in kept:
+        c.start()
+    spot.greet()
+    copies = Copies(n_planes, send, recv)
+    net = Spread(spot, copies, [own, own_gates], views, True)
+    net.begin()
+    work = ExpertWork(spot.dp, (w_gate, w_up, w_down, shared), scratch)
+    work.prepare()
+    n_units = n_dp // UNIT
+    blocks = 2 * UNIT
+    rows = work.rows.shape[1]
+    seqs = work.shared_hidden.shape[1]
+    order = net.order
+
+    def unit_of(i):
+        s = 0 * i
+        for j, plane in enumerate(order):
+            s = s + (i // 2 == j).astype(jnp.int32) * plane
+        yy = spot.y + (i % 2) * (1 - 2 * spot.y)
+        return s * 2 + yy
+
+    def loads(u, slot):
+        span = pl.ds(u * blocks, blocks)
+        return [
+            pltpu.make_async_copy(normed.at[span], work.tokens.at[slot], load.at[slot, 0]),
+            pltpu.make_async_copy(grads.at[span], work.grads.at[slot], load.at[slot, 1]),
+        ]
+
+    def stores(u, slot):
+        span = pl.ds(u * blocks, blocks)
+        some = pl.ds(pl.multiple_of(u * rows, rows), rows)
+        pairs = [
+            (work.out.at[slot], out_parts.at[span]),
+            (work.back.at[slot], back_parts.at[span]),
+            (work.rows.at[slot], rows_out.at[some]),
+            (work.grad_rows.at[slot], grad_rows_out.at[some]),
+            (work.hidden.at[slot], hidden_out.at[:, some]),
+            (work.shared_hidden.at[slot], shared_out.at[pl.ds(pl.multiple_of(u * seqs, seqs), seqs)]),
+        ]
+        return [pltpu.make_async_copy(a, b, store.at[slot, i]) for i, (a, b) in enumerate(pairs)]
+
+    def load_unit(i):
+        loads(unit_of(jnp.int32(i)), i % 2)[0].start()
+
+    def near(j):
+        net.twin_near(j)
+        load_unit(2 * j)
+
+    def far(j):
+        net.twin_far(j)
+        load_unit(2 * j + 1)
+
+    def on(j):
+        net.onward(j, net.mine[j][0])
+
+    middle = spot.has_up & spot.has_down
+    end = jnp.logical_not(middle)
+
+    goes = {
+        (j, c): (net.goes_down[j] & (middle if c else end), net.goes_up[j] & (middle if c else end))
+        for j in range(1, n_planes)
+        for c in (0, 1)
+    }
+
+    def relay(j, c):
+        pl.when(middle if c else end)(functools.partial(net.relay, j, goes[j, c]))
+
+    plan = {
+        (0, 0): [(on, 1)],
+        (0, 1): [(net.corner, 0)],
+        (0, 2): [(far, 0)],
+        (0, 4): [(relay, 2, 0), (relay, 3, 1)],
+        (1, 0): [(net.sides, 1)],
+        (1, 1): [(on, 2)],
+        (1, 2): [(near, 1)],
+        (1, 3): [(net.corner, 1)],
+        (2, 0): [(far, 1)],
+        (2, 3): [(net.sides, 2), (relay, 3, 0)],
+        (2, 4): [(on, 3)],
+        (3, 0): [(near, 2)],
+        (3, 1): [(net.corner, 2)],
+        (4, 0): [(net.sides, 3), (far, 2)],
+        (4, 3): [(net.corner, 3)],
+        (5, 0): [(near, 3)],
+        (6, 0): [(far, 3)],
+    }
+
+    net.relay(1)
+    relay(2, 1)
+    net.sides(0)
+    for c in kept:
+        c.wait()
+    near(0)
+    loads(unit_of(jnp.int32(0)), 0)[1].start()
+
+    def body(i, carry):
+        slot = i % 2
+        u = unit_of(i)
+
+        def hook(point):
+            for (k, at), actions in plan.items():
+                if at == point:
+
+                    @pl.when(i == k)
+                    def _(actions=actions):
+                        for action, *values in actions:
+                            action(*values)
+
+        hook(0)
+
+        @pl.when(i + 1 < n_units)
+        def _():
+            loads(unit_of(i + 1), 1 - slot)[1].start()
+
+        for c in loads(u, slot):
+            c.wait()
+
+        @pl.when(i >= 2)
+        def _():
+            for c in stores(unit_of(i - 2), slot):
+                c.wait()
+
+        work.run(slot, u, gates, grad_gates, hook)
+        for c in stores(u, slot):
+            c.start()
+        return carry
+
+    lax.fori_loop(0, n_units, body, 0)
+    for i in (n_units - 2, n_units - 1):
+        for c in stores(unit_of(jnp.int32(i)), i % 2):
+            c.wait()
+    copies.close()
+
+
+def expert_call(own, own_gates, grads, w_gate, w_up, w_down, shared, n_dp, capacity, collective_id):
+    own_rows, model = own.shape
+    blocks = 2 * n_dp
+    width = w_gate.shape[1]
+    bf16 = jnp.bfloat16
+    rows = n_dp * capacity
+    n_planes = n_dp // 4
+    vmem = pl.BlockSpec(memory_space=pltpu.VMEM)
+    everyone = jax.ShapeDtypeStruct((blocks, own_rows, model), bf16)
+    all_gates = (blocks,) + own_gates.shape
+    return pl.pallas_call(
+        functools.partial(expert_kernel, n_dp),
+        out_shape=[
+            everyone,
+            everyone,
+            everyone,
+            jax.ShapeDtypeStruct(all_gates, jnp.float32),
+            jax.ShapeDtypeStruct((rows, model), bf16),
+            jax.ShapeDtypeStruct((rows, model), bf16),
+            jax.ShapeDtypeStruct((3, rows, width), bf16),
+            jax.ShapeDtypeStruct((blocks * own_rows, 384), bf16),
+        ],
+        in_specs=[ANY, ANY, ANY, vmem, vmem, vmem, vmem],
+        out_specs=[ANY, ANY, ANY, vmem, ANY, ANY, ANY, ANY],
+        scratch_shapes=ExpertWork.scratch(model, width, capacity, own_rows)
+        + [
+            pltpu.VMEM(all_gates, jnp.float32),
+            pltpu.SemaphoreType.DMA((2, 2)),
+            pltpu.SemaphoreType.DMA((2, 6)),
+            pltpu.SemaphoreType.DMA((2,)),
+            pltpu.SemaphoreType.DMA((11 * n_planes, 2)),
+            pltpu.SemaphoreType.DMA((11 * n_planes, 2)),
+        ],
+        compiler_params=pltpu.CompilerParams(
+            collective_id=collective_id, has_side_effects=True, vmem_limit_bytes=60 << 20
+        ),
+    )(own, own_gates, grads, w_gate, w_up, w_down, shared)
 
 
 def swap_halves(own, x):
@@ -1051,9 +1431,9 @@
     small = jnp.concatenate([attention_gain, expert_norm_gain, router.reshape(-1)])
     small = jnp.pad(small, (0, -small.shape[0] % 2048)).reshape(-1, 128)
     axes = (0, 0, 0, 1)
-    query_all, key_all, value_all, out_all, sequence, smalls = fetch(
+    query_all, key_all, value_all, out_all, sequence, smalls, cotangent_all = fetch(
         [query_projection, key_projection, value_projection, output_projection],
-        axes, tokens, small, n_dp, 1,
+        axes, tokens, small, cotangent, n_dp, 1,
     )
     flat = smalls.swapaxes(0, 1).reshape(2 * n_dp, -1)
     first_gain = flat[:, :width].reshape(-1).astype(f32)
@@ -1072,7 +1452,6 @@
     )
     shared_in = lax.all_to_all(shared_out, DP, split_axis=0, concat_axis=0, tiled=True)
     shared_rows = jnp.moveaxis(shared_in, 0, 2).reshape(3, hidden_pad, model_dim)
-    sgate_t, sup_t, sdown = shared_rows[0], shared_rows[1], shared_rows[2]
 
     full_tokens = sequence.reshape(sequence_length, model_dim).astype(f32)
     full_scale = lax.rsqrt(jnp.mean(full_tokens * full_tokens, axis=-1, keepdims=True) + norm_eps)
@@ -1121,66 +1500,24 @@
     gate_probs = gate_exp / jnp.sum(gate_exp, axis=-1, keepdims=True)
     gates = jnp.sum(jnp.where(chosen, gate_probs[:, :, None], 0.0), axis=1)
 
-    (cotangent_all,) = gather_everywhere([cotangent], n_dp, 3)
-    normed_all, gates_all = gather_everywhere([normed_two, gates.T], n_dp, 2)
-
-    normed_seq = normed_all.reshape(n_dp, sequence_length, model_dim)
-    grad_seq = cotangent_all.reshape(n_dp, sequence_length, model_dim)
-    gate_seq = lax.dynamic_index_in_dim(gates_all, dp, 1, keepdims=False).reshape(n_dp, sequence_length)
-    routed = gate_seq > 0.0
-    rank = jnp.cumsum(routed.astype(jnp.int32), axis=1) - 1
-    pick = (rank[:, None, :] == jnp.arange(capacity, dtype=jnp.int32)[None, :, None]) & routed[:, None, :]
-    pick_low = pick.astype(bf16)
-    rows = n_dp * capacity
-    received = jnp.einsum("sjt,std->sjd", pick_low, normed_seq, preferred_element_type=f32)
-    received = received.astype(bf16).reshape(rows, model_dim)
-    grad_rows = jnp.einsum("sjt,std->sjd", pick_low, grad_seq, preferred_element_type=f32)
-    grad_rows = grad_rows.astype(bf16).reshape(rows, model_dim)
-    gate_rows = jnp.sum(jnp.where(pick, gate_seq[:, None, :], 0.0), axis=-1).reshape(rows, 1)
-    w_gate, w_up, w_down = expert_gate_matrix[0], expert_up_matrix[0], expert_down_matrix[0]
-    gate_pre = dot(received, w_gate)
-    up_pre = dot(received, w_up)
-    hidden_rows = silu(gate_pre) * up_pre
-    gated_hidden = (hidden_rows * gate_rows).astype(bf16)
-    produced = dot(gated_hidden, w_down).astype(bf16)
-    grad_hidden = dot(grad_rows, w_down.T)
-    grad_gate_rows = jnp.sum(hidden_rows * grad_hidden, axis=-1).reshape(n_dp, capacity)
-    grad_hidden = grad_hidden * gate_rows
-    grad_gate = (grad_hidden * up_pre * silu_slope(gate_pre)).astype(bf16)
-    grad_up = (grad_hidden * silu(gate_pre)).astype(bf16)
-    grad_received = (dot(grad_gate, w_gate.T) + dot(grad_up, w_up.T)).astype(bf16)
-    expert_gate_gradient = dot(received.T, grad_gate)[None]
-    expert_up_gradient = dot(received.T, grad_up)[None]
-    expert_down_gradient = dot(gated_hidden.T, grad_rows)[None]
-
+
+    shared_rows = jnp.pad(shared_rows, ((0, 0), (0, 128 - hidden_pad), (0, 0))).reshape(384, model_dim)
+    normed_all, output_parts, normed_parts, grad_gate_parts, received, grad_rows, hidden_rows, shared_hidden = (
+        expert_call(
+            normed_two, gates.T, cotangent_all, expert_gate_matrix[0], expert_up_matrix[0], expert_down_matrix[0],
+            shared_rows, n_dp, capacity, 2,
+        )
+    )
+    expert_gate_gradient = dot(received.T, hidden_rows[1])[None]
+    expert_up_gradient = dot(received.T, hidden_rows[2])[None]
+    expert_down_gradient = dot(hidden_rows[0].T, grad_rows)[None]
     normed_flat = normed_all.reshape(-1, model_dim)
     grad_flat = cotangent_all.reshape(-1, model_dim)
-    gate_shared = dot(normed_flat, sgate_t.T)
-    up_shared = dot(normed_flat, sup_t.T)
-    hidden_shared = (silu(gate_shared) * up_shared).astype(bf16)
-    grad_hidden_sh = dot(grad_flat, sdown.T)
-    grad_gate_sh = (grad_hidden_sh * up_shared * silu_slope(gate_shared)).astype(bf16)
-    grad_up_sh = (grad_hidden_sh * silu(gate_shared)).astype(bf16)
-    shared_grads = jnp.stack(
-        [dot(grad_gate_sh.T, normed_flat), dot(grad_up_sh.T, normed_flat), dot(hidden_shared.T, grad_flat)]
+    shared_grads = jnp.concatenate(
+        [dot(shared_hidden[:, 128:].T, normed_flat), dot(shared_hidden[:, :128].T, grad_flat)]
     ).astype(bf16)
-
-    def scatter(rows_out, shared_part):
-        back = jnp.einsum(
-            "sjt,sjd->std", pick_low, rows_out.reshape(n_dp, capacity, model_dim), preferred_element_type=f32
-        )
-        total = back.reshape(-1, model_dim) + shared_part
-        return total.astype(bf16).reshape(2 * n_dp, own_rows, model_dim)
-
-    output_parts = scatter(produced, dot(hidden_shared, sdown))
-    normed_parts = scatter(grad_received, dot(grad_gate_sh, sgate_t) + dot(grad_up_sh, sup_t))
-    grad_gate_tokens = jnp.sum(jnp.where(pick, grad_gate_rows[:, :, None], 0.0), axis=1)
-    grad_gate_parts = jnp.where(
-        jnp.arange(experts)[None, :, None] == dp, grad_gate_tokens.reshape(2 * n_dp, 1, own_rows), 0.0
-    )
+    shared_grads = shared_grads.reshape(3, 128, model_dim)[:, :hidden_pad]
     grad_normed_two, grad_gates_t = sum_everywhere([normed_parts, grad_gate_parts], [f32, f32], n_dp, 4)
-    (ffn_own,) = sum_everywhere([output_parts], [f32], n_dp, 5)
-    output = (residual + ffn_own).astype(bf16)
 
     grad_gates = grad_gates_t.T
     grad_logits = (
@@ -1232,8 +1569,9 @@
     small_rows = tiles.shape[1] // 128
     sums = sum_back(
         [grad_wquery, grad_wkey, grad_wvalue, grad_wout.astype(bf16), tiles.reshape(-1, 128)],
-        axes + (0,), n_dp, 6,
-    )
+        axes + (0,), output_parts, n_dp, 6,
+    )
+    output = (residual + sums[5]).astype(bf16)
     mine = sums[4].reshape(-1)
     gain_one_own, gain_two_own = mine[:width], mine[width : 2 * width]
     router_own = mine[2 * width : (2 + experts) * width].reshape(width, experts)

time: 943 us -> 690 us (0.73)
  matrix products: 293 us -> 94.5 us
  local copies, waits for them, and re-layouts: 92.9 us -> 51.9 us
  other arithmetic: 38.2 us -> 20.2 us
  waiting for transfers between devices: 3.37 us -> 14.9 us
    dot_general x33 -> x20, matrix products: 240 us -> 85.5 us  [dot(): return jnp.dot(a, b, preferred_element_type=f32)]
    pallas_call x2 -> x1, Pallas kernels: 155 us -> 79.1 us  [sum_everywhere(): pl.pallas_call(functools.partial(sum_kernel, n_planes, n), out_shape=[jax...]
    pallas_call x1, Pallas kernels: 73.2 us -> 138 us  [fetch(): pl.pallas_call(functools.partial(fetch_kernel, n_planes, axes), out_shape...]
    pallas_call x1, Pallas kernels: 82 us -> 141 us  [sum_back(): pl.pallas_call(functools.partial(return_kernel, n_planes, axes), out_shap...]
    pallas_call x2 -> x1, Pallas kernels: 176 us -> 123 us  [expert_call(): pl.pallas_call(functools.partial(expert_kernel, n_dp), out_shape=[everyon...]
    dot_general x4 -> x0, matrix products: 45 us -> none  [the longest x2 27.7 us: scatter(): jnp.einsum('sjt,sjd->std', pick_low, rows_out.reshape(n_dp, capacity, mod...]
    dot_general x4 -> x2, local copies, waits for them, and re-layouts: 51.4 us -> 7.92 us  [dot(): return jnp.dot(a, b, preferred_element_type=f32)]
    all_to_all x1, waiting for transfers between devices: 0.01 us -> 11 us  [gather_plan(): lax.all_to_all(shared_out, DP, split_axis=0, concat_axis=0, tiled=True)]
  transfers between devices with their start and end apart: 5 -> 5, of which waited for: 1 -> 2; matrix products, arithmetic and copies ran while one was open for 26% -> 12% of each run, Pallas kernels for 28% -> 21%
where the time goes in v2:
time: 690 us; the launch traced here: 679 us
  Pallas kernels  482 us (70%)
  matrix products  94.5 us (14%)
  local copies, waits for them, and re-layouts  51.9 us (8%)
  other arithmetic  20.2 us (3%)
  waiting for transfers between devices  14.9 us (2%)
  starting transfers between devices  13.5 us (2%)
    pallas_call x1, Pallas kernels, sum_back(): pl.pallas_call(functools.partial(return_kernel, n_planes, axes), out_shap...  141 us
    pallas_call x1, Pallas kernels, fetch(): pl.pallas_call(functools.partial(fetch_kernel, n_planes, axes), out_shape...  138 us
    pallas_call x1, Pallas kernels, expert_call(): pl.pallas_call(functools.partial(expert_kernel, n_dp), out_shape=[everyon...  123 us
    dot_general x20, matrix products, dot(): return jnp.dot(a, b, preferred_element_type=f32)  85.5 us
    pallas_call x1, Pallas kernels, sum_everywhere(): pl.pallas_call(functools.partial(sum_kernel, n_planes, n), out_shape=[jax...  79.1 us
    unnamed x118, local copies, waits for them, and re-layouts  24.4 us
  transfers between devices with their start and end apart: 5, of which 2 were waited for; matrix products, arithmetic and copies ran while one was open for 12% of the time, Pallas kernels for 21%

profile of v2, /device:TPU:24, one launch (start us, length us, event | category | flops | bytes accessed | tf_op | source)
XLA Modules:
  0.0 678.9 jit_solution(12246406383587010357)
XLA Ops:
  5.5 138.2 %shard_map.280 = (bf16[2048,1024]{1,0:T(8,128)(2,1)}, bf16[2048,256]{1,0:T(8,128)(2,1)}, bf16[2048,256]{1,0:T(8,128)(2,1)}, bf16[1024,2048]{1,0:T(8,128)(2,1)}, ...) custom-call(bf16[128,1024]{1,0:T(8,128)(2,1)} %refs_0_.1, ...), custom_call_target="tpu_custom_call" | custom-call | tf_op jit(solution)/shard_map/pallas_call | solution.py:725
  144.8 1.6 multiply_reduce_fusion
  150.3 6.4 copy.209
  157.2 3.5 fusion.57
  162.1 2.0 convolution_convert_fusion.8
  164.2 3.2 fusion.55
  167.4 2.1 convolution_convert_fusion.6
  177.8 5.5 all-to-all-start
  183.3 4.6 copy.175
  187.9 4.6 copy.176
  194.4 1.6 multiply_reduce_fusion.3
  197.2 11.0 %all-to-all-done = bf16[16,3,96,128]{3,2,1,0:T(8,128)(2,1)} async-done(((bf16[16,3,96,128]{3,2,1,0:T(8,128)(2,1)}), bf16[16,3,96,128]{3,2,1,0:T(8,128)(2,1)}, u32[]{:S(2)}, u32[]{:S(2)}) %all-to-all-start) | async-done | bytes 1179680 | tf_op jit(solution)/shard_map/all_to_all | solution.py:1453
  211.0 123.3 %shard_map.281 = (bf16[32,128,2048]{2,1,0:T(8,128)(2,1)}, bf16[32,128,2048]{2,1,0:T(8,128)(2,1)}, bf16[32,128,2048]{2,1,0:T(8,128)(2,1)}, f32[32,16,128]{2,1,0:T...) custom-call(bf16[128,2048]{1,0:T(8,128)(2,1)} %copy-done.4, ...), custom_call_target="tpu_custom_call" | custom-call | tf_op jit(solution)/shard_map/pallas_call | solution.py:1359
  334.3 11.3 %convolution_bitcast_fusion.1 = f32[1,2048,704]{1,2,0:T(8,128)} fusion(bf16[2048,2048]{1,0:T(8,128)(2,1)} %get-tuple-element.58, bf16[3,2048,704]{2,1,0:T(8,128)(2,1)} %get-tuple-element.59), kind=kOutput, calls=%fused_computation.4 | convolution fusion | flops 5905580032 | bytes 17301504 | tf_op jit(solution)/shard_map/dot_general | solution.py:1428
  345.6 20.9 %convolution_bitcast_fusion.2 = f32[1,2048,704]{1,2,0:T(8,128)} fusion(bf16[2048,2048]{1,0:T(8,128)(2,1)S(1)} %copy-done.44, bf16[3,2048,704]{2,1,0:T(8,128)(2,1)} %get-tuple-element.59), kind=kOutput, calls=%fused_computation.5 | convolution fusion | flops 5905580032 | bytes 17301504 | tf_op jit(solution)/shard_map/dot_general | solution.py:1428
  366.4 79.1 %shard_map.282 = (f32[128,2048]{1,0:T(8,128)}, f32[16,128]{1,0:T(8,128)}) custom-call(bf16[32,128,2048]{2,1,0:T(8,128)(2,1)} %get-tuple-element.45.refs_0_, f32[32,16,128]{2,1,0:T(8,128)} %get-tuple-element.46.refs_1_), custom_call_target="tpu_custom_call" | custom-call | tf_op jit(solution)/shard_map/pallas_call | solution.py:959
  447.1 1.9 multiply_reduce_fusion.1
  449.1 1.5 fusion.52
  450.6 8.4 %convolution_convert_fusion.5 = bf16[128,2048]{1,0:T(8,128)(2,1)S(1)} fusion(bf16[4096,2048]{1,0:T(8,128)(2,1)} %bitcast.205, bf16[4096,384]{1,0:T(8,128)(2,1)S(1)} %copy-done.7), kind=kOutput, calls=%fused_computation.18 | convolution fusion | flops 2147745792 | bytes 18350080 | tf_op jit(solution)/shard_map/dot_general | solution.py:1428
  460.4 4.5 convolution_convert_fusion.2
  466.9 6.4 all-to-all-start.1
  473.2 11.4 %convolution_bitcast_fusion = f32[1,704,2048]{2,1,0:T(8,128)} fusion(bf16[2048,2048]{1,0:T(8,128)(2,1)} %get-tuple-element.60, bf16[3,2048,704]{2,1,0:T(8,128)(2,1)} %get-tuple-element.59), kind=kOutput, calls=%fused_computation.3 | convolution fusion | flops 5905580032 | bytes 17301504 | tf_op jit(solution)/shard_map/dot_general | solution.py:1428
  486.6 1.8 reshape.407
  488.4 4.9 convolution_convert_fusion.7
  494.6 2.2 fusion.16
  500.1 1.6 copy-done.10
  506.9 4.9 convolution_convert_fusion.refs_3_
  513.2 3.3 convolution_convert_fusion.1.refs_0_
  516.5 3.8 collective-permute-done.2
  521.7 141.4 %shard_map.283 = (f32[128,1024]{1,0:T(8,128)}, f32[128,256]{1,0:T(8,128)}, f32[128,256]{1,0:T(8,128)}, f32[1024,128]{1,0:T(8,128)}, f32[16,128]{1,0:T(8,128)}, /*index=5*/f32[128,2048]{1,0:T(8,128)}) custom-call(bf16[2048,1024]{1,0:T(8,128)(2,1)} %convolution_convert_fusion.1.refs_0_, bf16[2048,256]{1,0:T(8,128)(2,1)} %convolution_convert_fusion.4.refs_1_, ...), custom_call_target="tpu_custom_call" | custom-call | tf_op jit(solution)/shard_map/pallas_call | solution.py:1025
  666.0 2.2 add_convert_fusion
  668.2 2.7 fusion.21
  (198 shorter events, 55.0 us)
Async XLA Ops:
  0.6 193.7 %copy-start = (s32[256,6]{0,1:T(8,128)S(1)}, s32[256,6]{0,1:T(8,128)}, u32[]{:S(2)}) copy-start(s32[256,6]{0,1:T(8,128)} %param.32) | copy-start | bytes 18436
  144.8 3.9 copy-start.25
  161.8 5.6 copy-start.17
  162.1 5.3 copy-start.19
  170.3 3.7 copy-start.24
  172.9 21.5 %collective-permute-start = (bf16[128,2048]{1,0:T(8,128)(2,1)S(1)}, bf16[128,2048]{1,0:T(8,128)(2,1)S(1)}, u32[]{:S(2)}, u32[]{:S(2)}) collective-permute-start(bf16[128,2048]{1,0:T(8,128)(2,1)S(1)} %dynamic-slice_convert_fusion.1), channel_id=1, source_target_pairs={{0,1},{1,0},{2,3},{3,2},{4,5},{5,4},{6,7},{7,6},{8,9},{9,8},{10,11... | collective-permute-start | bytes 1572872 | tf_op jit(solution)/shard_map/ppermute | solution.py:1389
  176.7 6.6 copy-start.26
  177.8 30.5 %all-to-all-start = ((bf16[16,3,96,128]{3,2,1,0:T(8,128)(2,1)}), bf16[16,3,96,128]{3,2,1,0:T(8,128)(2,1)}, u32[]{:S(2)}, u32[]{:S(2)}) async-start(bf16[16,3,96,128]{3,2,1,0:T(8,128)(2,1)} %copy.179), calls=%async_computation | async-start | bytes 2359296 | tf_op jit(solution)/shard_map/all_to_all | solution.py:1453
  187.9 4.6 copy-start.37
  187.9 5.9 copy-start.41
  187.9 6.5 copy-start.6
  196.2 14.8 %copy-start.4 = (bf16[128,2048]{1,0:T(8,128)(2,1)}, bf16[128,2048]{1,0:T(8,128)(2,1)S(1)}, u32[]{:S(2)}) copy-start(bf16[128,2048]{1,0:T(8,128)(2,1)S(1)} %multiply_convert_fusion.1.refs_0_) | copy-start | bytes 1572868
  334.2 11.3 %copy-start.44 = (bf16[2048,2048]{1,0:T(8,128)(2,1)S(1)}, bf16[2048,2048]{1,0:T(8,128)(2,1)}, u32[]{:S(2)}) copy-start(bf16[2048,2048]{1,0:T(8,128)(2,1)} %get-tuple-element.58) | copy-start | bytes 25165828
  366.4 79.2 %copy-start.31 = (f32[128,16]{0,1:T(8,128)S(1)}, f32[128,16]{0,1:T(8,128)}, u32[]{:S(2)}) copy-start(f32[128,16]{0,1:T(8,128)} %select_reduce_fusion) | copy-start | bytes 24580
  366.4 80.6 %copy-start.9 = (bf16[2048,16]{1,0:T(8,128)(2,1)S(1)}, bf16[2048,16]{1,0:T(8,128)(2,1)}, u32[]{:S(2)}) copy-start(bf16[2048,16]{1,0:T(8,128)(2,1)} %reshape.396) | copy-start | bytes 196612
  449.0 10.0 %slice-start = ((s8[16777216]{0:T(1024)(128)(4,1)}), s8[4194304]{0:T(1024)(128)(4,1)S(1)}, s32[]{:S(2)}) async-start(s8[16777216]{0:T(1024)(128)(4,1)} %bitcast.211), calls=%async_computation.2 | async-start | bytes 8388608
  450.6 37.8 %collective-permute-start.1 = (bf16[128,2048]{1,0:T(8,128)(2,1)}, bf16[128,2048]{1,0:T(8,128)(2,1)}, u32[]{:S(2)}, u32[]{:S(2)}) collective-permute-start(bf16[128,2048]{1,0:T(8,128)(2,1)} %get-tuple-element.155), channel_id=1, source_target_pairs={{0,1},{1,0},{2,3},{3,2},{4,5},{5,4},{6,7},{7,6},{8,9},{9,8},{10,11... | collective-permute-start | bytes 1572872 | tf_op jit(solution)/shard_map/ppermute | solution.py:1389
  450.6 8.4 %slice-start.1 = ((s8[16777216]{0:T(1024)(128)(4,1)}), s8[4194304]{0:T(1024)(128)(4,1)S(1)}, s32[]{:S(2)}) async-start(s8[16777216]{0:T(1024)(128)(4,1)} %bitcast.211), calls=%async_computation.3 | async-start | bytes 8388608
  450.6 8.6 %slice-start.2 = ((s8[16777216]{0:T(1024)(128)(4,1)}), s8[4194304]{0:T(1024)(128)(4,1)S(1)}, s32[]{:S(2)}) async-start(s8[16777216]{0:T(1024)(128)(4,1)} %bitcast.211), calls=%async_computation.4 | async-start | bytes 8388608
  450.6 9.8 %slice-start.3 = ((s8[16777216]{0:T(1024)(128)(4,1)}), s8[4194304]{0:T(1024)(128)(4,1)S(1)}, s32[]{:S(2)}) async-start(s8[16777216]{0:T(1024)(128)(4,1)} %bitcast.211), calls=%async_computation.5 | async-start | bytes 8388608
  466.9 204.1 %all-to-all-start.1 = ((bf16[16,3,96,128]{3,2,1,0:T(8,128)(2,1)}), bf16[16,3,96,128]{3,2,1,0:T(8,128)(2,1)}, u32[]{:S(2)}, u32[]{:S(2)}) async-start(bf16[16,3,96,128]{3,2,1,0:T(8,128)(2,1)} %copy.189), calls=%async_computation.1 | async-start | bytes 2359296 | tf_op jit(solution)/shard_map/all_to_all | solution.py:1578
  473.2 12.1 %copy-start.5 = (bf16[128,2048]{1,0:T(8,128)(2,1)S(1)}, bf16[128,2048]{1,0:T(8,128)(2,1)}, u32[]{:S(2)}) copy-start(bf16[128,2048]{1,0:T(8,128)(2,1)} %copy-done.4) | copy-start | bytes 1572868
  488.4 6.2 copy-start.39
  506.2 14.1 %copy-start.2 = (f32[256,2048]{1,0:T(8,128)}, f32[256,2048]{1,0:T(8,128)S(1)}, u32[]{:S(2)}) copy-start(f32[256,2048]{1,0:T(8,128)S(1)} %convolution_add_fusion) | copy-start | bytes 6291460
  506.3 14.1 %collective-permute-start.2 = (bf16[128,2048]{1,0:T(8,128)(2,1)S(1)}, bf16[128,2048]{1,0:T(8,128)(2,1)S(1)}, u32[]{:S(2)}, u32[]{:S(2)}) collective-permute-start(bf16[128,2048]{1,0:T(8,128)(2,1)S(1)} %dynamic-slice_convert_fusion), channel_id=1, source_target_pairs={{0,1},{1,0},{2,3},{3,2},{4,5},{5,4},{6,7},{7,6},{8,9},{9,8},{10,11... | collective-permute-start | bytes 1572872 | tf_op jit(solution)/shard_map/ppermute | solution.py:1389
  513.2 7.2 %copy-start.42 = (f32[128]{0:T(128)S(1)}, f32[128]{0:T(128)}, u32[]{:S(2)}) copy-start(f32[128]{0:T(128)} %get-tuple-element.175) | copy-start | bytes 1540
  516.5 4.3 copy-start.36
  663.1 5.1 copy-start.11
  663.1 5.1 copy-start.43
  673.3 3.7 copy-start.34
  673.3 4.4 copy-start.22
  673.3 5.2 copy-start.1
  (25 other events, 50.4 us)

commit v3 on v2

--- a/solution.py
+++ b/solution.py
@@ -564,18 +564,32 @@
         self.goes_down = [(s > spot.z) & spot.has_down for s in self.order]
         self.goes_up = [(s < spot.z) & spot.has_up for s in self.order]
 
-    def onward(self, j, sources):
-        s, here, spot, start = self.order[j], self.mine[j][0], self.spot, self.copies.start
-        start(None, Y_ALL, s, sources, here, spot.side)
+    def place(self, j):
+        return self.own if j == 0 else self.mine[j][0]
+
+    def onward_y(self, j):
+        self.copies.start(None, Y_ALL, self.order[j], self.place(j), self.mine[j][0], self.spot.side)
+
+    def onward_x(self, j):
+        self.copies.start(None, X_ALL, self.order[j], self.place(j), self.mine[j][0], self.spot.across)
+
+    def onward_twin(self, j):
+        self.copies.start(None, C_OWN, self.order[j], self.place(j), self.mine[j][0], self.spot.twin)
+
+    def onward(self, j):
+        self.onward_y(j)
         if self.use_x:
-            start(None, X_ALL, s, sources, here, spot.across)
-        start(None, C_OWN, s, sources, here, spot.twin)
-
-    def begin(self):
+            self.onward_x(j)
+        self.onward_twin(j)
+
+    def begin_z(self):
         spot, here = self.spot, self.mine[0][0]
         self.copies.start(spot.has_up, Z_UP, spot.z, self.own, here, spot.up)
         self.copies.start(spot.has_down, Z_DOWN, spot.z, self.own, here, spot.down, Z_UP)
-        self.onward(0, self.own)
+
+    def begin(self):
+        self.begin_z()
+        self.onward(0)
 
     def relay(self, j, goes=None):
         s, here, spot = self.order[j], self.mine[j][0], self.spot
@@ -587,20 +601,34 @@
     def column(self, j):
         if j < len(self.order):
             self.relay(j)
-            self.onward(j, self.mine[j][0])
+            self.onward(j)
+
+    def from_side(self, j):
+        s, there, spot = self.order[j], self.mine[j][1], self.spot
+        self.copies.arrive(Y_ALL, s, there, spot.side)
+        self.copies.start(None, C_Y, s, there, there, spot.twin)
+
+    def from_across(self, j):
+        s, there, spot = self.order[j], self.mine[j][3], self.spot
+        self.copies.arrive(X_ALL, s, there, spot.across)
+        self.copies.start(None, C_X, s, there, there, spot.twin)
+
+    def over_x(self, j):
+        part = self.mine[j][2]
+        self.copies.start(None, X_HALF, self.order[j], part, part, self.spot.across)
+
+    def over_y(self, j):
+        part = self.mine[j][4]
+        self.copies.start(None, Y_HALF, self.order[j], part, part, self.spot.side)
 
     def side(self, j):
-        s, (_, there, part, *_), spot = self.order[j], self.mine[j], self.spot
-        self.copies.arrive(Y_ALL, s, there, spot.side)
+        self.from_side(j)
         if self.use_x:
-            self.copies.start(None, X_HALF, s, part, part, spot.across)
-        self.copies.start(None, C_Y, s, there, there, spot.twin)
+            self.over_x(j)
 
     def across(self, j):
-        s, (_, _, _, there, part, *_), spot = self.order[j], self.mine[j], self.spot
-        self.copies.arrive(X_ALL, s, there, spot.across)
-        self.copies.start(None, Y_HALF, s, part, part, spot.side)
-        self.copies.start(None, C_X, s, there, there, spot.twin)
+        self.from_across(j)
+        self.over_y(j)
 
     def sides(self, j):
         if 0 <= j < len(self.order):
@@ -611,7 +639,8 @@
     def corner(self, j):
         if not self.use_x or not 0 <= j < len(self.order):
             return
-        s, (_, _, _, _, _, first, second), spot = self.order[j], self.mine[j], self.spot
+        s, spot = self.order[j], self.spot
+        first, second = self.mine[j][5:]
         self.copies.arrive(X_HALF, s, first, spot.across)
         self.copies.start(None, C_XH, s, first, first, spot.twin)
         self.copies.arrive(Y_HALF, s, second, spot.side)
@@ -623,12 +652,17 @@
         if self.use_x:
             self.copies.arrive(C_X, s, there[3], spot.twin)
 
+    def twin_side(self, j):
+        self.copies.arrive(C_Y, self.order[j], self.twins[j][1], self.spot.twin)
+
+    def twin_corner(self, j):
+        self.copies.arrive(C_XH, self.order[j], self.twins[j][5], self.spot.twin)
+        self.copies.arrive(C_YH, self.order[j], self.twins[j][6], self.spot.twin)
+
     def twin_far(self, j):
-        s, there, spot = self.order[j], self.twins[j], self.spot
-        self.copies.arrive(C_Y, s, there[1], spot.twin)
+        self.twin_side(j)
         if self.use_x:
-            self.copies.arrive(C_XH, s, there[5], spot.twin)
-            self.copies.arrive(C_YH, s, there[6], spot.twin)
+            self.twin_corner(j)
 
     def twin_all(self):
         for j in range(len(self.order)):
@@ -652,97 +686,230 @@
     return (s * 2 + yy) * 2 + cc
 
 
-def fetch_kernel(n_planes, axes, *refs):
+def plain_dot(a, b, contract):
+    return lax.dot_general(a, b, (contract, ((), ())), preferred_element_type=jnp.float32)
+
+
+ROWS_COLUMNS = ((1,), (0,))
+ROWS_ROWS = ((1,), (1,))
+COLUMNS_COLUMNS = ((0,), (0,))
+
+
+def turn(heads, cosine, sine):
+    return heads * cosine + pltpu.roll(heads, heads.shape[1] // 2, 1) * sine
+
+
+def front_kernel(n_planes, axes, *refs):
     n = len(axes)
-    ins, (tokens, small, grads), outs = refs[:n], refs[n : n + 3], refs[n + 3 : 2 * n + 3]
-    sequence, smalls, all_grads = refs[2 * n + 3 : 2 * n + 6]
-    send, recv, local, x_send, x_recv, g_send, g_recv = refs[2 * n + 6 :]
+    shards_in, (tokens, tile, grads, chosen, cosine, sine, allowed) = refs[:n], refs[n : n + 7]
+    outs = refs[n + 7 : 2 * n + 7]
+    (
+        all_grads, params, normed_one, query, key, value, probs, mixed, residual, normed_two, gates,
+    ) = refs[2 * n + 7 : 2 * n + 18]
+    (
+        wq, wk, wv, wo, sequence, pair, sent, received, w_send, w_recv, p_send, p_recv, g_send, g_recv, local,
+        load, x_send, x_recv,
+    ) = refs[2 * n + 18 :]
     spot = Spot(n_planes)
-
-    def views(s, yy, cc, xx, part):
+    x = spot.x
+    bf16, f32 = jnp.bfloat16, jnp.float32
+    own_rows, model = tokens.shape
+
+    def weight_views(s, yy, cc, xx, part):
         i = dp_of(s, yy, cc)
         places = []
-        for o, a, axis in zip(outs, ins, axes):
+        for o, a, axis in zip(outs, shards_in, axes):
             size = a.shape[axis]
             span = pl.ds(pl.multiple_of(i * size, size), size)
             places.append(o.at[span] if axis == 0 else o.at[:, span])
-        return places + [smalls.at[xx, i]]
-
-    sources = list(ins) + [small]
-    mine = views(spot.z, spot.y, spot.core, spot.x, ALL)
-    own = [pltpu.make_async_copy(a, v, local.at[i]) for i, (a, v) in enumerate(zip(sources, mine))]
-    own.append(pltpu.make_async_copy(tokens, sequence.at[spot.x], local.at[n + 1]))
-    own.append(pltpu.make_async_copy(grads, all_grads.at[spot.dp * 2 + spot.x], local.at[n + 2]))
-    half = grads.shape[0] // 2
+        return places
+
+    def param_views(s, yy, cc, xx, part):
+        size = tile.shape[1]
+        return [params.at[:, pl.ds(pl.multiple_of(dp_of(s, yy, cc) * size, size), size)]]
 
     def grad_views(s, yy, cc, xx, part):
         b = dp_of(s, yy, cc) * 2 + xx
         if part == ALL:
             return [all_grads.at[b]]
-        return [all_grads.at[b, pl.ds(0 if part == FIRST else half, half)]]
-
-    for c in own:
-        c.start()
-    spot.greet()
-
-    def across(i, src, dst):
+        return [all_grads.at[b, pl.ds(0 if part == FIRST else own_rows // 2, own_rows // 2)]]
+
+    def mine(views):
+        return views(spot.z, spot.y, spot.core, x, ALL)
+
+    def swap(i, src, dst):
         return pltpu.make_async_remote_copy(
             src_ref=src, dst_ref=dst, send_sem=x_send.at[i], recv_sem=x_recv.at[i],
             device_id=spot.across, device_id_type=MESH,
         )
 
-    across(0, tokens, sequence.at[spot.x]).start()
-    copies = Copies(n_planes, send, recv)
-    weights = Spread(spot, copies, sources, views, False)
-    gradients = Spread(spot, Copies(n_planes, g_send, g_recv), [grads], grad_views, True)
+    kept = list(zip(list(shards_in) + [tokens, grads, tile], mine(weight_views) + [sequence.at[x]] + mine(grad_views) + [pair.at[x]]))
+    kept = [pltpu.make_async_copy(a, b, local.at[i]) for i, (a, b) in enumerate(kept)]
+    for c in kept:
+        c.start()
+    spot.greet()
+    swaps = [swap(0, tile, pair.at[x]), swap(1, tokens, sequence.at[x]), swap(2, sent, received)]
+    swaps[0].start()
+    weights = Spread(spot, Copies(n_planes, w_send, w_recv), list(shards_in), weight_views, False)
+    small = Spread(spot, Copies(n_planes, p_send, p_recv), mine(param_views), param_views, False)
+    net = Spread(spot, Copies(n_planes, g_send, g_recv), [grads], grad_views, True)
     weights.begin()
-    gradients.begin()
-    for step in range(1, n_planes + 2):
+    swaps[1].start()
+    for c in kept:
+        c.wait()
+    swap(0, pair.at[1 - x], pair.at[1 - x]).wait_recv()
+    mine(param_views)[0][...] = pair[0] + pair[1]
+    small.begin()
+    net.onward_x(0)
+    net.onward_twin(0)
+    for step in range(1, n_planes + 1):
         weights.stage(step)
-        gradients.stage(step)
+        small.stage(step)
+        if step == n_planes - 1:
+            net.begin_z()
+    net.onward_y(0)
+    net.from_across(0)
+
+    def column(j):
+        net.relay(j)
+        net.onward_x(j)
+        net.onward_twin(j)
+
+    column(1)
+
+    small.twin_all()
+    swap(1, sequence.at[1 - x], sequence.at[1 - x]).wait_recv()
+
+    experts = chosen.shape[0]
+    first_gain = params[experts : experts + 1, :].astype(f32)
+    step = 32
+    for h in range(2):
+        for r in range(own_rows // step):
+            rows = sequence[h, pl.ds(r * step, step)].astype(f32)
+            scale = lax.rsqrt(jnp.mean(rows * rows, axis=1, keepdims=True) + norm_eps)
+            normed_one[pl.ds(h * own_rows + r * step, step)] = (rows * scale * first_gain).astype(bf16)
     weights.twin_all()
-    gradients.twin_all()
-    weights.copies.close()
-    gradients.copies.close()
-    for c in own:
+    loads = [pltpu.make_async_copy(a, b, load.at[i]) for i, (a, b) in enumerate(zip(outs, (wq, wk, wv, wo)))]
+    for c in loads:
+        c.start()
+    heads, head_dim = query.shape[1] // cosine.shape[1], cosine.shape[1]
+    kv_heads = key.shape[1] // head_dim
+    group = heads // kv_heads
+    for c in loads[:3]:
         c.wait()
-    across(1, smalls.at[spot.x], smalls.at[spot.x]).start()
-    across(0, tokens, sequence.at[spot.x]).wait_send()
-    across(1, smalls.at[spot.x], smalls.at[spot.x]).wait_send()
-    across(0, sequence.at[1 - spot.x], sequence.at[1 - spot.x]).wait_recv()
-    across(1, smalls.at[1 - spot.x], smalls.at[1 - spot.x]).wait_recv()
-
-
-def fetch(arrays, axes, tokens, small, grads, n_dp, collective_id):
+    cos, sin = cosine[...], sine[...]
+    raw = plain_dot(normed_one[...], wk[...], ROWS_COLUMNS)
+    for g in range(kv_heads):
+        span = slice(g * head_dim, (g + 1) * head_dim)
+        key[:, span] = turn(raw[:, span], cos, sin).astype(bf16)
+    value[...] = plain_dot(normed_one[...], wv[...], ROWS_COLUMNS).astype(bf16)
+    raw = plain_dot(normed_one[...], wq[...], ROWS_COLUMNS)
+    for h in range(heads):
+        span = slice(h * head_dim, (h + 1) * head_dim)
+        query[:, span] = turn(raw[:, span], cos, sin).astype(bf16)
+    net.from_side(0)
+    net.onward_y(1)
+    column(2)
+    net.from_across(1)
+    may = allowed[...] > 0.0
+    for h in range(heads):
+        span = slice(h * head_dim, (h + 1) * head_dim)
+        shared = slice(h // group * head_dim, (h // group + 1) * head_dim)
+        scores = plain_dot(query[:, span], key[:, shared], ROWS_ROWS) * (head_dim ** -0.5)
+        scores = jnp.where(may, scores, neg_big)
+        weight = jnp.exp(scores - jnp.max(scores, axis=1, keepdims=True))
+        weight = weight / jnp.sum(weight, axis=1, keepdims=True)
+        probs[h] = weight
+        mixed[:, span] = plain_dot(weight.astype(bf16), value[:, shared], ROWS_COLUMNS).astype(bf16)
+    loads[3].wait()
+    other = mixed[pl.ds(pl.multiple_of((1 - x) * own_rows, own_rows), own_rows), :]
+    sent[...] = plain_dot(other, wo[...], ROWS_COLUMNS).astype(bf16)
+    swaps[2].start()
+    other = mixed[pl.ds(pl.multiple_of(x * own_rows, own_rows), own_rows), :]
+    residual[...] = plain_dot(other, wo[...], ROWS_COLUMNS)
+    net.from_side(1)
+    net.onward_y(2)
+    column(3)
+    net.from_across(2)
+    swap(2, received, received).wait_recv()
+    second_gain = params[experts + 1 : experts + 2, :].astype(f32)
+    for r in range(own_rows // step):
+        span = pl.ds(r * step, step)
+        rows = sequence[x, span].astype(f32) + (residual[span] + received[span].astype(f32))
+        residual[span] = rows
+        scale = lax.rsqrt(jnp.mean(rows * rows, axis=1, keepdims=True) + norm_eps)
+        normed_two[span] = (rows * scale * second_gain).astype(bf16)
+    logits = plain_dot(params[:experts, :], normed_two[...], ROWS_ROWS)
+    picked = chosen[...] > 0.0
+    top = jnp.max(jnp.where(picked, logits, neg_big), axis=0, keepdims=True)
+    weight = jnp.where(picked, jnp.exp(jnp.where(picked, logits - top, 0.0)), 0.0)
+    gates[...] = weight / jnp.sum(weight, axis=0, keepdims=True)
+
+    net.from_side(2)
+    net.from_across(3)
+    for j in range(n_planes):
+        net.twin_near(j)
+        if j < n_planes - 1:
+            net.twin_side(j)
+    for each in (weights, small, net):
+        each.copies.close()
+    for c in swaps:
+        c.wait_send()
+
+
+def front(arrays, axes, tokens, tile, grads, chosen, cosine, sine, allowed, n_dp, collective_id):
     n, n_planes = len(arrays), n_dp // 4
-    sems = (11 * n_planes, n + 1)
+    bf16, f32 = jnp.bfloat16, jnp.float32
+    shape = jax.ShapeDtypeStruct
 
     def whole(a, axis):
-        shape = list(a.shape)
-        shape[axis] *= n_dp
-        return jax.ShapeDtypeStruct(tuple(shape), a.dtype)
-
+        full = list(a.shape)
+        full[axis] *= n_dp
+        return shape(tuple(full), a.dtype)
+
+    own_rows, model = tokens.shape
+    seq = 2 * own_rows
+    experts = chosen.shape[0]
+    wide, narrow_ = arrays[0].shape[1], arrays[1].shape[1]
+    heads = wide // cosine.shape[1]
+    gathered = [whole(a, axis) for a, axis in zip(arrays, axes)]
+    vmem = pl.BlockSpec(memory_space=pltpu.VMEM)
+    dma = pltpu.SemaphoreType.DMA
     return pl.pallas_call(
-        functools.partial(fetch_kernel, n_planes, axes),
-        out_shape=[whole(a, axis) for a, axis in zip(arrays, axes)]
+        functools.partial(front_kernel, n_planes, axes),
+        out_shape=gathered
         + [
-            jax.ShapeDtypeStruct((2,) + tokens.shape, tokens.dtype),
-            jax.ShapeDtypeStruct((2, n_dp) + small.shape, small.dtype),
-            jax.ShapeDtypeStruct((2 * n_dp,) + grads.shape, grads.dtype),
+            shape((2 * n_dp,) + grads.shape, bf16),
+            shape((tile.shape[0], tile.shape[1] * n_dp), bf16),
+            shape((seq, model), bf16),
+            shape((seq, wide), bf16),
+            shape((seq, narrow_), bf16),
+            shape((seq, narrow_), bf16),
+            shape((heads, seq, seq), f32),
+            shape((seq, wide), bf16),
+            shape((own_rows, model), f32),
+            shape((own_rows, model), bf16),
+            shape((experts, own_rows), f32),
         ],
-        in_specs=[ANY] * (n + 3),
-        out_specs=[ANY] * (n + 3),
-        scratch_shapes=[
-            pltpu.SemaphoreType.DMA(sems),
-            pltpu.SemaphoreType.DMA(sems),
-            pltpu.SemaphoreType.DMA((n + 3,)),
-            pltpu.SemaphoreType.DMA((2,)),
-            pltpu.SemaphoreType.DMA((2,)),
-            pltpu.SemaphoreType.DMA((11 * n_planes, 1)),
-            pltpu.SemaphoreType.DMA((11 * n_planes, 1)),
-        ],
-        compiler_params=pltpu.CompilerParams(collective_id=collective_id, has_side_effects=True),
-    )(*arrays, tokens, small, grads)
+        in_specs=[ANY] * (n + 3) + [vmem] * 4,
+        out_specs=[ANY] * (n + 1) + [vmem] * 10,
+        scratch_shapes=[pltpu.VMEM(g.shape, bf16) for g in gathered]
+        + [
+            pltpu.VMEM((2, own_rows, model), bf16),
+            pltpu.VMEM((2,) + tile.shape, bf16),
+            pltpu.VMEM((own_rows, model), bf16),
+            pltpu.VMEM((own_rows, model), bf16),
+        ]
+        + [dma((11 * n_planes, n))] * 2
+        + [dma((11 * n_planes, 1))] * 4
+        + [dma((n + 3,)), dma((n,)), dma((3,)), dma((3,))],
+        compiler_params=pltpu.CompilerParams(
+            collective_id=collective_id, has_side_effects=True, vmem_limit_bytes=56 << 20
+        ),
+        cost_estimate=pl.CostEstimate(
+            flops=6 * seq * model * wide, bytes_accessed=16 * n_dp * own_rows * model, transcendentals=heads * seq * seq
+        ),
+    )(*arrays, tokens, tile, grads, chosen, cosine, sine, allowed)
 
 
 (T_YX, T_Y, T_X, T_OWN, R_XHALF, R_YHALF, R_YALL, R_XALL, R_UP, R_DOWN) = range(10)
@@ -765,67 +932,70 @@
 
 class Reduce:
     @staticmethod
-    def scratch(shapes, dtypes, n_planes, use_x):
-        n = len(shapes)
+    def scratch(shapes, dtypes, n_planes, use_x, cut=0, direct=False):
         kinds = 4 if use_x else 2
         out = []
         for i, (shape, dtype) in enumerate(zip(shapes, dtypes)):
-            half = (shape[0] // 2, shape[1]) if i == 0 else shape
+            rows = cut if i == 0 else shape[0]
             out.append(pltpu.VMEM((kinds, n_planes) + shape, dtype))
-            out.append(pltpu.VMEM((kinds, n_planes) + shape, dtype))
+            out.append(pltpu.VMEM((n_planes + 1,) + shape, dtype))
             out.append(pltpu.VMEM((n_planes,) + shape, dtype))
-            out.append(pltpu.VMEM((n_planes,) + shape, dtype))
-            out.append(pltpu.VMEM((n_planes,) + shape, dtype))
+            if not direct:
+                out.append(pltpu.VMEM((kinds, 2) + shape, dtype))
             if use_x:
                 out.append(pltpu.VMEM((n_planes,) + shape, dtype))
-                out.append(pltpu.VMEM((n_planes,) + half, dtype))
-                out.append(pltpu.VMEM((n_planes,) + (half if i == 0 else (8, 128)), dtype))
-        sems = (10 * n_planes, n)
-        out.append(pltpu.SemaphoreType.DMA(sems))
-        out.append(pltpu.SemaphoreType.DMA(sems))
+                out.append(pltpu.VMEM((n_planes, rows) + shape[1:], dtype))
+                if i == 0 and cut < shape[0]:
+                    out.append(pltpu.VMEM((n_planes, shape[0] - cut) + shape[1:], dtype))
+        n = len(shapes)
+        out.append(pltpu.SemaphoreType.DMA((10 * n_planes, n)))
+        out.append(pltpu.SemaphoreType.DMA((10 * n_planes, n)))
         out.append(pltpu.SemaphoreType.DMA((kinds * n_planes, n)))
         return out
 
-    @staticmethod
-    def n_scratch(n, use_x):
-        return n * (8 if use_x else 5) + 3
-
-    def __init__(self, spot, blocks, outs, scratch, use_x):
-        self.spot, self.outs, self.use_x = spot, outs, use_x
-        self.n, self.n_planes = len(outs), spot.n_planes
-        per = 8 if use_x else 5
-        send, recv, self.local = scratch[self.n * per :]
-        sets = [scratch[i * per : (i + 1) * per] for i in range(self.n)]
-        self.mine = [s[0] for s in sets]
-        self.twin = [s[1] for s in sets]
-        self.above = [s[2] for s in sets]
-        self.below = [s[3] for s in sets]
-        self.near = [s[4] for s in sets]
-        self.across = [s[5] for s in sets] if use_x else None
-        self.first = [s[6] for s in sets] if use_x else None
-        self.second = sets[0][7] if use_x else None
-        self.half = sets[0][0].shape[2] // 2
+    def __init__(self, spot, blocks, outs, scratch, use_x, cut=0, direct=False):
+        self.spot, self.outs, self.use_x, self.direct = spot, outs, use_x, direct
+        self.n, self.n_planes, self.cut = len(outs), spot.n_planes, cut
+        left = list(scratch)
+        self.twin, self.line, self.near, self.ring, self.across, self.first = [], [], [], [], [], []
+        self.second = None
+        for i in range(self.n):
+            self.twin.append(left.pop(0))
+            self.line.append(left.pop(0))
+            self.near.append(left.pop(0))
+            if not direct:
+                self.ring.append(left.pop(0))
+            if use_x:
+                self.across.append(left.pop(0))
+                self.first.append(left.pop(0))
+                if i == 0 and cut < self.near[0].shape[1]:
+                    self.second = left.pop(0)
+        send, recv, self.local = left
         self.copies = Copies(self.n_planes, send, recv)
         y, x, core = spot.y, spot.x, spot.core
         self.order = spot.far_first()
         places = {T_YX: (1 - y, 1 - x), T_Y: (1 - y, x), T_X: (y, 1 - x), T_OWN: (y, x)}
         self.kinds = [T_YX, T_Y, T_X, T_OWN] if use_x else [T_Y, T_OWN]
-        self.terms = {(k, j): blocks(s, places[k][0], core, places[k][1]) for k in self.kinds for j, s in enumerate(self.order)}
-        self.others = {(k, j): blocks(s, places[k][0], 1 - core, places[k][1]) for k in self.kinds for j, s in enumerate(self.order)}
+        every = [(k, j) for j in range(self.n_planes) for k in self.kinds]
+        self.terms = {(k, j): blocks(self.order[j], places[k][0], core, places[k][1]) for k, j in every}
+        self.others = {(k, j): blocks(self.order[j], places[k][0], 1 - core, places[k][1]) for k, j in every}
 
     def load(self, kind, j):
-        k = self.kinds.index(kind)
-        s = self.order[j]
+        k, s = self.kinds.index(kind), self.order[j]
         return [
-            pltpu.make_async_copy(ref, self.mine[i].at[k, s], self.local.at[k * self.n_planes + s, i])
+            pltpu.make_async_copy(ref, self.ring[i].at[k, j % 2], self.local.at[k * self.n_planes + s, i])
             for i, ref in enumerate(self.terms[kind, j])
         ]
 
+    def start_load(self, kind, j):
+        if not self.direct and j < self.n_planes:
+            for c in self.load(kind, j):
+                c.start()
+
     def start_loads(self):
-        for j in range(self.n_planes):
+        for j in range(2):
             for kind in self.kinds:
-                for c in self.load(kind, j):
-                    c.start()
+                self.start_load(kind, j)
 
     def start_twins(self):
         for j in range(self.n_planes):
@@ -835,53 +1005,60 @@
 
     def ready(self, kind, j):
         k, s = self.kinds.index(kind), self.order[j]
+        twin = [t.at[k, s] for t in self.twin]
+        self.copies.arrive(kind, s, twin, self.spot.twin)
+        if self.direct:
+            return twin, self.terms[kind, j]
         for c in self.load(kind, j):
             c.wait()
-        self.copies.arrive(kind, s, [t.at[k, s] for t in self.twin], self.spot.twin)
-        return [m.at[k, s] for m in self.mine], [t.at[k, s] for t in self.twin]
+        return twin, [r.at[k, j % 2] for r in self.ring]
 
     def corner(self, j):
         if not self.use_x or not 0 <= j < self.n_planes:
             return
-        s, half = self.order[j], self.half
-        mine, twin = self.ready(T_YX, j)
+        s, cut = self.order[j], self.cut
+        twin, mine = self.ready(T_YX, j)
         for m, t in zip(mine, twin):
-            add_up(m, [m, t])
-        head = [mine[0].at[pl.ds(0, half)]] + mine[1:]
+            add_up(t, [m, t])
+        self.start_load(T_YX, j + 2)
+        head = twin if self.second is None else [twin[0].at[pl.ds(0, cut)]] + twin[1:]
         self.copies.start(None, R_XHALF, s, head, [f.at[s] for f in self.first], self.spot.across)
-        tail = [mine[0].at[pl.ds(half, half)]]
-        self.copies.start(None, R_YHALF, s, tail, [self.second.at[s]], self.spot.side)
+        if self.second is not None:
+            tail = [twin[0].at[pl.ds(cut, self.second.shape[1])]]
+            self.copies.start(None, R_YHALF, s, tail, [self.second.at[s]], self.spot.side)
 
     def side(self, j):
-        s, half = self.order[j], self.half
-        mine, twin = self.ready(T_Y, j)
+        s, cut = self.order[j], self.cut
+        twin, mine = self.ready(T_Y, j)
         if self.use_x:
             first = [f.at[s] for f in self.first]
             self.copies.arrive(R_XHALF, s, first, self.spot.across)
         for i, (m, t) in enumerate(zip(mine, twin)):
             if not self.use_x:
-                add_up(m, [m, t])
-            elif i == 0:
-                a, b = pl.ds(0, half), pl.ds(half, half)
-                add_up(m.at[a], [m.at[a], t.at[a], first[0]])
-                add_up(m.at[b], [m.at[b], t.at[b]])
+                add_up(t, [m, t])
+            elif i == 0 and self.second is not None:
+                a, b = pl.ds(0, cut), pl.ds(cut, self.second.shape[1])
+                add_up(t.at[a], [m.at[a], t.at[a], first[0]])
+                add_up(t.at[b], [m.at[b], t.at[b]])
             else:
-                add_up(m, [m, t, first[i]])
-        self.copies.start(None, R_YALL, s, mine, [t.at[s] for t in self.near], self.spot.side)
+                add_up(t, [m, t, first[i]])
+        self.start_load(T_Y, j + 2)
+        self.copies.start(None, R_YALL, s, twin, [t.at[s] for t in self.near], self.spot.side)
 
     def over(self, j):
-        s, half = self.order[j], self.half
-        mine, twin = self.ready(T_X, j)
-        second = self.second.at[s]
-        self.copies.arrive(R_YHALF, s, [second], self.spot.side)
+        s, cut = self.order[j], self.cut
+        twin, mine = self.ready(T_X, j)
+        if self.second is not None:
+            self.copies.arrive(R_YHALF, s, [self.second.at[s]], self.spot.side)
         for i, (m, t) in enumerate(zip(mine, twin)):
-            if i == 0:
-                a, b = pl.ds(0, half), pl.ds(half, half)
-                add_up(m.at[a], [m.at[a], t.at[a]])
-                add_up(m.at[b], [m.at[b], t.at[b], second])
+            if i == 0 and self.second is not None:
+                a, b = pl.ds(0, cut), pl.ds(cut, self.second.shape[1])
+                add_up(t.at[a], [m.at[a], t.at[a]])
+                add_up(t.at[b], [m.at[b], t.at[b], self.second.at[s]])
             else:
-                add_up(m, [m, t])
-        self.copies.start(None, R_XALL, s, mine, [t.at[s] for t in self.across], self.spot.across)
+                add_up(t, [m, t])
+        self.start_load(T_X, j + 2)
+        self.copies.start(None, R_XALL, s, twin, [t.at[s] for t in self.across], self.spot.across)
 
     def sides(self, j):
         if 0 <= j < self.n_planes:
@@ -893,7 +1070,7 @@
         if not 0 <= j < self.n_planes:
             return
         s, spot, copies, n = self.order[j], self.spot, self.copies, self.n
-        mine, twin = self.ready(T_OWN, j)
+        twin, mine = self.ready(T_OWN, j)
         near = [t.at[s] for t in self.near]
         copies.arrive(R_YALL, s, near, spot.side)
         here = [[m, t, a] for m, t, a in zip(mine, twin, near)]
@@ -901,32 +1078,38 @@
             across = [t.at[s] for t in self.across]
             copies.arrive(R_XALL, s, across, spot.across)
             here = [h + [a] for h, a in zip(here, across)]
-        above = [t.at[s] for t in self.above]
-        below = [t.at[s] for t in self.below]
+        line = [t.at[s] for t in self.line]
 
         def add_all(targets, *more):
             for i in range(n):
                 add_up(targets[i], here[i] + [m[i] for m in more])
 
         if j == self.n_planes - 1:
-            when(spot.has_up, lambda: copies.arrive(R_DOWN, s, above, spot.up))
+            below = [t.at[self.n_planes] for t in self.line]
+            when(spot.has_up, lambda: copies.arrive(R_DOWN, s, line, spot.up))
             when(spot.has_down, lambda: copies.arrive(R_UP, s, below, spot.down))
-            when(spot.has_up & spot.has_down, lambda: add_all(self.outs, above, below))
-            when(spot.z == 0, lambda: add_all(self.outs, above))
+            when(spot.has_up & spot.has_down, lambda: add_all(self.outs, line, below))
+            when(spot.z == 0, lambda: add_all(self.outs, line))
             when(spot.z == self.n_planes - 1, lambda: add_all(self.outs, below))
             return
-        for goes, more, group, buffers, device, source in (
-            (s < spot.z, spot.has_up, R_DOWN, above, spot.down, spot.up),
-            (s > spot.z, spot.has_down, R_UP, below, spot.up, spot.down),
+        for goes, more, group, last, device, source in (
+            (s < spot.z, spot.has_up, R_DOWN, None, spot.down, spot.up),
+            (s > spot.z, spot.has_down, R_UP, s - spot.z == 1, spot.up, spot.down),
         ):
 
             def partial():
-                copies.arrive(group, s, buffers, source)
-                add_all(mine, buffers)
+                copies.arrive(group, s, line, source)
+                add_all(twin, line)
 
             when(goes & more, partial)
-            when(goes & jnp.logical_not(more), lambda: add_all(mine))
-            copies.start(goes, group, s, mine, buffers, device)
+            when(goes & jnp.logical_not(more), lambda: add_all(twin))
+            if last is None:
+                copies.start(goes, group, s, twin, line, device)
+            else:
+                below = [t.at[self.n_planes] for t in self.line]
+                copies.start(goes & last, group, s, twin, below, device)
+                copies.start(goes & jnp.logical_not(last), group, s, twin, line, device)
+        self.start_load(T_OWN, j + 2)
 
     def stage(self, step):
         self.corner(step)
@@ -937,108 +1120,399 @@
         self.copies.close()
 
 
+class WeightGradients:
+    width = 256
+
+    def __init__(self, ins, outs, scratch):
+        self.sources, (self.hidden, self.shared) = ins[:4], ins[4:]
+        self.outs = outs
+        self.buffers, self.small_hidden, self.small_shared = scratch[:4], scratch[4], scratch[5]
+        self.tall, self.flat, self.sums, self.load, self.store, self.once = scratch[6:]
+        self.n_parts = self.sources[0].shape[1] // self.width
+
+    @staticmethod
+    def scratch(rows, tokens, width, shared):
+        bf16, f32 = jnp.bfloat16, jnp.float32
+        w = WeightGradients.width
+        return [
+            pltpu.VMEM((2, rows, w), bf16),
+            pltpu.VMEM((2, rows, w), bf16),
+            pltpu.VMEM((2, tokens, w), bf16),
+            pltpu.VMEM((2, tokens, w), bf16),
+            pltpu.VMEM((3, rows, width), bf16),
+            pltpu.VMEM((tokens, shared), bf16),
+            pltpu.VMEM((2, 2, w, width), f32),
+            pltpu.VMEM((2, width, w), f32),
+            pltpu.VMEM((2, shared, w), bf16),
+            pltpu.SemaphoreType.DMA((2, 4)),
+            pltpu.SemaphoreType.DMA((2, 4)),
+            pltpu.SemaphoreType.DMA((2,)),
+        ]
+
+    def span(self, p):
+        return pl.ds(p * self.width, self.width)
+
+    def loads(self, p):
+        return [
+            pltpu.make_async_copy(a.at[:, self.span(p)], b.at[p % 2], self.load.at[p % 2, i])
+            for i, (a, b) in enumerate(zip(self.sources, self.buffers))
+        ]
+
+    def stores(self, p):
+        gate, up, down, shared = self.outs
+        slot, span = p % 2, self.span(p)
+        pairs = [
+            (self.tall.at[slot, 0], gate.at[span]),
+            (self.tall.at[slot, 1], up.at[span]),
+            (self.flat.at[slot], down.at[:, span]),
+            (self.sums.at[slot], shared.at[:, span]),
+        ]
+        return [pltpu.make_async_copy(a, b, self.store.at[slot, i]) for i, (a, b) in enumerate(pairs)]
+
+    def resident(self):
+        return [
+            pltpu.make_async_copy(self.hidden, self.small_hidden, self.once.at[0]),
+            pltpu.make_async_copy(self.shared, self.small_shared, self.once.at[1]),
+        ]
+
+    def begin(self):
+        for c in self.resident() + self.loads(0):
+            c.start()
+
+    def part(self, p):
+        if p >= self.n_parts:
+            return
+        if p == 0:
+            for c in self.resident():
+                c.wait()
+        if p + 1 < self.n_parts:
+            for c in self.loads(p + 1):
+                c.start()
+        for c in self.loads(p):
+            c.wait()
+        if p >= 2:
+            for c in self.stores(p - 2):
+                c.wait()
+        slot = p % 2
+        rows, grad_rows, tokens, grads = [b.at[slot] for b in self.buffers]
+
+        def across(a, b):
+            return lax.dot_general(a, b, (((0,), (0,)), ((), ())), preferred_element_type=jnp.float32)
+
+        self.tall[slot, 0] = across(rows[...], self.small_hidden[1])
+        self.tall[slot, 1] = across(rows[...], self.small_hidden[2])
+        self.flat[slot] = across(self.small_hidden[0], grad_rows[...])
+        n = self.small_shared.shape[1] // 3
+        self.sums[slot, pl.ds(0, 2 * n)] = across(self.small_shared[:, n:], tokens[...]).astype(jnp.bfloat16)
+        self.sums[slot, pl.ds(2 * n, n)] = across(self.small_shared[:, :n], grads[...]).astype(jnp.bfloat16)
+        for c in self.stores(p):
+            c.start()
+
+    def end(self):
+        for p in (self.n_parts - 2, self.n_parts - 1):
+            for c in self.stores(p):
+                c.wait()
+
+
 def sum_kernel(n_planes, n, *refs):
-    ins, outs, scratch = refs[:n], refs[n : 2 * n], refs[2 * n :]
+    ins, work_ins, outs, work_outs = refs[:n], refs[n : n + 6], refs[n + 6 : 2 * n + 6], refs[2 * n + 6 : 2 * n + 10]
+    scratch = refs[2 * n + 10 :]
+    cut = len(scratch) - 12
     spot = Spot(n_planes)
+    rows = ins[0].shape[1] // 2
 
     def blocks(s, yy, cc, xx):
         return [a.at[dp_of(s, yy, cc) * 2 + xx] for a in ins]
 
-    net = Reduce(spot, blocks, outs, scratch, True)
+    net = Reduce(spot, blocks, outs, scratch[:cut], True, rows)
+    work = WeightGradients(work_ins, work_outs, scratch[cut:])
     net.start_loads()
     spot.greet()
     net.start_twins()
+    work.begin()
+    done = 0
     for step in range(n_planes + 2):
-        net.stage(step)
+        for action in (net.corner, net.sides, net.column):
+            j = step - (net.corner, net.sides, net.column).index(action)
+            action(j)
+            if 0 <= j < n_planes and done < work.n_parts:
+                work.part(done)
+                done += 1
     net.close()
-
-
-def sum_everywhere(arrays, out_dtypes, n_dp, collective_id):
+    work.end()
+
+
+def sum_everywhere(arrays, out_dtypes, work_arrays, n_dp, collective_id):
     n, n_planes = len(arrays), n_dp // 4
     shapes = [a.shape[1:] for a in arrays]
+    rows, model = work_arrays[0].shape
+    tokens = work_arrays[2].shape[0]
+    width = work_arrays[4].shape[2]
+    shared = work_arrays[5].shape[1]
     return pl.pallas_call(
         functools.partial(sum_kernel, n_planes, n),
-        out_shape=[jax.ShapeDtypeStruct(s, t) for s, t in zip(shapes, out_dtypes)],
-        in_specs=[ANY] * n,
-        out_specs=[pl.BlockSpec(memory_space=pltpu.VMEM)] * n,
-        scratch_shapes=Reduce.scratch(shapes, [a.dtype for a in arrays], n_planes, True),
+        out_shape=[jax.ShapeDtypeStruct(s, t) for s, t in zip(shapes, out_dtypes)]
+        + [
+            jax.ShapeDtypeStruct((model, width), jnp.float32),
+            jax.ShapeDtypeStruct((model, width), jnp.float32),
+            jax.ShapeDtypeStruct((width, model), jnp.float32),
+            jax.ShapeDtypeStruct((shared, model), jnp.bfloat16),
+        ],
+        in_specs=[ANY] * (n + 6),
+        out_specs=[pl.BlockSpec(memory_space=pltpu.VMEM)] * n + [ANY] * 4,
+        scratch_shapes=Reduce.scratch(shapes, [a.dtype for a in arrays], n_planes, True, shapes[0][0] // 2)
+        + WeightGradients.scratch(rows, tokens, width, shared),
         compiler_params=pltpu.CompilerParams(
-            collective_id=collective_id, has_side_effects=True, vmem_limit_bytes=56 << 20
+            collective_id=collective_id, has_side_effects=True, vmem_limit_bytes=62 << 20
         ),
-    )(*arrays)
-
-
-def return_kernel(n_planes, axes, *refs):
+    )(*arrays, *work_arrays)
+
+
+def back_kernel(n_planes, axes, *refs):
     n = len(axes)
-    ins, parts, outs, out_sum = refs[:n], refs[n], refs[n + 1 : 2 * n + 1], refs[2 * n + 1]
-    scratch, (tile_sum, tile_in, x_send, x_recv) = refs[2 * n + 2 : -4], refs[-4:]
+    (
+        grad_own, mixed, normed_one, query, key, value, probs, wq, wk, wv, wo, cosine, sine, tokens, grad_residual,
+        gain, small, parts,
+    ) = refs[:18]
+    outs, grad_tokens, small_out, out_sum = refs[18 : 18 + n], *refs[18 + n : 21 + n]
+    (
+        grad_attn, grad_mixed, grad_query, grad_key, grad_value, gq, gk, gv, go, some_p, some_o, some_q, some_k,
+        some_v, sent, received, terms, small_sum, small_in, load, x_send, x_recv,
+    ) = refs[21 + n : 43 + n]
+    scratch = refs[43 + n :]
     spot = Spot(n_planes)
-
-    def blocks(s, yy, cc, xx):
+    x = spot.x
+    bf16, f32 = jnp.bfloat16, jnp.float32
+    own_rows, model = tokens.shape
+    grads = (gq, gk, gv, go)
+
+    def weight_blocks(s, yy, cc, xx):
         i = dp_of(s, yy, cc)
         places = []
-        for j, (a, o, axis) in enumerate(zip(ins, outs, axes)):
-            size = o.shape[axis] * (2 if j == n - 1 else 1)
+        for a, o, axis in zip(grads, outs, axes):
+            size = o.shape[axis]
             span = pl.ds(pl.multiple_of(i * size, size), size)
             places.append(a.at[span] if axis == 0 else a.at[:, span])
         return places
 
-    cut = Reduce.n_scratch(n, False)
-    weights = Reduce(spot, blocks, list(outs[:-1]) + [tile_sum], scratch[:cut], False)
-    tokens = Reduce(
-        spot, lambda s, yy, cc, xx: [parts.at[dp_of(s, yy, cc) * 2 + xx]], [out_sum], scratch[cut:], True
-    )
-    weights.start_loads()
-    tokens.start_loads()
+    def small_blocks(s, yy, cc, xx):
+        size = small_sum.shape[1]
+        return [terms.at[:, pl.ds(pl.multiple_of(dp_of(s, yy, cc) * size, size), size)]]
+
+    def token_blocks(s, yy, cc, xx):
+        return [parts.at[dp_of(s, yy, cc) * 2 + xx]]
+
+    count = 3 * n + 3
+    weights = Reduce(spot, weight_blocks, outs, scratch[:count], False, direct=True)
+    params = Reduce(spot, small_blocks, [small_sum], scratch[count : count + 6], False, direct=True)
+    sums = Reduce(spot, token_blocks, [out_sum], scratch[count + 6 :], True, own_rows)
+
+    def swap(i, src, dst):
+        return pltpu.make_async_remote_copy(
+            src_ref=src, dst_ref=dst, send_sem=x_send.at[i], recv_sem=x_recv.at[i],
+            device_id=spot.across, device_id_type=MESH,
+        )
+
+    own = pltpu.make_async_copy(grad_own, grad_attn.at[x], load.at[4, 0])
+    own.start()
+    sums.start_loads()
     spot.greet()
+    swap(0, grad_own, grad_attn.at[x]).start()
+    sums.start_twins()
+    terms[...] = small[...]
+
+    heads, head_dim = probs.shape[0], cosine.shape[1]
+    kv_heads = key.shape[1] // head_dim
+    group = heads // kv_heads
+    chunk = some_o.shape[1]
+    n_chunks = wo.shape[0] // chunk
+    per_chunk = chunk // head_dim
+
+    def load_o(c):
+        return pltpu.make_async_copy(wo.at[pl.ds(c * chunk, chunk)], some_o.at[c % 2], load.at[0, c % 2])
+
+    def load_p(h):
+        return pltpu.make_async_copy(probs.at[h], some_p.at[h % 2], load.at[1, h % 2])
+
+    load_o(0).start()
+    load_p(0).start()
+    sums.corner(0)
+    sums.sides(0)
+    own.wait()
+    swap(0, grad_attn.at[1 - x], grad_attn.at[1 - x]).wait_recv()
+    whole = grad_attn[...].reshape(2 * own_rows, model)
+    cos, sin = cosine[...], -sine[...]
+    scale = head_dim ** -0.5
+    for c in range(n_chunks):
+        if c + 1 < n_chunks:
+            load_o(c + 1).start()
+        load_o(c).wait()
+        span = slice(c * chunk, (c + 1) * chunk)
+        grad_mixed[:, span] = plain_dot(whole, some_o[c % 2], ROWS_ROWS).astype(bf16)
+        go[span, :] = plain_dot(mixed[:, span], whole, COLUMNS_COLUMNS).astype(bf16)
+    sums.corner(1)
+    sums.sides(1)
+    for h in range(heads):
+        if h + 1 < heads:
+            load_p(h + 1).start()
+        load_p(h).wait()
+        span = slice(h * head_dim, (h + 1) * head_dim)
+        shared = slice(h // group * head_dim, (h // group + 1) * head_dim)
+        weight, back = some_p[h % 2], grad_mixed[:, span]
+        grad_v = plain_dot(weight.astype(bf16), back, COLUMNS_COLUMNS)
+        grad_p = plain_dot(back, value[:, shared], ROWS_ROWS)
+        inner = jnp.sum(weight * grad_p, axis=1, keepdims=True)
+        grad_s = (weight * (grad_p - inner)).astype(bf16)
+        grad_q = plain_dot(grad_s, key[:, shared], ROWS_COLUMNS) * scale
+        grad_query[:, span] = turn(grad_q, cos, sin).astype(bf16)
+        grad_k = plain_dot(grad_s, query[:, span], COLUMNS_COLUMNS) * scale
+        if h % group == 0:
+            total_k, total_v = grad_k, grad_v
+        else:
+            total_k, total_v = total_k + grad_k, total_v + grad_v
+        if h % group == group - 1:
+            grad_key[:, shared] = turn(total_k, cos, sin).astype(bf16)
+            grad_value[:, shared] = total_v.astype(bf16)
+    for target, source in ((gk, grad_key), (gv, grad_value), (gq, grad_query)):
+        target[...] = plain_dot(normed_one[...], source[...], COLUMNS_COLUMNS).astype(bf16)
     weights.start_twins()
-    tokens.start_twins()
-    for step in range(n_planes + 2):
-        weights.sides(step)
-        tokens.corner(step)
-        tokens.sides(step - 1)
-        weights.column(step - 1)
-        tokens.column(step - 2)
-    rows = tile_in.shape[0]
-    swap = pltpu.make_async_remote_copy(
-        src_ref=tile_sum.at[pl.ds(pl.multiple_of((1 - spot.x) * rows, rows), rows)], dst_ref=tile_in,
-        send_sem=x_send, recv_sem=x_recv, device_id=spot.across, device_id_type=MESH,
-    )
-    swap.start()
-    swap.wait()
-    outs[-1][...] = tile_sum[pl.ds(pl.multiple_of(spot.x * rows, rows), rows), :] + tile_in[...]
-    weights.close()
-    tokens.close()
-
-
-def sum_back(arrays, axes, parts, n_dp, collective_id):
-    n, n_planes = len(arrays), n_dp // 4
+
+    rows = some_q.shape[1]
+    n_chunks = model // rows
+
+    def load_w(c):
+        span = pl.ds(c * rows, rows)
+        return [
+            pltpu.make_async_copy(w.at[span], b.at[c % 2], load.at[i, c % 2])
+            for i, (w, b) in ((0, (wq, some_q)), (2, (wk, some_k)), (3, (wv, some_v)))
+        ]
+
+    for c in load_w(0):
+        c.start()
+    sums.column(0)
+    sums.corner(2)
+    sums.sides(2)
+    weights.sides(0)
+    other = pl.ds(pl.multiple_of((1 - x) * own_rows, own_rows), own_rows)
+    mine = pl.ds(pl.multiple_of(x * own_rows, own_rows), own_rows)
+    for c in range(n_chunks):
+        if c + 1 < n_chunks:
+            for each in load_w(c + 1):
+                each.start()
+        for each in load_w(c):
+            each.wait()
+        columns = slice(c * rows, (c + 1) * rows)
+        for here, target in ((other, sent), (mine, grad_tokens)):
+            total = plain_dot(grad_query[here, :], some_q[c % 2], ROWS_ROWS)
+            total = total + plain_dot(grad_key[here, :], some_k[c % 2], ROWS_ROWS)
+            total = total + plain_dot(grad_value[here, :], some_v[c % 2], ROWS_ROWS)
+            target[:, columns] = total.astype(target.dtype)
+    swap(1, sent, received).start()
+    sums.column(1)
+    sums.corner(3)
+    sums.sides(3)
+    weights.sides(1)
+    swap(1, received, received).wait_recv()
+    step = 32
+    gain_row = gain[...].astype(f32)
+    total = jnp.zeros((1, model), f32)
+    for r in range(own_rows // step):
+        span = pl.ds(r * step, step)
+        rows_in = tokens[span, :].astype(f32)
+        grad = grad_tokens[span, :] + received[span, :].astype(f32)
+        size = lax.rsqrt(jnp.mean(rows_in * rows_in, axis=1, keepdims=True) + norm_eps)
+        weighted = grad * gain_row
+        inner = jnp.mean(rows_in * weighted, axis=1, keepdims=True)
+        total = total + jnp.sum(grad * rows_in * size, axis=0, keepdims=True)
+        grad_tokens[span, :] = size * weighted - rows_in * (size * size * size) * inner + grad_residual[span, :]
+    place = small.shape[0] - 8
+    terms[pl.ds(place, 1), :] = total
+    params.start_twins()
+    sums.column(2)
+    weights.column(0)
+    weights.sides(2)
+    params.sides(0)
+    sums.column(3)
+    weights.column(1)
+    weights.sides(3)
+    for j in range(1, n_planes):
+        params.sides(j)
+        params.column(j - 1)
+    weights.column(2)
+    params.column(n_planes - 1)
+    weights.column(3)
+    swap(2, small_sum, small_in).start()
+    swap(2, small_sum, small_in).wait()
+    small_out[...] = small_sum[...] + small_in[...]
+    swap(0, grad_own, grad_attn.at[x]).wait_send()
+    swap(1, sent, received).wait_send()
+    for each in (weights, params, sums):
+        each.close()
+
+
+def backward(
+    grad_own, mixed, normed_one, query, key, value, probs, weights, axes, cosine, sine, tokens, grad_residual, gain,
+    small, parts, n_dp, collective_id,
+):
+    n, n_planes = len(weights), n_dp // 4
+    bf16, f32 = jnp.bfloat16, jnp.float32
+    shape, vmem_ref = jax.ShapeDtypeStruct, pltpu.VMEM
+    own_rows, model = tokens.shape
+    seq = 2 * own_rows
+    wide, narrow_ = query.shape[1], key.shape[1]
 
     def part(a, axis):
-        shape = list(a.shape)
-        shape[axis] //= n_dp
-        return tuple(shape)
-
-    shapes = [part(a, axis) for a, axis in zip(arrays, axes)]
-    tile = (shapes[-1][0] // 2, shapes[-1][1])
+        some = list(a.shape)
+        some[axis] //= n_dp
+        return tuple(some)
+
+    shapes = [part(a, axis) for a, axis in zip(weights, axes)]
+    tile = (small.shape[0], model // n_dp)
     block = parts.shape[1:]
+    vmem = pl.BlockSpec(memory_space=pltpu.VMEM)
+    dma = pltpu.SemaphoreType.DMA
+    chunk = 256
     return pl.pallas_call(
-        functools.partial(return_kernel, n_planes, axes),
-        out_shape=[jax.ShapeDtypeStruct(s, jnp.float32) for s in shapes[:-1] + [tile, block]],
-        in_specs=[ANY] * (n + 1),
-        out_specs=[pl.BlockSpec(memory_space=pltpu.VMEM)] * (n + 1),
-        scratch_shapes=Reduce.scratch(shapes, [a.dtype for a in arrays], n_planes, False)
-        + Reduce.scratch([block], [parts.dtype], n_planes, True)
+        functools.partial(back_kernel, n_planes, axes),
+        out_shape=[shape(s, f32) for s in shapes] + [shape((own_rows, model), f32), shape(tile, f32), shape(block, f32)],
+        in_specs=[ANY] + [vmem] * 5 + [ANY] * 5 + [vmem] * 6 + [ANY],
+        out_specs=[vmem] * (n + 3),
+        scratch_shapes=[
+            vmem_ref((2, own_rows, model), bf16),
+            vmem_ref((seq, wide), bf16),
+            vmem_ref((seq, wide), bf16),
+            vmem_ref((seq, narrow_), bf16),
+            vmem_ref((seq, narrow_), bf16),
+        ]
+        + [vmem_ref(w.shape, bf16) for w in weights]
         + [
-            pltpu.VMEM(shapes[-1], jnp.float32),
-            pltpu.VMEM(tile, jnp.float32),
-            pltpu.SemaphoreType.DMA(()),
-            pltpu.SemaphoreType.DMA(()),
-        ],
+            vmem_ref((2,) + probs.shape[1:], f32),
+            vmem_ref((2, chunk, model), bf16),
+            vmem_ref((2, chunk, wide), bf16),
+            vmem_ref((2, chunk, narrow_), bf16),
+            vmem_ref((2, chunk, narrow_), bf16),
+            vmem_ref((own_rows, model), bf16),
+            vmem_ref((own_rows, model), bf16),
+            vmem_ref(small.shape, f32),
+            vmem_ref(tile, f32),
+            vmem_ref(tile, f32),
+            dma((5, 2)),
+            dma((3,)),
+            dma((3,)),
+        ]
+        + Reduce.scratch(shapes, [bf16] * n, n_planes, False, direct=True)
+        + Reduce.scratch([tile], [f32], n_planes, False, direct=True)
+        + Reduce.scratch([block], [parts.dtype], n_planes, True, block[0]),
         compiler_params=pltpu.CompilerParams(
-            collective_id=collective_id, has_side_effects=True, vmem_limit_bytes=60 << 20
+            collective_id=collective_id, has_side_effects=True, vmem_limit_bytes=63 << 20
         ),
-    )(*arrays, parts)
+        cost_estimate=pl.CostEstimate(
+            flops=12 * seq * model * wide, bytes_accessed=16 * n_dp * own_rows * model, transcendentals=0
+        ),
+    )(
+        grad_own, mixed, normed_one, query, key, value, probs, *weights, cosine, sine, tokens, grad_residual, gain,
+        small, parts,
+    )
 UNIT = 2
 
 
@@ -1193,9 +1667,9 @@
 
 
 def expert_kernel(n_dp, *refs):
-    own, own_gates, grads, w_gate, w_up, w_down, shared = refs[:7]
-    normed, out_parts, back_parts, grad_gates, rows_out, grad_rows_out, hidden_out, shared_out = refs[7:15]
-    scratch, (gates, load, store, local, send, recv) = refs[15:-6], refs[-6:]
+    own, own_gates, _, w_gate, w_up, w_down, shared = refs[:7]
+    normed, grads, out_parts, back_parts, grad_gates, rows_out, grad_rows_out, hidden_out, shared_out = refs[7:16]
+    scratch, (gates, load, store, local, send, recv, g_send, g_recv) = refs[16:-8], refs[-8:]
     n_planes = n_dp // 4
     spot = Spot(n_planes)
     half = own.shape[0] // 2
@@ -1207,6 +1681,12 @@
         if part == FIRST:
             return [normed.at[b, pl.ds(0, half)], gates.at[b]]
         return [normed.at[b, pl.ds(half, half)]]
+
+    def grad_views(s, yy, cc, xx, part):
+        b = dp_of(s, yy, cc) * 2 + xx
+        if part == ALL:
+            return [grads.at[b]]
+        return [grads.at[b, pl.ds(0 if part == FIRST else half, half)]]
 
     kept = [
         pltpu.make_async_copy(a, v, local.at[i])
@@ -1217,6 +1697,7 @@
     spot.greet()
     copies = Copies(n_planes, send, recv)
     net = Spread(spot, copies, [own, own_gates], views, True)
+    rest = Spread(spot, Copies(n_planes, g_send, g_recv), None, grad_views, True)
     net.begin()
     work = ExpertWork(spot.dp, (w_gate, w_up, w_down, shared), scratch)
     work.prepare()
@@ -1254,7 +1735,8 @@
         return [pltpu.make_async_copy(a, b, store.at[slot, i]) for i, (a, b) in enumerate(pairs)]
 
     def load_unit(i):
-        loads(unit_of(jnp.int32(i)), i % 2)[0].start()
+        for c in loads(unit_of(jnp.int32(i)), i % 2):
+            c.start()
 
     def near(j):
         net.twin_near(j)
@@ -1262,10 +1744,16 @@
 
     def far(j):
         net.twin_far(j)
+        rest.twin_corner(j)
+        if j == n_planes - 1:
+            rest.twin_side(j)
         load_unit(2 * j + 1)
 
-    def on(j):
-        net.onward(j, net.mine[j][0])
+    def over(j):
+        if j == n_planes - 1:
+            rest.from_side(j)
+        rest.over_x(j)
+        rest.over_y(j)
 
     middle = spot.has_up & spot.has_down
     end = jnp.logical_not(middle)
@@ -1280,21 +1768,21 @@
         pl.when(middle if c else end)(functools.partial(net.relay, j, goes[j, c]))
 
     plan = {
-        (0, 0): [(on, 1)],
+        (0, 0): [(net.onward, 1)],
         (0, 1): [(net.corner, 0)],
-        (0, 2): [(far, 0)],
+        (0, 2): [(rest.corner, 0), (far, 0), (over, 1)],
         (0, 4): [(relay, 2, 0), (relay, 3, 1)],
         (1, 0): [(net.sides, 1)],
-        (1, 1): [(on, 2)],
+        (1, 1): [(net.onward, 2), (rest.onward_y, 3)],
         (1, 2): [(near, 1)],
-        (1, 3): [(net.corner, 1)],
-        (2, 0): [(far, 1)],
+        (1, 3): [(net.corner, 1), (rest.corner, 1)],
+        (2, 0): [(far, 1), (over, 2)],
         (2, 3): [(net.sides, 2), (relay, 3, 0)],
-        (2, 4): [(on, 3)],
-        (3, 0): [(near, 2)],
-        (3, 1): [(net.corner, 2)],
+        (2, 4): [(net.onward, 3)],
+        (3, 0): [(near, 2), (over, 3)],
+        (3, 1): [(net.corner, 2), (rest.corner, 2)],
         (4, 0): [(net.sides, 3), (far, 2)],
-        (4, 3): [(net.corner, 3)],
+        (4, 3): [(net.corner, 3), (rest.corner, 3)],
         (5, 0): [(near, 3)],
         (6, 0): [(far, 3)],
     }
@@ -1302,10 +1790,10 @@
     net.relay(1)
     relay(2, 1)
     net.sides(0)
+    over(0)
     for c in kept:
         c.wait()
     near(0)
-    loads(unit_of(jnp.int32(0)), 0)[1].start()
 
     def body(i, carry):
         slot = i % 2
@@ -1321,10 +1809,6 @@
                             action(*values)
 
         hook(0)
-
-        @pl.when(i + 1 < n_units)
-        def _():
-            loads(unit_of(i + 1), 1 - slot)[1].start()
 
         for c in loads(u, slot):
             c.wait()
@@ -1344,6 +1828,7 @@
         for c in stores(unit_of(jnp.int32(i)), i % 2):
             c.wait()
     copies.close()
+    rest.copies.close()
 
 
 def expert_call(own, own_gates, grads, w_gate, w_up, w_down, shared, n_dp, capacity, collective_id):
@@ -1362,6 +1847,7 @@
             everyone,
             everyone,
             everyone,
+            everyone,
             jax.ShapeDtypeStruct(all_gates, jnp.float32),
             jax.ShapeDtypeStruct((rows, model), bf16),
             jax.ShapeDtypeStruct((rows, model), bf16),
@@ -1369,7 +1855,8 @@
             jax.ShapeDtypeStruct((blocks * own_rows, 384), bf16),
         ],
         in_specs=[ANY, ANY, ANY, vmem, vmem, vmem, vmem],
-        out_specs=[ANY, ANY, ANY, vmem, ANY, ANY, ANY, ANY],
+        out_specs=[ANY, ANY, ANY, ANY, vmem, ANY, ANY, ANY, ANY],
+        input_output_aliases={2: 1},
         scratch_shapes=ExpertWork.scratch(model, width, capacity, own_rows)
         + [
             pltpu.VMEM(all_gates, jnp.float32),
@@ -1378,21 +1865,13 @@
             pltpu.SemaphoreType.DMA((2,)),
             pltpu.SemaphoreType.DMA((11 * n_planes, 2)),
             pltpu.SemaphoreType.DMA((11 * n_planes, 2)),
+            pltpu.SemaphoreType.DMA((11 * n_planes, 1)),
+            pltpu.SemaphoreType.DMA((11 * n_planes, 1)),
         ],
         compiler_params=pltpu.CompilerParams(
             collective_id=collective_id, has_side_effects=True, vmem_limit_bytes=60 << 20
         ),
     )(own, own_gates, grads, w_gate, w_up, w_down, shared)
-
-
-def swap_halves(own, x):
-    return lax.ppermute(own, TENSOR, [(0, 1), (1, 0)])
-
-
-def halves_sum(partial, rows, x):
-    kept = lax.dynamic_slice_in_dim(partial, x * rows, rows, 0)
-    given = lax.dynamic_slice_in_dim(partial, (1 - x) * rows, rows, 0).astype(jnp.bfloat16)
-    return kept + swap_halves(given, x).astype(jnp.float32)
 
 
 def gather_plan(
@@ -1428,17 +1907,31 @@
         return jnp.dot(a, b, preferred_element_type=f32)
 
     width = attention_gain.shape[0]
-    small = jnp.concatenate([attention_gain, expert_norm_gain, router.reshape(-1)])
-    small = jnp.pad(small, (0, -small.shape[0] % 2048)).reshape(-1, 128)
+    lanes = 2 * width
+    tile = jnp.concatenate(
+        [router.T, attention_gain[None], expert_norm_gain[None], jnp.zeros((-(experts + 2) % 16, width), bf16)]
+    )
+    tile = lax.dynamic_update_slice(jnp.zeros((tile.shape[0], lanes), bf16), tile, (0, x * width))
+    rotary_cosine, rotary_sine = rotation(sequence_length, HEAD_SIZE)
+    cosine = jnp.concatenate([rotary_cosine, rotary_cosine], axis=1)
+    sine = jnp.concatenate([-rotary_sine, rotary_sine], axis=1)
+    doc_ends = jnp.cumsum(document_lengths[0])
+    positions = jnp.arange(sequence_length, dtype=jnp.int32)
+    doc_ids = jnp.sum((positions[:, None] >= doc_ends[None, :]).astype(jnp.int32), axis=-1)
+    allowed = (doc_ids[:, None] == doc_ids[None, :]) & (positions[:, None] >= positions[None, :])
+    own_indices = lax.dynamic_slice_in_dim(expert_indices, x * own_rows, own_rows, 0)
+    chosen = jnp.any(own_indices[None] == jnp.arange(experts, dtype=jnp.int32)[:, None, None], axis=2)
     axes = (0, 0, 0, 1)
-    query_all, key_all, value_all, out_all, sequence, smalls, cotangent_all = fetch(
+    (
+        query_all, key_all, value_all, out_all, cotangent_all, params, full_one, rows_of_query, key_rows,
+        rows_of_value, attn_probs, mixed_heads, residual, normed_two, gates_t,
+    ) = front(
         [query_projection, key_projection, value_projection, output_projection],
-        axes, tokens, small, cotangent, n_dp, 1,
-    )
-    flat = smalls.swapaxes(0, 1).reshape(2 * n_dp, -1)
-    first_gain = flat[:, :width].reshape(-1).astype(f32)
-    second_gain = flat[:, width : 2 * width].reshape(-1).astype(f32)
-    router_full = flat[:, 2 * width : (2 + experts) * width].reshape(model_dim, experts)
+        axes, tokens, tile, cotangent, chosen.astype(f32), cosine, sine, allowed.astype(f32), n_dp, 1,
+    )
+    router_full = params[:experts]
+    first_gain = params[experts].astype(f32)
+    second_gain = params[experts + 1].astype(f32)
 
     hidden = shared_gate_matrix.shape[1] // n_dp
     hidden_pad = -(-hidden // 16) * 16
@@ -1453,128 +1946,48 @@
     shared_in = lax.all_to_all(shared_out, DP, split_axis=0, concat_axis=0, tiled=True)
     shared_rows = jnp.moveaxis(shared_in, 0, 2).reshape(3, hidden_pad, model_dim)
 
-    full_tokens = sequence.reshape(sequence_length, model_dim).astype(f32)
-    full_scale = lax.rsqrt(jnp.mean(full_tokens * full_tokens, axis=-1, keepdims=True) + norm_eps)
-    full_one = (full_tokens * full_scale * first_gain).astype(bf16)
-    input_values = tokens.astype(f32)
-    scale_one = lax.dynamic_slice_in_dim(full_scale, x * own_rows, own_rows, 0)
-    q_heads = query_all.shape[1] // HEAD_SIZE
-    kv_heads = key_all.shape[1] // HEAD_SIZE
-    group_size = q_heads // kv_heads
-    rotary_cosine, rotary_sine = rotation(sequence_length, HEAD_SIZE)
-    query_unrotated = dot(full_one, query_all).reshape(sequence_length, q_heads, HEAD_SIZE)
-    key_unrotated = dot(full_one, key_all).reshape(sequence_length, kv_heads, HEAD_SIZE)
-    rows_of_query = (
-        apply_rotary(query_unrotated, rotary_cosine, rotary_sine)
-        .astype(bf16)
-        .reshape(sequence_length, kv_heads, group_size, HEAD_SIZE)
-    )
-    key_rows = apply_rotary(key_unrotated, rotary_cosine, rotary_sine).astype(bf16)
-    rows_of_value = dot(full_one, value_all).astype(bf16).reshape(sequence_length, kv_heads, HEAD_SIZE)
-    doc_ends = jnp.cumsum(document_lengths[0])
-    positions = jnp.arange(sequence_length, dtype=jnp.int32)
-    doc_ids = jnp.sum((positions[:, None] >= doc_ends[None, :]).astype(jnp.int32), axis=-1)
-    score_scale = HEAD_SIZE ** (-0.5)
-    allowed = (doc_ids[:, None] == doc_ids[None, :]) & (positions[:, None] >= positions[None, :])
-    scores = (
-        jnp.einsum("qkgd,skd->kgqs", rows_of_query, key_rows, preferred_element_type=f32) * score_scale
-    )
-    scores = jnp.where(allowed, scores, neg_big)
-    exp_scores = jnp.exp(scores - jnp.max(scores, axis=-1, keepdims=True))
-    attn_probs = exp_scores / jnp.sum(exp_scores, axis=-1, keepdims=True)
-    probs_low = attn_probs.astype(bf16)
-    mixed_heads = (
-        jnp.einsum("kgqs,skd->qkgd", probs_low, rows_of_value, preferred_element_type=f32)
-        .reshape(sequence_length, q_heads * HEAD_SIZE)
-        .astype(bf16)
-    )
-    residual = input_values + halves_sum(dot(mixed_heads, out_all), own_rows, x)
-
-    scale_two = lax.rsqrt(jnp.mean(residual * residual, axis=-1, keepdims=True) + norm_eps)
-    normed_two = (residual * scale_two * second_gain).astype(bf16)
-    logits = dot(normed_two, router_full)
-    own_indices = lax.dynamic_slice_in_dim(expert_indices, x * own_rows, own_rows, 0)
-    chosen = own_indices[:, :, None] == jnp.arange(experts, dtype=jnp.int32)[None, None, :]
-    selected = jnp.sum(jnp.where(chosen, logits[:, None, :], 0.0), axis=-1)
-    gate_exp = jnp.exp(selected - jnp.max(selected, axis=-1, keepdims=True))
-    gate_probs = gate_exp / jnp.sum(gate_exp, axis=-1, keepdims=True)
-    gates = jnp.sum(jnp.where(chosen, gate_probs[:, :, None], 0.0), axis=1)
-
-
     shared_rows = jnp.pad(shared_rows, ((0, 0), (0, 128 - hidden_pad), (0, 0))).reshape(384, model_dim)
-    normed_all, output_parts, normed_parts, grad_gate_parts, received, grad_rows, hidden_rows, shared_hidden = (
+    (
+        normed_all, cotangent_all, output_parts, normed_parts, grad_gate_parts, received, grad_rows, hidden_rows,
+        shared_hidden,
+    ) = (
         expert_call(
-            normed_two, gates.T, cotangent_all, expert_gate_matrix[0], expert_up_matrix[0], expert_down_matrix[0],
+            normed_two, gates_t, cotangent_all, expert_gate_matrix[0], expert_up_matrix[0], expert_down_matrix[0],
             shared_rows, n_dp, capacity, 2,
         )
     )
-    expert_gate_gradient = dot(received.T, hidden_rows[1])[None]
-    expert_up_gradient = dot(received.T, hidden_rows[2])[None]
-    expert_down_gradient = dot(hidden_rows[0].T, grad_rows)[None]
-    normed_flat = normed_all.reshape(-1, model_dim)
-    grad_flat = cotangent_all.reshape(-1, model_dim)
-    shared_grads = jnp.concatenate(
-        [dot(shared_hidden[:, 128:].T, normed_flat), dot(shared_hidden[:, :128].T, grad_flat)]
-    ).astype(bf16)
+    (
+        grad_normed_two, grad_gates_t, expert_gate_gradient, expert_up_gradient, expert_down_gradient, shared_grads,
+    ) = sum_everywhere(
+        [normed_parts, grad_gate_parts],
+        [f32, f32],
+        [
+            received, grad_rows, normed_all.reshape(-1, model_dim), cotangent_all.reshape(-1, model_dim),
+            hidden_rows, shared_hidden,
+        ],
+        n_dp, 4,
+    )
     shared_grads = shared_grads.reshape(3, 128, model_dim)[:, :hidden_pad]
-    grad_normed_two, grad_gates_t = sum_everywhere([normed_parts, grad_gate_parts], [f32, f32], n_dp, 4)
-
+
+    gates = gates_t.T
+    scale_two = lax.rsqrt(jnp.mean(residual * residual, axis=-1, keepdims=True) + norm_eps)
     grad_gates = grad_gates_t.T
     grad_logits = (
         gates * (grad_gates - jnp.sum(gates * grad_gates, axis=-1, keepdims=True))
     ).astype(bf16)
-    grad_normed_two = grad_normed_two + dot(grad_logits, router_full.T)
+    grad_normed_two = grad_normed_two + dot(grad_logits, router_full)
     grad_router_part = dot(normed_two.T, grad_logits)
     grad_residual, grad_gain_two = rms_back(grad_normed_two, residual, scale_two, second_gain)
     grad_residual = grad_residual + cotangent.astype(f32)
-    grad_low = grad_residual.astype(bf16)
-    grad_other = swap_halves(grad_low, x)
-    grad_attn = jnp.where(
-        x == 0, jnp.concatenate([grad_low, grad_other]), jnp.concatenate([grad_other, grad_low])
-    )
-
-    grad_wout = dot(mixed_heads.T, grad_attn)
-    grad_mixed = (
-        dot(grad_attn, out_all.T).astype(bf16).reshape(sequence_length, kv_heads, group_size, HEAD_SIZE)
-    )
-    grad_values = jnp.einsum("kgqs,qkgd->skd", probs_low, grad_mixed, preferred_element_type=f32)
-    grad_probs = jnp.einsum("qkgd,skd->kgqs", grad_mixed, rows_of_value, preferred_element_type=f32)
-    inner_sum = jnp.sum(attn_probs * grad_probs, axis=-1, keepdims=True)
-    grad_scores = (attn_probs * (grad_probs - inner_sum)).astype(bf16)
-    grad_query = (
-        jnp.einsum("kgqs,skd->qkgd", grad_scores, key_rows, preferred_element_type=f32) * score_scale
-    ).reshape(sequence_length, q_heads, HEAD_SIZE)
-    grad_keys = (
-        jnp.einsum("kgqs,qkgd->skd", grad_scores, rows_of_query, preferred_element_type=f32) * score_scale
-    )
-    grad_q_raw = rotate_back(grad_query, rotary_cosine, rotary_sine).astype(bf16)
-    grad_q_raw = grad_q_raw.reshape(sequence_length, q_heads * HEAD_SIZE)
-    grad_k_raw = rotate_back(grad_keys, rotary_cosine, rotary_sine).astype(bf16)
-    grad_k_raw = grad_k_raw.reshape(sequence_length, kv_heads * HEAD_SIZE)
-    grad_v_low = grad_values.astype(bf16).reshape(sequence_length, kv_heads * HEAD_SIZE)
-    grad_wquery = dot(full_one.T, grad_q_raw).astype(bf16)
-    grad_wkey = dot(full_one.T, grad_k_raw).astype(bf16)
-    grad_wvalue = dot(full_one.T, grad_v_low).astype(bf16)
-    grad_normed_one = halves_sum(
-        dot(grad_q_raw, query_all.T) + dot(grad_k_raw, key_all.T) + dot(grad_v_low, value_all.T), own_rows, x
-    )
-    grad_inputs, grad_gain_one = rms_back(grad_normed_one, input_values, scale_one, first_gain)
-    grad_inputs = grad_inputs + grad_residual
-
-    def by_owner(v):
-        return v.reshape(2 * n_dp, -1)
-
-    tiles = jnp.concatenate([by_owner(grad_gain_one), by_owner(grad_gain_two), by_owner(grad_router_part)], axis=1)
-    tiles = jnp.pad(tiles, ((0, 0), (0, -tiles.shape[1] % 2048)))
-    small_rows = tiles.shape[1] // 128
-    sums = sum_back(
-        [grad_wquery, grad_wkey, grad_wvalue, grad_wout.astype(bf16), tiles.reshape(-1, 128)],
-        axes + (0,), output_parts, n_dp, 6,
-    )
-    output = (residual + sums[5]).astype(bf16)
-    mine = sums[4].reshape(-1)
-    gain_one_own, gain_two_own = mine[:width], mine[width : 2 * width]
-    router_own = mine[2 * width : (2 + experts) * width].reshape(width, experts)
+    small_grads = jnp.concatenate([grad_router_part.T, jnp.zeros((8, model_dim), f32).at[1].set(grad_gain_two)])
+    *weight_grads, grad_inputs, small_sums, ffn_own = backward(
+        grad_residual.astype(bf16), mixed_heads, full_one, rows_of_query, key_rows, rows_of_value, attn_probs,
+        [query_all, key_all, value_all, out_all], axes, cosine, sine, tokens, grad_residual, first_gain[None],
+        small_grads, output_parts, n_dp, 6,
+    )
+    output = (residual + ffn_own).astype(bf16)
+    mine = lax.dynamic_slice_in_dim(small_sums, x * width, width, 1)
+    gain_one_own, gain_two_own, router_own = mine[experts], mine[experts + 1], mine[:experts].T
     returned = lax.all_to_all(
         shared_grads.reshape(3, hidden_pad, n_dp, -1).transpose(2, 0, 1, 3),
         DP, split_axis=0, concat_axis=0, tiled=True,
@@ -1585,17 +1998,14 @@
         grad_inputs,
         gain_one_own,
         gain_two_own,
-        sums[0],
-        sums[1],
-        sums[2],
-        sums[3],
+        *weight_grads,
         router_own,
         returned[0].T,
         returned[1].T,
         returned[2],
-        expert_gate_gradient,
-        expert_up_gradient,
-        expert_down_gradient,
+        expert_gate_gradient[None],
+        expert_up_gradient[None],
+        expert_down_gradient[None],
     )
 
 

time: 690 us -> 659 us (0.955)
  Pallas kernels: 482 us -> 581 us
  matrix products: 94.5 us -> 0.75 us
  waiting for transfers between devices: 14.9 us -> 0.01 us
  other arithmetic: 20.2 us -> 10.6 us
  local copies, waits for them, and re-layouts: 51.9 us -> 44.9 us
    dot_general x20 -> x2, matrix products: 85.5 us -> 0.75 us  [dot(): return jnp.dot(a, b, preferred_element_type=f32)]
    pallas_call x2, Pallas kernels: 280 us -> 347 us  [the longest x1 194 us: backward(): pl.pallas_call(functools.partial(back_kernel, n_planes, axes), out_shape=...]
    pallas_call x1, Pallas kernels: 123 us -> 154 us  [expert_call(): pl.pallas_call(functools.partial(expert_kernel, n_dp), out_shape=[everyon...]
    unnamed x118 -> x61, local copies, waits for them, and re-layouts: 24.4 us -> 36.9 us
    all_to_all x1, waiting for transfers between devices: 11 us -> 0.01 us  [gather_plan(): lax.all_to_all(shared_out, DP, split_axis=0, concat_axis=0, tiled=True)]
    dot_general x2 -> x0, local copies, waits for them, and re-layouts: 7.92 us -> none  [dot(): return jnp.dot(a, b, preferred_element_type=f32)]
  transfers between devices with their start and end apart: 5 -> 2, of which waited for: 2 -> 0; matrix products, arithmetic and copies ran while one was open for 12% -> 5% of each run, Pallas kernels for 21% -> 53%
where the time goes in v3:
time: 659 us; the launch traced here: 650 us
  Pallas kernels  581 us (88%)
  local copies, waits for them, and re-layouts  44.9 us (7%)
  starting transfers between devices  12.3 us (2%)
  other arithmetic  10.6 us (2%)
    pallas_call x1, Pallas kernels, backward(): pl.pallas_call(functools.partial(back_kernel, n_planes, axes), out_shape=...  194 us
    pallas_call x1, Pallas kernels, expert_call(): pl.pallas_call(functools.partial(expert_kernel, n_dp), out_shape=[everyon...  154 us
    pallas_call x1, Pallas kernels, front(): pl.pallas_call(functools.partial(front_kernel, n_planes, axes), out_shape...  153 us
    pallas_call x1, Pallas kernels, sum_everywhere(): pl.pallas_call(functools.partial(sum_kernel, n_planes, n), out_shape=[jax...  79.6 us
    unnamed x61, local copies, waits for them, and re-layouts  36.9 us
  transfers between devices with their start and end apart: 2, of which 0 were waited for; matrix products, arithmetic and copies ran while one was open for 5% of the time, Pallas kernels for 53%

profile of v3, /device:TPU:24, one launch (start us, length us, event | category | flops | bytes accessed | tf_op | source)
XLA Modules:
  0.0 650.2 jit_solution(17865671789621908042)
XLA Ops:
  0.7 1.2 copy.94
  1.9 1.2 copy.93
  3.4 1.1 copy.95
  4.5 6.1 all-to-all-start
  11.4 4.6 copy.91
  16.0 4.6 copy.92
  21.5 0.8 pad_maximum_fusion.1
  22.4 0.8 fusion.1.refs_10_
  23.2 153.0 %shard_map.280 = (bf16[2048,1024]{1,0:T(8,128)(2,1)}, bf16[2048,256]{1,0:T(8,128)(2,1)}, bf16[2048,256]{1,0:T(8,128)(2,1)}, bf16[1024,2048]{1,0:T(8,128)(2,1)}, ...) custom-call(bf16[128,1024]{1,0:T(8,128)(2,1)} %refs_0_.1, ...), custom_call_target="tpu_custom_call" | custom-call | flops 3221225472 | bytes 67108864 | tf_op jit(solution)/shard_map/pallas_call | solution.py:878
  176.2 1.4 multiply_reduce_fusion.2
  177.5 1.4 slice_convert_fusion
  179.1 1.3 pad.20
  180.5 153.9 %shard_map.281 = (bf16[32,128,2048]{2,1,0:T(8,128)(2,1)}, bf16[32,128,2048]{2,1,0:T(8,128)(2,1)}, bf16[32,128,2048]{2,1,0:T(8,128)(2,1)}, bf16[32,128,2048]{2,1,...) custom-call(bf16[128,2048]{1,0:T(8,128)(2,1)} %get-tuple-element.65., ...), custom_call_target="tpu_custom_call", output_to_operand_aliasing={{1}: (2, {})} | custom-call | tf_op jit(solution)/shard_map/pallas_call | solution.py:1844
  334.4 79.6 %shard_map.282 = (f32[128,2048]{1,0:T(8,128)}, f32[16,128]{1,0:T(8,128)}, f32[2048,704]{1,0:T(8,128)}, f32[2048,704]{1,0:T(8,128)}, f32[704,2048]{1,0:T(8,128)}, /*index=5*/bf16[384,2048]{1,0:T(8,128)(2,1)}) custom-call(bf16[32,128,2048]{2,1,0:T(8,128)(2,1)} %get-tuple-element.68.refs_0_, f32[32,16,128]{2,1,0:T(8,128)} %get-tuple-element.69.refs_1_, ...), custom_call_target="tpu_custom_call" | custom-call | tf_op jit(solution)/shard_map/pallas_call | solution.py:1252
  414.0 1.4 slice.61
  415.9 1.3 copy.97
  417.2 6.2 all-to-all-start.1
  424.2 0.7 select_maximum_fusion.refs_16_
  424.9 1.5 fusion.10
  426.5 194.1 %shard_map.283 = (f32[128,1024]{1,0:T(8,128)}, f32[128,256]{1,0:T(8,128)}, f32[128,256]{1,0:T(8,128)}, f32[1024,128]{1,0:T(8,128)}, f32[128,2048]{1,0:T(8,128)}, /*index=5*/f32[24,128]{1,0:T(8,128)}, f32[128,2048]{1,0:T(8,128)}) custom-call(bf16[128,2048]{1,0:T(8,128)(2,1)} %get-tuple-element.193.refs_0_, bf16[256,1024]{1,0:T(8,128)(2,1)} %get-tuple-element.79.refs_1_, ...), custom_call_target="tpu_custom_call" | custom-call | flops 6442450944 | bytes 67108864 | tf_op jit(solution)/shard_map/pallas_call | solution.py:1475
  620.6 6.4 copy.101
  626.9 6.5 %copy.102 = f32[1,2048,704]{1,2,0:T(8,128)} copy(f32[1,2048,704]{2,1,0:T(8,128)} %bitcast.78) | data formatting | bytes 11534336
  634.0 0.7 dynamic-slice_bitcast_fusion
  634.7 0.9 add_convert_fusion
  635.6 1.4 convert_bitcast_fusion
  637.0 1.0 fusion.11
  638.0 1.1 copy.100
  639.1 1.1 copy.99
  640.3 1.0 copy.116
  641.2 0.8 copy.117
  643.4 0.8 copy.120
  644.2 5.9 copy.121
  (75 shorter events, 5.3 us)
Async XLA Ops:
  0.6 9.9 %copy-start = (s32[256,6]{0,1:T(8,128)S(1)}, s32[256,6]{0,1:T(8,128)}, u32[]{:S(2)}) copy-start(s32[256,6]{0,1:T(8,128)} %param.34) | copy-start | bytes 18436
  0.7 2.5 copy-start.11
  3.4 7.8 %copy-start.22 = (s32[1,4]{1,0:T(1,128)S(1)}, s32[1,4]{1,0:T(1,128)}, u32[]{:S(2)}) copy-start(s32[1,4]{1,0:T(1,128)} %param.33) | copy-start | bytes 52
  4.5 174.5 %all-to-all-start = ((bf16[16,3,96,128]{3,2,1,0:T(8,128)(2,1)}), bf16[16,3,96,128]{3,2,1,0:T(8,128)(2,1)S(1)}, u32[]{:S(2)}, u32[]{:S(2)}) async-start(bf16[16,3,96,128]{3,2,1,0:T(8,128)(2,1)} %copy.95), calls=%async_computation | async-start | bytes 2359296 | tf_op jit(solution)/shard_map/all_to_all | solution.py:1946
  16.0 4.7 copy-start.19
  16.0 4.7 copy-start.20
  16.0 4.7 copy-start.21
  20.9 2.3 copy-start.17
  415.9 7.5 %copy-start.14 = (f32[16,128]{1,0:T(8,128)S(1)}, f32[16,128]{1,0:T(8,128)}, u32[]{:S(2)}) copy-start(f32[16,128]{1,0:T(8,128)} %get-tuple-element.66.refs_1_) | copy-start | bytes 24580
  415.9 7.5 %copy-start.16 = (f32[16,128]{1,0:T(8,128)S(1)}, f32[16,128]{1,0:T(8,128)}, u32[]{:S(2)}) copy-start(f32[16,128]{1,0:T(8,128)} %get-tuple-element.77) | copy-start | bytes 24580
  415.9 7.6 %copy-start.4 = (bf16[128,2048]{1,0:T(8,128)(2,1)S(1)}, bf16[128,2048]{1,0:T(8,128)(2,1)}, u32[]{:S(2)}) copy-start(bf16[128,2048]{1,0:T(8,128)(2,1)} %get-tuple-element.65.refs_0_) | copy-start | bytes 1572868
  417.2 6.4 copy-start.2
  417.2 6.4 copy-start.5
  417.2 6.4 copy-start.15
  417.2 218.4 %all-to-all-start.1 = ((bf16[16,3,96,128]{3,2,1,0:T(8,128)(2,1)}), bf16[16,3,96,128]{3,2,1,0:T(8,128)(2,1)}, u32[]{:S(2)}, u32[]{:S(2)}) async-start(bf16[16,3,96,128]{3,2,1,0:T(8,128)(2,1)} %copy.97), calls=%async_computation.1 | async-start | bytes 2359296 | tf_op jit(solution)/shard_map/all_to_all | solution.py:1991
  423.5 1.5 copy-start.8
  626.9 6.5 %copy-start.18 = (f32[24,128]{1,0:T(8,128)S(1)}, f32[24,128]{1,0:T(8,128)}, u32[]{:S(2)}) copy-start(f32[24,128]{1,0:T(8,128)} %get-tuple-element.92) | copy-start | bytes 36868
  626.9 7.8 %copy-start.3 = (f32[128,2048]{1,0:T(8,128)S(1)}, f32[128,2048]{1,0:T(8,128)}, u32[]{:S(2)}) copy-start(f32[128,2048]{1,0:T(8,128)} %get-tuple-element.64) | copy-start | bytes 3145732
  626.9 7.8 %copy-start.7 = (f32[128,2048]{1,0:T(8,128)S(1)}, f32[128,2048]{1,0:T(8,128)}, u32[]{:S(2)}) copy-start(f32[128,2048]{1,0:T(8,128)} %get-tuple-element.90) | copy-start | bytes 3145732
  638.0 2.3 copy-start.6
  639.1 2.1 copy-start.10
  639.1 2.9 copy-start.13
  639.1 3.6 copy-start.12
  640.3 3.1 copy-start.9
  644.2 5.9 copy-start.1

commit v4 on v3

--- a/solution.py
+++ b/solution.py
@@ -538,13 +538,13 @@
             when(condition, body)
 
 
-(Z_UP, Z_DOWN, Y_ALL, Y_HALF, X_ALL, X_HALF, C_OWN, C_Y, C_X, C_XH, C_YH) = range(11)
+(Z_UP, Z_DOWN, Y_ALL, Y_HALF, X_ALL, X_HALF, C_OWN, C_Y, C_X, C_XH, C_YH, D_UP, D_DOWN, C_D) = range(14)
 (ALL, FIRST, SECOND) = range(3)
 
 
 class Spread:
-    def __init__(self, spot, copies, own, views, use_x):
-        self.spot, self.copies, self.own, self.use_x = spot, copies, own, use_x
+    def __init__(self, spot, copies, own, views, use_x, by_z=False):
+        self.spot, self.copies, self.own, self.use_x, self.by_z = spot, copies, own, use_x, by_z
         self.order = spot.far_first()[::-1]
         y, x, core = spot.y, spot.x, spot.core
 
@@ -557,12 +557,20 @@
                 views(s, y, cc, 1 - x, SECOND),
                 views(s, 1 - y, cc, 1 - x, FIRST),
                 views(s, 1 - y, cc, 1 - x, SECOND),
+                views(s, 1 - y, cc, 1 - x, ALL),
             )
 
         self.mine = [places(s, core) for s in self.order]
         self.twins = [places(s, 1 - core) for s in self.order]
         self.goes_down = [(s > spot.z) & spot.has_down for s in self.order]
         self.goes_up = [(s < spot.z) & spot.has_up for s in self.order]
+        middle = spot.has_up & spot.has_down
+        self.among = (jnp.logical_not(middle), middle)
+        self.goes = {
+            (j, c): (self.goes_down[j] & self.among[c], self.goes_up[j] & self.among[c], self.among[c])
+            for j in range(len(self.order))
+            for c in (0, 1)
+        }
 
     def place(self, j):
         return self.own if j == 0 else self.mine[j][0]
@@ -593,10 +601,16 @@
 
     def relay(self, j, goes=None):
         s, here, spot = self.order[j], self.mine[j][0], self.spot
-        goes_down, goes_up = goes or (self.goes_down[j], self.goes_up[j])
+        goes_down, goes_up, _ = goes or (self.goes_down[j], self.goes_up[j], None)
         self.copies.arrive(Z_UP, s, here, spot.up)
         self.copies.start(goes_down, Z_DOWN, s, here, here, spot.down, Z_UP)
         self.copies.start(goes_up, Z_UP, s, here, here, spot.up)
+
+    def relay_of(self, j, c):
+        pl.when(self.among[c])(functools.partial(self.relay, j, self.goes[j, c]))
+
+    def corner_of(self, j, c):
+        pl.when(self.among[c])(functools.partial(self.corner, j, self.goes[j, c]))
 
     def column(self, j):
         if j < len(self.order):
@@ -623,12 +637,13 @@
 
     def side(self, j):
         self.from_side(j)
-        if self.use_x:
+        if self.use_x and (j == 0 or not self.by_z):
             self.over_x(j)
 
     def across(self, j):
         self.from_across(j)
-        self.over_y(j)
+        if j == 0 or not self.by_z:
+            self.over_y(j)
 
     def sides(self, j):
         if 0 <= j < len(self.order):
@@ -636,15 +651,25 @@
             if self.use_x:
                 self.across(j)
 
-    def corner(self, j):
+    def corner(self, j, goes=None):
         if not self.use_x or not 0 <= j < len(self.order):
             return
         s, spot = self.order[j], self.spot
-        first, second = self.mine[j][5:]
+        first, second, whole = self.mine[j][5:]
+        if self.by_z and j > 0:
+            goes_down, goes_up, always = goes or (self.goes_down[j], self.goes_up[j], None)
+            self.copies.arrive(D_UP, s, whole, spot.up)
+            self.copies.start(goes_down, D_DOWN, s, whole, whole, spot.down, D_UP)
+            self.copies.start(goes_up, D_UP, s, whole, whole, spot.up)
+            self.copies.start(always, C_D, s, whole, whole, spot.twin)
+            return
         self.copies.arrive(X_HALF, s, first, spot.across)
         self.copies.start(None, C_XH, s, first, first, spot.twin)
         self.copies.arrive(Y_HALF, s, second, spot.side)
         self.copies.start(None, C_YH, s, second, second, spot.twin)
+        if self.by_z:
+            self.copies.start(spot.has_up, D_UP, s, whole, whole, spot.up)
+            self.copies.start(spot.has_down, D_DOWN, s, whole, whole, spot.down, D_UP)
 
     def twin_near(self, j):
         s, there, spot = self.order[j], self.twins[j], self.spot
@@ -656,6 +681,9 @@
         self.copies.arrive(C_Y, self.order[j], self.twins[j][1], self.spot.twin)
 
     def twin_corner(self, j):
+        if self.by_z and j > 0:
+            self.copies.arrive(C_D, self.order[j], self.twins[j][7], self.spot.twin)
+            return
         self.copies.arrive(C_XH, self.order[j], self.twins[j][5], self.spot.twin)
         self.copies.arrive(C_YH, self.order[j], self.twins[j][6], self.spot.twin)
 
@@ -770,12 +798,10 @@
     net.onward_y(0)
     net.from_across(0)
 
-    def column(j):
-        net.relay(j)
-        net.onward_x(j)
-        net.onward_twin(j)
-
-    column(1)
+    net.relay(1)
+    net.relay_of(2, 1)
+    net.onward_x(1)
+    net.onward_twin(1)
 
     small.twin_all()
     swap(1, sequence.at[1 - x], sequence.at[1 - x]).wait_recv()
@@ -809,7 +835,10 @@
         query[:, span] = turn(raw[:, span], cos, sin).astype(bf16)
     net.from_side(0)
     net.onward_y(1)
-    column(2)
+    net.relay_of(2, 0)
+    net.relay_of(3, 1)
+    net.onward_x(2)
+    net.onward_twin(2)
     net.from_across(1)
     may = allowed[...] > 0.0
     for h in range(heads):
@@ -829,7 +858,9 @@
     residual[...] = plain_dot(other, wo[...], ROWS_COLUMNS)
     net.from_side(1)
     net.onward_y(2)
-    column(3)
+    net.relay_of(3, 0)
+    net.onward_x(3)
+    net.onward_twin(3)
     net.from_across(2)
     swap(2, received, received).wait_recv()
     second_gain = params[experts + 1 : experts + 2, :].astype(f32)
@@ -900,8 +931,8 @@
             pltpu.VMEM((own_rows, model), bf16),
             pltpu.VMEM((own_rows, model), bf16),
         ]
-        + [dma((11 * n_planes, n))] * 2
-        + [dma((11 * n_planes, 1))] * 4
+        + [dma((14 * n_planes, n))] * 2
+        + [dma((14 * n_planes, 1))] * 4
         + [dma((n + 3,)), dma((n,)), dma((3,)), dma((3,))],
         compiler_params=pltpu.CompilerParams(
             collective_id=collective_id, has_side_effects=True, vmem_limit_bytes=56 << 20
@@ -912,7 +943,7 @@
     )(*arrays, tokens, tile, grads, chosen, cosine, sine, allowed)
 
 
-(T_YX, T_Y, T_X, T_OWN, R_XHALF, R_YHALF, R_YALL, R_XALL, R_UP, R_DOWN) = range(10)
+(T_YX, T_Y, T_X, T_OWN, R_XHALF, R_YHALF, R_YALL, R_XALL, R_UP, R_DOWN, R_DUP, R_DDOWN) = range(12)
 
 
 def add_up(target, sources):
@@ -932,7 +963,7 @@
 
 class Reduce:
     @staticmethod
-    def scratch(shapes, dtypes, n_planes, use_x, cut=0, direct=False):
+    def scratch(shapes, dtypes, n_planes, use_x, cut=0, direct=False, by_z=False):
         kinds = 4 if use_x else 2
         out = []
         for i, (shape, dtype) in enumerate(zip(shapes, dtypes)):
@@ -944,17 +975,20 @@
                 out.append(pltpu.VMEM((kinds, 2) + shape, dtype))
             if use_x:
                 out.append(pltpu.VMEM((n_planes,) + shape, dtype))
-                out.append(pltpu.VMEM((n_planes, rows) + shape[1:], dtype))
+                out.append(pltpu.VMEM((1 if by_z else n_planes, rows) + shape[1:], dtype))
+                if by_z:
+                    out.append(pltpu.VMEM((n_planes + 1,) + shape, dtype))
                 if i == 0 and cut < shape[0]:
-                    out.append(pltpu.VMEM((n_planes, shape[0] - cut) + shape[1:], dtype))
+                    out.append(pltpu.VMEM((1 if by_z else n_planes, shape[0] - cut) + shape[1:], dtype))
         n = len(shapes)
-        out.append(pltpu.SemaphoreType.DMA((10 * n_planes, n)))
-        out.append(pltpu.SemaphoreType.DMA((10 * n_planes, n)))
+        out.append(pltpu.SemaphoreType.DMA((12 * n_planes, n)))
+        out.append(pltpu.SemaphoreType.DMA((12 * n_planes, n)))
         out.append(pltpu.SemaphoreType.DMA((kinds * n_planes, n)))
         return out
 
-    def __init__(self, spot, blocks, outs, scratch, use_x, cut=0, direct=False):
-        self.spot, self.outs, self.use_x, self.direct = spot, outs, use_x, direct
+    def __init__(self, spot, blocks, outs, scratch, use_x, cut=0, direct=False, by_z=False):
+        self.spot, self.outs, self.use_x, self.direct, self.by_z = spot, outs, use_x, direct, by_z
+        self.slant = []
         self.n, self.n_planes, self.cut = len(outs), spot.n_planes, cut
         left = list(scratch)
         self.twin, self.line, self.near, self.ring, self.across, self.first = [], [], [], [], [], []
@@ -968,6 +1002,8 @@
             if use_x:
                 self.across.append(left.pop(0))
                 self.first.append(left.pop(0))
+                if by_z:
+                    self.slant.append(left.pop(0))
                 if i == 0 and cut < self.near[0].shape[1]:
                     self.second = left.pop(0)
         send, recv, self.local = left
@@ -1013,28 +1049,69 @@
             c.wait()
         return twin, [r.at[k, j % 2] for r in self.ring]
 
+    def along(self, j, here, line, targets, up, down):
+        s, spot, copies = self.order[j], self.spot, self.copies
+        some = [t.at[s] for t in line]
+        below = [t.at[self.n_planes] for t in line]
+
+        def add_all(*more):
+            for i in range(self.n):
+                add_up(targets[i], here[i] + [m[i] for m in more])
+
+        if j == self.n_planes - 1:
+            when(spot.has_up, lambda: copies.arrive(down, s, some, spot.up))
+            when(spot.has_down, lambda: copies.arrive(up, s, below, spot.down))
+            when(spot.has_up & spot.has_down, lambda: add_all(some, below))
+            when(spot.z == 0, lambda: add_all(some))
+            when(spot.z == self.n_planes - 1, lambda: add_all(below))
+            return
+        for goes, more, group, last, device, source in (
+            (s < spot.z, spot.has_up, down, None, spot.down, spot.up),
+            (s > spot.z, spot.has_down, up, s - spot.z == 1, spot.up, spot.down),
+        ):
+
+            def partial():
+                copies.arrive(group, s, some, source)
+                add_all(some)
+
+            when(goes & more, partial)
+            when(goes & jnp.logical_not(more), add_all)
+            if last is None:
+                copies.start(goes, group, s, targets, some, device)
+            else:
+                copies.start(goes & last, group, s, targets, below, device)
+                copies.start(goes & jnp.logical_not(last), group, s, targets, some, device)
+
     def corner(self, j):
         if not self.use_x or not 0 <= j < self.n_planes:
             return
         s, cut = self.order[j], self.cut
         twin, mine = self.ready(T_YX, j)
-        for m, t in zip(mine, twin):
-            add_up(t, [m, t])
+        if self.by_z:
+            self.along(j, [[m, t] for m, t in zip(mine, twin)], self.slant, twin, R_DUP, R_DDOWN)
+        else:
+            for m, t in zip(mine, twin):
+                add_up(t, [m, t])
         self.start_load(T_YX, j + 2)
+        if self.by_z and j < self.n_planes - 1:
+            return
+        p = 0 if self.by_z else s
         head = twin if self.second is None else [twin[0].at[pl.ds(0, cut)]] + twin[1:]
-        self.copies.start(None, R_XHALF, s, head, [f.at[s] for f in self.first], self.spot.across)
+        self.copies.start(None, R_XHALF, s, head, [f.at[p] for f in self.first], self.spot.across)
         if self.second is not None:
             tail = [twin[0].at[pl.ds(cut, self.second.shape[1])]]
-            self.copies.start(None, R_YHALF, s, tail, [self.second.at[s]], self.spot.side)
+            self.copies.start(None, R_YHALF, s, tail, [self.second.at[p]], self.spot.side)
 
     def side(self, j):
         s, cut = self.order[j], self.cut
         twin, mine = self.ready(T_Y, j)
-        if self.use_x:
-            first = [f.at[s] for f in self.first]
+        over = self.use_x and (j == self.n_planes - 1 or not self.by_z)
+        p = 0 if self.by_z else s
+        if over:
+            first = [f.at[p] for f in self.first]
             self.copies.arrive(R_XHALF, s, first, self.spot.across)
         for i, (m, t) in enumerate(zip(mine, twin)):
-            if not self.use_x:
+            if not over:
                 add_up(t, [m, t])
             elif i == 0 and self.second is not None:
                 a, b = pl.ds(0, cut), pl.ds(cut, self.second.shape[1])
@@ -1048,13 +1125,15 @@
     def over(self, j):
         s, cut = self.order[j], self.cut
         twin, mine = self.ready(T_X, j)
-        if self.second is not None:
-            self.copies.arrive(R_YHALF, s, [self.second.at[s]], self.spot.side)
+        over = self.second is not None and (j == self.n_planes - 1 or not self.by_z)
+        p = 0 if self.by_z else s
+        if over:
+            self.copies.arrive(R_YHALF, s, [self.second.at[p]], self.spot.side)
         for i, (m, t) in enumerate(zip(mine, twin)):
-            if i == 0 and self.second is not None:
+            if i == 0 and over:
                 a, b = pl.ds(0, cut), pl.ds(cut, self.second.shape[1])
                 add_up(t.at[a], [m.at[a], t.at[a]])
-                add_up(t.at[b], [m.at[b], t.at[b], self.second.at[s]])
+                add_up(t.at[b], [m.at[b], t.at[b], self.second.at[p]])
             else:
                 add_up(t, [m, t])
         self.start_load(T_X, j + 2)
@@ -1069,7 +1148,7 @@
     def column(self, j):
         if not 0 <= j < self.n_planes:
             return
-        s, spot, copies, n = self.order[j], self.spot, self.copies, self.n
+        s, spot, copies = self.order[j], self.spot, self.copies
         twin, mine = self.ready(T_OWN, j)
         near = [t.at[s] for t in self.near]
         copies.arrive(R_YALL, s, near, spot.side)
@@ -1078,37 +1157,7 @@
             across = [t.at[s] for t in self.across]
             copies.arrive(R_XALL, s, across, spot.across)
             here = [h + [a] for h, a in zip(here, across)]
-        line = [t.at[s] for t in self.line]
-
-        def add_all(targets, *more):
-            for i in range(n):
-                add_up(targets[i], here[i] + [m[i] for m in more])
-
-        if j == self.n_planes - 1:
-            below = [t.at[self.n_planes] for t in self.line]
-            when(spot.has_up, lambda: copies.arrive(R_DOWN, s, line, spot.up))
-            when(spot.has_down, lambda: copies.arrive(R_UP, s, below, spot.down))
-            when(spot.has_up & spot.has_down, lambda: add_all(self.outs, line, below))
-            when(spot.z == 0, lambda: add_all(self.outs, line))
-            when(spot.z == self.n_planes - 1, lambda: add_all(self.outs, below))
-            return
-        for goes, more, group, last, device, source in (
-            (s < spot.z, spot.has_up, R_DOWN, None, spot.down, spot.up),
-            (s > spot.z, spot.has_down, R_UP, s - spot.z == 1, spot.up, spot.down),
-        ):
-
-            def partial():
-                copies.arrive(group, s, line, source)
-                add_all(twin, line)
-
-            when(goes & more, partial)
-            when(goes & jnp.logical_not(more), lambda: add_all(twin))
-            if last is None:
-                copies.start(goes, group, s, twin, line, device)
-            else:
-                below = [t.at[self.n_planes] for t in self.line]
-                copies.start(goes & last, group, s, twin, below, device)
-                copies.start(goes & jnp.logical_not(last), group, s, twin, line, device)
+        self.along(j, here, self.line, self.outs if j == self.n_planes - 1 else twin, R_UP, R_DOWN)
         self.start_load(T_OWN, j + 2)
 
     def stage(self, step):
@@ -1270,16 +1319,18 @@
 
 def back_kernel(n_planes, axes, *refs):
     n = len(axes)
-    (
-        grad_own, mixed, normed_one, query, key, value, probs, wq, wk, wv, wo, cosine, sine, tokens, grad_residual,
-        gain, small, parts,
-    ) = refs[:18]
+    grad_own, *inputs = refs[:18]
+    probs, wq, wk, wv, wo, parts = inputs[5], *inputs[6:10], inputs[16]
+    inputs = inputs[:5] + inputs[10:16]
+    held = refs[-len(inputs) - 1 : -1]
+    mixed, normed_one, query, key, value, cosine, sine, tokens, grad_residual, gain, small = held
+    held_load = refs[-1]
     outs, grad_tokens, small_out, out_sum = refs[18 : 18 + n], *refs[18 + n : 21 + n]
     (
         grad_attn, grad_mixed, grad_query, grad_key, grad_value, gq, gk, gv, go, some_p, some_o, some_q, some_k,
         some_v, sent, received, terms, small_sum, small_in, load, x_send, x_recv,
     ) = refs[21 + n : 43 + n]
-    scratch = refs[43 + n :]
+    scratch = refs[43 + n : -len(inputs) - 1]
     spot = Spot(n_planes)
     x = spot.x
     bf16, f32 = jnp.bfloat16, jnp.float32
@@ -1305,7 +1356,7 @@
     count = 3 * n + 3
     weights = Reduce(spot, weight_blocks, outs, scratch[:count], False, direct=True)
     params = Reduce(spot, small_blocks, [small_sum], scratch[count : count + 6], False, direct=True)
-    sums = Reduce(spot, token_blocks, [out_sum], scratch[count + 6 :], True, own_rows)
+    sums = Reduce(spot, token_blocks, [out_sum], scratch[count + 6 :], True, own_rows // 2, by_z=True)
 
     def swap(i, src, dst):
         return pltpu.make_async_remote_copy(
@@ -1319,7 +1370,9 @@
     spot.greet()
     swap(0, grad_own, grad_attn.at[x]).start()
     sums.start_twins()
-    terms[...] = small[...]
+    fetched = [pltpu.make_async_copy(a, b, held_load.at[i]) for i, (a, b) in enumerate(zip(inputs, held))]
+    for c in fetched:
+        c.start()
 
     heads, head_dim = probs.shape[0], cosine.shape[1]
     kv_heads = key.shape[1] // head_dim
@@ -1338,6 +1391,11 @@
     load_p(0).start()
     sums.corner(0)
     sums.sides(0)
+    sums.corner(1)
+    sums.sides(1)
+    for c in fetched:
+        c.wait()
+    terms[...] = small[...]
     own.wait()
     swap(0, grad_attn.at[1 - x], grad_attn.at[1 - x]).wait_recv()
     whole = grad_attn[...].reshape(2 * own_rows, model)
@@ -1350,8 +1408,9 @@
         span = slice(c * chunk, (c + 1) * chunk)
         grad_mixed[:, span] = plain_dot(whole, some_o[c % 2], ROWS_ROWS).astype(bf16)
         go[span, :] = plain_dot(mixed[:, span], whole, COLUMNS_COLUMNS).astype(bf16)
-    sums.corner(1)
-    sums.sides(1)
+    sums.corner(2)
+    sums.sides(2)
+    sums.column(0)
     for h in range(heads):
         if h + 1 < heads:
             load_p(h + 1).start()
@@ -1373,6 +1432,8 @@
         if h % group == group - 1:
             grad_key[:, shared] = turn(total_k, cos, sin).astype(bf16)
             grad_value[:, shared] = total_v.astype(bf16)
+    sums.corner(3)
+    sums.column(1)
     for target, source in ((gk, grad_key), (gv, grad_value), (gq, grad_query)):
         target[...] = plain_dot(normed_one[...], source[...], COLUMNS_COLUMNS).astype(bf16)
     weights.start_twins()
@@ -1389,10 +1450,8 @@
 
     for c in load_w(0):
         c.start()
-    sums.column(0)
-    sums.corner(2)
-    sums.sides(2)
     weights.sides(0)
+    sums.sides(3)
     other = pl.ds(pl.multiple_of((1 - x) * own_rows, own_rows), own_rows)
     mine = pl.ds(pl.multiple_of(x * own_rows, own_rows), own_rows)
     for c in range(n_chunks):
@@ -1408,10 +1467,8 @@
             total = total + plain_dot(grad_value[here, :], some_v[c % 2], ROWS_ROWS)
             target[:, columns] = total.astype(target.dtype)
     swap(1, sent, received).start()
-    sums.column(1)
-    sums.corner(3)
-    sums.sides(3)
     weights.sides(1)
+    sums.column(2)
     swap(1, received, received).wait_recv()
     step = 32
     gain_row = gain[...].astype(f32)
@@ -1428,13 +1485,12 @@
     place = small.shape[0] - 8
     terms[pl.ds(place, 1), :] = total
     params.start_twins()
-    sums.column(2)
     weights.column(0)
     weights.sides(2)
     params.sides(0)
-    sums.column(3)
     weights.column(1)
     weights.sides(3)
+    sums.column(3)
     for j in range(1, n_planes):
         params.sides(j)
         params.column(j - 1)
@@ -1475,7 +1531,7 @@
     return pl.pallas_call(
         functools.partial(back_kernel, n_planes, axes),
         out_shape=[shape(s, f32) for s in shapes] + [shape((own_rows, model), f32), shape(tile, f32), shape(block, f32)],
-        in_specs=[ANY] + [vmem] * 5 + [ANY] * 5 + [vmem] * 6 + [ANY],
+        in_specs=[ANY] * 18,
         out_specs=[vmem] * (n + 3),
         scratch_shapes=[
             vmem_ref((2, own_rows, model), bf16),
@@ -1502,7 +1558,12 @@
         ]
         + Reduce.scratch(shapes, [bf16] * n, n_planes, False, direct=True)
         + Reduce.scratch([tile], [f32], n_planes, False, direct=True)
-        + Reduce.scratch([block], [parts.dtype], n_planes, True, block[0]),
+        + Reduce.scratch([block], [parts.dtype], n_planes, True, block[0] // 2, by_z=True)
+        + [
+            vmem_ref(a.shape, a.dtype)
+            for a in (mixed, normed_one, query, key, value, cosine, sine, tokens, grad_residual, gain, small)
+        ]
+        + [dma((11,))],
         compiler_params=pltpu.CompilerParams(
             collective_id=collective_id, has_side_effects=True, vmem_limit_bytes=63 << 20
         ),
@@ -1591,7 +1652,6 @@
             for source, target in ((self.tokens, self.rows), (self.grads, self.grad_rows)):
                 whole = source[slot, pl.ds(2 * q, 2)].reshape(seq, model)
                 target[slot, span] = dot_f32(low, whole).astype(bf16)
-        hook(1)
         row_gate = jnp.concatenate(row_gates, axis=0)
         rows, grad_rows = self.rows.at[slot], self.grad_rows.at[slot]
         self.pre[0] = dot_f32(rows[...], self.w_gate[...])
@@ -1657,19 +1717,16 @@
                 out = dot_f32(self.left_grad[q], self.right_grad[q, :, cols]).astype(bf16)
                 self.back[slot, pl.ds(2 * q, 2), :, cols] = out.reshape(2, own_rows, column)
 
-            @pl.when(c == n_columns // 2)
-            def _():
-                hook(4)
-
             return carry
 
         lax.fori_loop(0, n_columns, combine, 0)
 
 
 def expert_kernel(n_dp, *refs):
-    own, own_gates, _, w_gate, w_up, w_down, shared = refs[:7]
+    own, own_gates, _, *weights_in = refs[:7]
     normed, grads, out_parts, back_parts, grad_gates, rows_out, grad_rows_out, hidden_out, shared_out = refs[7:16]
-    scratch, (gates, load, store, local, send, recv, g_send, g_recv) = refs[16:-8], refs[-8:]
+    scratch, weights = refs[16:-13], refs[-13:-9]
+    fetch, gates, load, store, local, send, recv, g_send, g_recv = refs[-9:]
     n_planes = n_dp // 4
     spot = Spot(n_planes)
     half = own.shape[0] // 2
@@ -1694,13 +1751,21 @@
     ]
     for c in kept:
         c.start()
+    pieces = 4
+    fetched = []
+    for k, (a, b) in enumerate(zip(weights_in, weights)):
+        size = a.shape[0] // pieces
+        for p in range(pieces):
+            span = pl.ds(p * size, size)
+            fetched.append(pltpu.make_async_copy(a.at[span], b.at[span], fetch.at[k, p]))
+    for c in fetched:
+        c.start()
     spot.greet()
     copies = Copies(n_planes, send, recv)
-    net = Spread(spot, copies, [own, own_gates], views, True)
+    net = Spread(spot, copies, [own, own_gates], views, True, by_z=True)
     rest = Spread(spot, Copies(n_planes, g_send, g_recv), None, grad_views, True)
     net.begin()
-    work = ExpertWork(spot.dp, (w_gate, w_up, w_down, shared), scratch)
-    work.prepare()
+    work = ExpertWork(spot.dp, weights, scratch)
     n_units = n_dp // UNIT
     blocks = 2 * UNIT
     rows = work.rows.shape[1]
@@ -1755,45 +1820,33 @@
         rest.over_x(j)
         rest.over_y(j)
 
-    middle = spot.has_up & spot.has_down
-    end = jnp.logical_not(middle)
-
-    goes = {
-        (j, c): (net.goes_down[j] & (middle if c else end), net.goes_up[j] & (middle if c else end))
-        for j in range(1, n_planes)
-        for c in (0, 1)
-    }
-
-    def relay(j, c):
-        pl.when(middle if c else end)(functools.partial(net.relay, j, goes[j, c]))
-
     plan = {
         (0, 0): [(net.onward, 1)],
-        (0, 1): [(net.corner, 0)],
-        (0, 2): [(rest.corner, 0), (far, 0), (over, 1)],
-        (0, 4): [(relay, 2, 0), (relay, 3, 1)],
-        (1, 0): [(net.sides, 1)],
-        (1, 1): [(net.onward, 2), (rest.onward_y, 3)],
+        (0, 2): [(net.corner, 0), (rest.corner, 0), (far, 0), (over, 1)],
+        (0, 3): [(net.relay_of, 2, 0), (net.relay_of, 3, 1)],
+        (1, 0): [(net.sides, 1), (net.onward, 2), (rest.onward_y, 3)],
         (1, 2): [(near, 1)],
-        (1, 3): [(net.corner, 1), (rest.corner, 1)],
+        (1, 3): [(net.corner, 1), (net.corner_of, 2, 1), (rest.corner, 1)],
         (2, 0): [(far, 1), (over, 2)],
-        (2, 3): [(net.sides, 2), (relay, 3, 0)],
-        (2, 4): [(net.onward, 3)],
+        (2, 3): [(net.sides, 2), (net.relay_of, 3, 0), (net.onward, 3), (net.corner_of, 3, 1)],
         (3, 0): [(near, 2), (over, 3)],
-        (3, 1): [(net.corner, 2), (rest.corner, 2)],
+        (3, 2): [(net.corner_of, 2, 0), (rest.corner, 2)],
         (4, 0): [(net.sides, 3), (far, 2)],
-        (4, 3): [(net.corner, 3), (rest.corner, 3)],
+        (4, 3): [(net.corner_of, 3, 0), (rest.corner, 3)],
         (5, 0): [(near, 3)],
         (6, 0): [(far, 3)],
     }
 
     net.relay(1)
-    relay(2, 1)
+    net.relay_of(2, 1)
     net.sides(0)
     over(0)
     for c in kept:
         c.wait()
     near(0)
+    for c in fetched:
+        c.wait()
+    work.prepare()
 
     def body(i, carry):
         slot = i % 2
@@ -1854,19 +1907,21 @@
             jax.ShapeDtypeStruct((3, rows, width), bf16),
             jax.ShapeDtypeStruct((blocks * own_rows, 384), bf16),
         ],
-        in_specs=[ANY, ANY, ANY, vmem, vmem, vmem, vmem],
+        in_specs=[ANY] * 7,
         out_specs=[ANY, ANY, ANY, ANY, vmem, ANY, ANY, ANY, ANY],
         input_output_aliases={2: 1},
         scratch_shapes=ExpertWork.scratch(model, width, capacity, own_rows)
+        + [pltpu.VMEM(w.shape, bf16) for w in (w_gate, w_up, w_down, shared)]
         + [
+            pltpu.SemaphoreType.DMA((4, 4)),
             pltpu.VMEM(all_gates, jnp.float32),
             pltpu.SemaphoreType.DMA((2, 2)),
             pltpu.SemaphoreType.DMA((2, 6)),
             pltpu.SemaphoreType.DMA((2,)),
-            pltpu.SemaphoreType.DMA((11 * n_planes, 2)),
-            pltpu.SemaphoreType.DMA((11 * n_planes, 2)),
-            pltpu.SemaphoreType.DMA((11 * n_planes, 1)),
-            pltpu.SemaphoreType.DMA((11 * n_planes, 1)),
+            pltpu.SemaphoreType.DMA((14 * n_planes, 2)),
+            pltpu.SemaphoreType.DMA((14 * n_planes, 2)),
+            pltpu.SemaphoreType.DMA((14 * n_planes, 1)),
+            pltpu.SemaphoreType.DMA((14 * n_planes, 1)),
         ],
         compiler_params=pltpu.CompilerParams(
             collective_id=collective_id, has_side_effects=True, vmem_limit_bytes=60 << 20

time: 659 us -> 613 us (0.930)
  Pallas kernels: 581 us -> 533 us
    pallas_call x1, Pallas kernels: 154 us -> 133 us  [expert_call(): pl.pallas_call(functools.partial(expert_kernel, n_dp), out_shape=[everyon...]
    pallas_call x1, Pallas kernels: 194 us -> 178 us  [backward(): pl.pallas_call(functools.partial(back_kernel, n_planes, axes), out_shape=...]
    pallas_call x1, Pallas kernels: 153 us -> 142 us  [front(): pl.pallas_call(functools.partial(front_kernel, n_planes, axes), out_shape...]
  transfers between devices with their start and end apart: 2 -> 2, of which waited for: 0 -> 0; matrix products, arithmetic and copies ran while one was open for 5% -> 6% of each run, Pallas kernels for 53% -> 53%
where the time goes in v4:
time: 613 us; the launch traced here: 603 us
  Pallas kernels  533 us (87%)
  local copies, waits for them, and re-layouts  44.9 us (7%)
  starting transfers between devices  12.4 us (2%)
  other arithmetic  10.6 us (2%)
    pallas_call x1, Pallas kernels, backward(): pl.pallas_call(functools.partial(back_kernel, n_planes, axes), out_shape=...  178 us
    pallas_call x1, Pallas kernels, front(): pl.pallas_call(functools.partial(front_kernel, n_planes, axes), out_shape...  142 us
    pallas_call x1, Pallas kernels, expert_call(): pl.pallas_call(functools.partial(expert_kernel, n_dp), out_shape=[everyon...  133 us
    pallas_call x1, Pallas kernels, sum_everywhere(): pl.pallas_call(functools.partial(sum_kernel, n_planes, n), out_shape=[jax...  79.8 us
    unnamed x61, local copies, waits for them, and re-layouts  36.9 us
  transfers between devices with their start and end apart: 2, of which 0 were waited for; matrix products, arithmetic and copies ran while one was open for 6% of the time, Pallas kernels for 53%

profile of v4, /device:TPU:24, one launch (start us, length us, event | category | flops | bytes accessed | tf_op | source)
XLA Modules:
  0.0 603.3 jit_solution(11342344417842901935)
XLA Ops:
  0.7 1.2 copy.94
  1.9 1.2 copy.93
  3.4 1.1 copy.95
  4.5 6.1 %all-to-all-start = ((bf16[16,3,96,128]{3,2,1,0:T(8,128)(2,1)}), bf16[16,3,96,128]{3,2,1,0:T(8,128)(2,1)S(1)}, u32[]{:S(2)}, u32[]{:S(2)}) async-start(bf16[16,3,96,128]{3,2,1,0:T(8,128)(2,1)} %copy.95), calls=%async_computation | async-start | bytes 2359296 | tf_op jit(solution)/shard_map/all_to_all | solution.py:2001
  11.4 4.6 copy.91
  16.0 4.6 copy.92
  21.5 0.8 pad_maximum_fusion.1
  22.4 0.8 fusion.1.refs_10_
  23.2 142.3 %shard_map.280 = (bf16[2048,1024]{1,0:T(8,128)(2,1)}, bf16[2048,256]{1,0:T(8,128)(2,1)}, bf16[2048,256]{1,0:T(8,128)(2,1)}, bf16[1024,2048]{1,0:T(8,128)(2,1)}, ...) custom-call(bf16[128,1024]{1,0:T(8,128)(2,1)} %refs_0_.1, ...), custom_call_target="tpu_custom_call" | custom-call | flops 3221225472 | bytes 67108864 | tf_op jit(solution)/shard_map/pallas_call | solution.py:909
  165.5 1.4 multiply_reduce_fusion.2
  166.9 1.4 slice_convert_fusion
  168.5 1.3 pad.20
  169.8 132.8 %shard_map.281 = (bf16[32,128,2048]{2,1,0:T(8,128)(2,1)}, bf16[32,128,2048]{2,1,0:T(8,128)(2,1)}, bf16[32,128,2048]{2,1,0:T(8,128)(2,1)}, bf16[32,128,2048]{2,1,...) custom-call(bf16[128,2048]{1,0:T(8,128)(2,1)} %get-tuple-element.65., ...), custom_call_target="tpu_custom_call", output_to_operand_aliasing={{1}: (2, {})} | custom-call | tf_op jit(solution)/shard_map/pallas_call | solution.py:1897
  302.6 79.8 %shard_map.282 = (f32[128,2048]{1,0:T(8,128)}, f32[16,128]{1,0:T(8,128)}, f32[2048,704]{1,0:T(8,128)}, f32[2048,704]{1,0:T(8,128)}, f32[704,2048]{1,0:T(8,128)}, /*index=5*/bf16[384,2048]{1,0:T(8,128)(2,1)}) custom-call(bf16[32,128,2048]{2,1,0:T(8,128)(2,1)} %get-tuple-element.68.refs_0_, f32[32,16,128]{2,1,0:T(8,128)} %get-tuple-element.69.refs_1_, ...), custom_call_target="tpu_custom_call" | custom-call | tf_op jit(solution)/shard_map/pallas_call | solution.py:1301
  382.5 1.4 slice.61
  384.3 1.3 copy.97
  385.7 6.4 %all-to-all-start.1 = ((bf16[16,3,96,128]{3,2,1,0:T(8,128)(2,1)}), bf16[16,3,96,128]{3,2,1,0:T(8,128)(2,1)}, u32[]{:S(2)}, u32[]{:S(2)}) async-start(bf16[16,3,96,128]{3,2,1,0:T(8,128)(2,1)} %copy.97), calls=%async_computation.1 | async-start | bytes 2359296 | tf_op jit(solution)/shard_map/all_to_all | solution.py:2046
  392.9 0.7 select_maximum_fusion.refs_16_
  393.6 1.5 fusion.10
  395.1 178.5 %shard_map.283 = (f32[128,1024]{1,0:T(8,128)}, f32[128,256]{1,0:T(8,128)}, f32[128,256]{1,0:T(8,128)}, f32[1024,128]{1,0:T(8,128)}, f32[128,2048]{1,0:T(8,128)}, /*index=5*/f32[24,128]{1,0:T(8,128)}, f32[128,2048]{1,0:T(8,128)}) custom-call(bf16[128,2048]{1,0:T(8,128)(2,1)} %get-tuple-element.193.refs_0_, bf16[256,1024]{1,0:T(8,128)(2,1)} %get-tuple-element.79.refs_1_, ...), custom_call_target="tpu_custom_call" | custom-call | flops 6442450944 | bytes 67108864 | tf_op jit(solution)/shard_map/pallas_call | solution.py:1531
  573.6 6.4 %copy.101 = f32[1,2048,704]{1,2,0:T(8,128)} copy(f32[1,2048,704]{2,1,0:T(8,128)} %bitcast.79) | data formatting | bytes 11534336
  580.0 6.5 %copy.102 = f32[1,2048,704]{1,2,0:T(8,128)} copy(f32[1,2048,704]{2,1,0:T(8,128)} %bitcast.78) | data formatting | bytes 11534336
  587.1 0.7 dynamic-slice_bitcast_fusion
  587.8 0.9 add_convert_fusion
  588.7 1.4 convert_bitcast_fusion
  590.0 1.0 fusion.11
  591.0 1.1 copy.100
  592.2 1.1 copy.99
  593.3 1.0 copy.116
  594.3 0.8 copy.117
  596.4 0.8 copy.120
  597.2 5.9 copy.121
  (75 shorter events, 5.3 us)
Async XLA Ops:
  0.6 9.9 %copy-start = (s32[256,6]{0,1:T(8,128)S(1)}, s32[256,6]{0,1:T(8,128)}, u32[]{:S(2)}) copy-start(s32[256,6]{0,1:T(8,128)} %param.34) | copy-start | bytes 18436
  0.7 2.5 copy-start.11
  3.4 7.8 %copy-start.22 = (s32[1,4]{1,0:T(1,128)S(1)}, s32[1,4]{1,0:T(1,128)}, u32[]{:S(2)}) copy-start(s32[1,4]{1,0:T(1,128)} %param.33) | copy-start | bytes 52
  4.5 163.8 %all-to-all-start = ((bf16[16,3,96,128]{3,2,1,0:T(8,128)(2,1)}), bf16[16,3,96,128]{3,2,1,0:T(8,128)(2,1)S(1)}, u32[]{:S(2)}, u32[]{:S(2)}) async-start(bf16[16,3,96,128]{3,2,1,0:T(8,128)(2,1)} %copy.95), calls=%async_computation | async-start | bytes 2359296 | tf_op jit(solution)/shard_map/all_to_all | solution.py:2001
  16.0 4.7 copy-start.19
  16.0 4.7 copy-start.20
  16.0 4.7 copy-start.21
  20.9 2.3 copy-start.17
  384.3 7.7 %copy-start.14 = (f32[16,128]{1,0:T(8,128)S(1)}, f32[16,128]{1,0:T(8,128)}, u32[]{:S(2)}) copy-start(f32[16,128]{1,0:T(8,128)} %get-tuple-element.66.refs_1_) | copy-start | bytes 24580
  384.3 7.7 %copy-start.16 = (f32[16,128]{1,0:T(8,128)S(1)}, f32[16,128]{1,0:T(8,128)}, u32[]{:S(2)}) copy-start(f32[16,128]{1,0:T(8,128)} %get-tuple-element.77) | copy-start | bytes 24580
  384.3 7.7 %copy-start.4 = (bf16[128,2048]{1,0:T(8,128)(2,1)S(1)}, bf16[128,2048]{1,0:T(8,128)(2,1)}, u32[]{:S(2)}) copy-start(bf16[128,2048]{1,0:T(8,128)(2,1)} %get-tuple-element.65.refs_0_) | copy-start | bytes 1572868
  385.7 6.6 %copy-start.2 = (f32[128,2048]{1,0:T(8,128)S(1)}, f32[128,2048]{1,0:T(8,128)}, u32[]{:S(2)}) copy-start(f32[128,2048]{1,0:T(8,128)} %get-tuple-element.64) | copy-start | bytes 3145732
  385.7 6.6 %copy-start.5 = (f32[128,2048]{1,0:T(8,128)S(1)}, f32[128,2048]{1,0:T(8,128)}, u32[]{:S(2)}) copy-start(f32[128,2048]{1,0:T(8,128)} %get-tuple-element.76) | copy-start | bytes 3145732
  385.7 6.6 %copy-start.15 = (bf16[32,2048]{1,0:T(8,128)(2,1)S(1)}, bf16[32,2048]{1,0:T(8,128)(2,1)}, u32[]{:S(2)}) copy-start(bf16[32,2048]{1,0:T(8,128)(2,1)} %get-tuple-element.78) | copy-start | bytes 393220
  385.7 203.0 %all-to-all-start.1 = ((bf16[16,3,96,128]{3,2,1,0:T(8,128)(2,1)}), bf16[16,3,96,128]{3,2,1,0:T(8,128)(2,1)}, u32[]{:S(2)}, u32[]{:S(2)}) async-start(bf16[16,3,96,128]{3,2,1,0:T(8,128)(2,1)} %copy.97), calls=%async_computation.1 | async-start | bytes 2359296 | tf_op jit(solution)/shard_map/all_to_all | solution.py:2046
  392.1 1.5 copy-start.8
  580.0 6.5 %copy-start.18 = (f32[24,128]{1,0:T(8,128)S(1)}, f32[24,128]{1,0:T(8,128)}, u32[]{:S(2)}) copy-start(f32[24,128]{1,0:T(8,128)} %get-tuple-element.92) | copy-start | bytes 36868
  580.0 7.8 %copy-start.3 = (f32[128,2048]{1,0:T(8,128)S(1)}, f32[128,2048]{1,0:T(8,128)}, u32[]{:S(2)}) copy-start(f32[128,2048]{1,0:T(8,128)} %get-tuple-element.64) | copy-start | bytes 3145732
  580.0 7.8 %copy-start.7 = (f32[128,2048]{1,0:T(8,128)S(1)}, f32[128,2048]{1,0:T(8,128)}, u32[]{:S(2)}) copy-start(f32[128,2048]{1,0:T(8,128)} %get-tuple-element.90) | copy-start | bytes 3145732
  591.0 2.3 copy-start.6
  592.2 2.1 copy-start.10
  592.2 2.9 copy-start.13
  592.2 3.6 copy-start.12
  593.3 3.1 copy-start.9
  597.2 5.9 copy-start.1

commit v5 on v4

--- a/solution.py
+++ b/solution.py
@@ -671,11 +671,16 @@
             self.copies.start(spot.has_up, D_UP, s, whole, whole, spot.up)
             self.copies.start(spot.has_down, D_DOWN, s, whole, whole, spot.down, D_UP)
 
+    def twin_own(self, j):
+        self.copies.arrive(C_OWN, self.order[j], self.twins[j][0], self.spot.twin)
+
+    def twin_across(self, j):
+        self.copies.arrive(C_X, self.order[j], self.twins[j][3], self.spot.twin)
+
     def twin_near(self, j):
-        s, there, spot = self.order[j], self.twins[j], self.spot
-        self.copies.arrive(C_OWN, s, there[0], spot.twin)
+        self.twin_own(j)
         if self.use_x:
-            self.copies.arrive(C_X, s, there[3], spot.twin)
+            self.twin_across(j)
 
     def twin_side(self, j):
         self.copies.arrive(C_Y, self.order[j], self.twins[j][1], self.spot.twin)
@@ -731,13 +736,13 @@
     n = len(axes)
     shards_in, (tokens, tile, grads, chosen, cosine, sine, allowed) = refs[:n], refs[n : n + 7]
     outs = refs[n + 7 : 2 * n + 7]
-    (
-        all_grads, params, normed_one, query, key, value, probs, mixed, residual, normed_two, gates,
-    ) = refs[2 * n + 7 : 2 * n + 18]
+    all_grads, params, *kept_out, residual, normed_two, gates = refs[2 * n + 7 : 2 * n + 18]
+    normed_one, query, key, value, probs, mixed = refs[-7:-1]
+    out_sems = refs[-1]
     (
         wq, wk, wv, wo, sequence, pair, sent, received, w_send, w_recv, p_send, p_recv, g_send, g_recv, local,
-        load, x_send, x_recv,
-    ) = refs[2 * n + 18 :]
+        x_send, x_recv,
+    ) = refs[2 * n + 18 : -7]
     spot = Spot(n_planes)
     x = spot.x
     bf16, f32 = jnp.bfloat16, jnp.float32
@@ -746,7 +751,7 @@
     def weight_views(s, yy, cc, xx, part):
         i = dp_of(s, yy, cc)
         places = []
-        for o, a, axis in zip(outs, shards_in, axes):
+        for o, a, axis in zip((wq, wk, wv, wo), shards_in, axes):
             size = a.shape[axis]
             span = pl.ds(pl.multiple_of(i * size, size), size)
             places.append(o.at[span] if axis == 0 else o.at[:, span])
@@ -815,14 +820,13 @@
             scale = lax.rsqrt(jnp.mean(rows * rows, axis=1, keepdims=True) + norm_eps)
             normed_one[pl.ds(h * own_rows + r * step, step)] = (rows * scale * first_gain).astype(bf16)
     weights.twin_all()
-    loads = [pltpu.make_async_copy(a, b, load.at[i]) for i, (a, b) in enumerate(zip(outs, (wq, wk, wv, wo)))]
-    for c in loads:
+    pairs = list(zip((wq, wk, wv, wo), outs)) + list(zip((normed_one, query, key, value, probs, mixed), kept_out))
+    written = [pltpu.make_async_copy(a, b, out_sems.at[i]) for i, (a, b) in enumerate(pairs)]
+    for c in written[: n + 1]:
         c.start()
     heads, head_dim = query.shape[1] // cosine.shape[1], cosine.shape[1]
     kv_heads = key.shape[1] // head_dim
     group = heads // kv_heads
-    for c in loads[:3]:
-        c.wait()
     cos, sin = cosine[...], sine[...]
     raw = plain_dot(normed_one[...], wk[...], ROWS_COLUMNS)
     for g in range(kv_heads):
@@ -850,17 +854,16 @@
         weight = weight / jnp.sum(weight, axis=1, keepdims=True)
         probs[h] = weight
         mixed[:, span] = plain_dot(weight.astype(bf16), value[:, shared], ROWS_COLUMNS).astype(bf16)
-    loads[3].wait()
+    for c in written[n + 1 :]:
+        c.start()
     other = mixed[pl.ds(pl.multiple_of((1 - x) * own_rows, own_rows), own_rows), :]
     sent[...] = plain_dot(other, wo[...], ROWS_COLUMNS).astype(bf16)
     swaps[2].start()
     other = mixed[pl.ds(pl.multiple_of(x * own_rows, own_rows), own_rows), :]
     residual[...] = plain_dot(other, wo[...], ROWS_COLUMNS)
+    net.relay_of(3, 0)
+    net.onward_twin(3)
     net.from_side(1)
-    net.onward_y(2)
-    net.relay_of(3, 0)
-    net.onward_x(3)
-    net.onward_twin(3)
     net.from_across(2)
     swap(2, received, received).wait_recv()
     second_gain = params[experts + 1 : experts + 2, :].astype(f32)
@@ -876,16 +879,18 @@
     weight = jnp.where(picked, jnp.exp(jnp.where(picked, logits - top, 0.0)), 0.0)
     gates[...] = weight / jnp.sum(weight, axis=0, keepdims=True)
 
-    net.from_side(2)
-    net.from_across(3)
     for j in range(n_planes):
-        net.twin_near(j)
+        net.twin_own(j)
         if j < n_planes - 1:
+            net.twin_across(j)
+        if j < n_planes - 2:
             net.twin_side(j)
     for each in (weights, small, net):
         each.copies.close()
     for c in swaps:
         c.wait_send()
+    for c in written:
+        c.wait()
 
 
 def front(arrays, axes, tokens, tile, grads, chosen, cosine, sine, allowed, n_dp, collective_id):
@@ -923,7 +928,7 @@
             shape((experts, own_rows), f32),
         ],
         in_specs=[ANY] * (n + 3) + [vmem] * 4,
-        out_specs=[ANY] * (n + 1) + [vmem] * 10,
+        out_specs=[ANY] * (n + 1) + [vmem] + [ANY] * 6 + [vmem] * 3,
         scratch_shapes=[pltpu.VMEM(g.shape, bf16) for g in gathered]
         + [
             pltpu.VMEM((2, own_rows, model), bf16),
@@ -933,7 +938,16 @@
         ]
         + [dma((14 * n_planes, n))] * 2
         + [dma((14 * n_planes, 1))] * 4
-        + [dma((n + 3,)), dma((n,)), dma((3,)), dma((3,))],
+        + [dma((n + 3,)), dma((3,)), dma((3,))]
+        + [
+            pltpu.VMEM((seq, model), bf16),
+            pltpu.VMEM((seq, wide), bf16),
+            pltpu.VMEM((seq, narrow_), bf16),
+            pltpu.VMEM((seq, narrow_), bf16),
+            pltpu.VMEM((heads, seq, seq), f32),
+            pltpu.VMEM((seq, wide), bf16),
+            dma((n + 6,)),
+        ],
         compiler_params=pltpu.CompilerParams(
             collective_id=collective_id, has_side_effects=True, vmem_limit_bytes=56 << 20
         ),
@@ -1176,7 +1190,7 @@
         self.sources, (self.hidden, self.shared) = ins[:4], ins[4:]
         self.outs = outs
         self.buffers, self.small_hidden, self.small_shared = scratch[:4], scratch[4], scratch[5]
-        self.tall, self.flat, self.sums, self.load, self.store, self.once = scratch[6:]
+        self.flat, self.sums, self.load, self.store, self.once = scratch[6:]
         self.n_parts = self.sources[0].shape[1] // self.width
 
     @staticmethod
@@ -1190,8 +1204,7 @@
             pltpu.VMEM((2, tokens, w), bf16),
             pltpu.VMEM((3, rows, width), bf16),
             pltpu.VMEM((tokens, shared), bf16),
-            pltpu.VMEM((2, 2, w, width), f32),
-            pltpu.VMEM((2, width, w), f32),
+            pltpu.VMEM((2, 3, width, w), f32),
             pltpu.VMEM((2, shared, w), bf16),
             pltpu.SemaphoreType.DMA((2, 4)),
             pltpu.SemaphoreType.DMA((2, 4)),
@@ -1208,12 +1221,12 @@
         ]
 
     def stores(self, p):
-        gate, up, down, shared = self.outs
+        gate_t, up_t, down, shared = self.outs
         slot, span = p % 2, self.span(p)
         pairs = [
-            (self.tall.at[slot, 0], gate.at[span]),
-            (self.tall.at[slot, 1], up.at[span]),
-            (self.flat.at[slot], down.at[:, span]),
+            (self.flat.at[slot, 0], gate_t.at[:, span]),
+            (self.flat.at[slot, 1], up_t.at[:, span]),
+            (self.flat.at[slot, 2], down.at[:, span]),
             (self.sums.at[slot], shared.at[:, span]),
         ]
         return [pltpu.make_async_copy(a, b, self.store.at[slot, i]) for i, (a, b) in enumerate(pairs)]
@@ -1248,9 +1261,9 @@
         def across(a, b):
             return lax.dot_general(a, b, (((0,), (0,)), ((), ())), preferred_element_type=jnp.float32)
 
-        self.tall[slot, 0] = across(rows[...], self.small_hidden[1])
-        self.tall[slot, 1] = across(rows[...], self.small_hidden[2])
-        self.flat[slot] = across(self.small_hidden[0], grad_rows[...])
+        self.flat[slot, 0] = across(self.small_hidden[1], rows[...])
+        self.flat[slot, 1] = across(self.small_hidden[2], rows[...])
+        self.flat[slot, 2] = across(self.small_hidden[0], grad_rows[...])
         n = self.small_shared.shape[1] // 3
         self.sums[slot, pl.ds(0, 2 * n)] = across(self.small_shared[:, n:], tokens[...]).astype(jnp.bfloat16)
         self.sums[slot, pl.ds(2 * n, n)] = across(self.small_shared[:, :n], grads[...]).astype(jnp.bfloat16)
@@ -1266,7 +1279,7 @@
 def sum_kernel(n_planes, n, *refs):
     ins, work_ins, outs, work_outs = refs[:n], refs[n : n + 6], refs[n + 6 : 2 * n + 6], refs[2 * n + 6 : 2 * n + 10]
     scratch = refs[2 * n + 10 :]
-    cut = len(scratch) - 12
+    cut = len(scratch) - 11
     spot = Spot(n_planes)
     rows = ins[0].shape[1] // 2
 
@@ -1302,8 +1315,8 @@
         functools.partial(sum_kernel, n_planes, n),
         out_shape=[jax.ShapeDtypeStruct(s, t) for s, t in zip(shapes, out_dtypes)]
         + [
-            jax.ShapeDtypeStruct((model, width), jnp.float32),
-            jax.ShapeDtypeStruct((model, width), jnp.float32),
+            jax.ShapeDtypeStruct((width, model), jnp.float32),
+            jax.ShapeDtypeStruct((width, model), jnp.float32),
             jax.ShapeDtypeStruct((width, model), jnp.float32),
             jax.ShapeDtypeStruct((shared, model), jnp.bfloat16),
         ],
@@ -1390,15 +1403,15 @@
     load_o(0).start()
     load_p(0).start()
     sums.corner(0)
-    sums.sides(0)
-    sums.corner(1)
-    sums.sides(1)
+    for j in range(n_planes - 1):
+        sums.sides(j)
     for c in fetched:
         c.wait()
     terms[...] = small[...]
     own.wait()
     swap(0, grad_attn.at[1 - x], grad_attn.at[1 - x]).wait_recv()
     whole = grad_attn[...].reshape(2 * own_rows, model)
+    sums.corner(1)
     cos, sin = cosine[...], -sine[...]
     scale = head_dim ** -0.5
     for c in range(n_chunks):
@@ -1409,8 +1422,6 @@
         grad_mixed[:, span] = plain_dot(whole, some_o[c % 2], ROWS_ROWS).astype(bf16)
         go[span, :] = plain_dot(mixed[:, span], whole, COLUMNS_COLUMNS).astype(bf16)
     sums.corner(2)
-    sums.sides(2)
-    sums.column(0)
     for h in range(heads):
         if h + 1 < heads:
             load_p(h + 1).start()
@@ -1433,7 +1444,6 @@
             grad_key[:, shared] = turn(total_k, cos, sin).astype(bf16)
             grad_value[:, shared] = total_v.astype(bf16)
     sums.corner(3)
-    sums.column(1)
     for target, source in ((gk, grad_key), (gv, grad_value), (gq, grad_query)):
         target[...] = plain_dot(normed_one[...], source[...], COLUMNS_COLUMNS).astype(bf16)
     weights.start_twins()
@@ -1450,8 +1460,9 @@
 
     for c in load_w(0):
         c.start()
+    sums.column(0)
+    sums.sides(3)
     weights.sides(0)
-    sums.sides(3)
     other = pl.ds(pl.multiple_of((1 - x) * own_rows, own_rows), own_rows)
     mine = pl.ds(pl.multiple_of(x * own_rows, own_rows), own_rows)
     for c in range(n_chunks):
@@ -1467,6 +1478,7 @@
             total = total + plain_dot(grad_value[here, :], some_v[c % 2], ROWS_ROWS)
             target[:, columns] = total.astype(target.dtype)
     swap(1, sent, received).start()
+    sums.column(1)
     weights.sides(1)
     sums.column(2)
     swap(1, received, received).wait_recv()
@@ -1654,8 +1666,8 @@
                 target[slot, span] = dot_f32(low, whole).astype(bf16)
         row_gate = jnp.concatenate(row_gates, axis=0)
         rows, grad_rows = self.rows.at[slot], self.grad_rows.at[slot]
-        self.pre[0] = dot_f32(rows[...], self.w_gate[...])
-        self.pre[1] = dot_f32(rows[...], self.w_up[...])
+        self.pre[0] = dot_t(rows[...], self.w_gate[...])
+        self.pre[1] = dot_t(rows[...], self.w_up[...])
         self.pre[2] = dot_t(grad_rows[...], self.w_down[...])
         hook(2)
         step = 32
@@ -1706,8 +1718,8 @@
         def combine(c, carry):
             cols = pl.ds(pl.multiple_of(c * column, column), column)
             made = dot_f32(self.hidden[slot, 0], self.w_down[:, cols]).astype(bf16)
-            back = dot_t(self.hidden[slot, 1], self.w_gate[cols, :])
-            back = (back + dot_t(self.hidden[slot, 2], self.w_up[cols, :])).astype(bf16)
+            back = dot_f32(self.hidden[slot, 1], self.w_gate[:, cols])
+            back = (back + dot_f32(self.hidden[slot, 2], self.w_up[:, cols])).astype(bf16)
             for q in range(UNIT):
                 span = slice(q * capacity, (q + 1) * capacity)
                 self.right_out[q, pl.ds(0, capacity), cols] = made[span]
@@ -1805,32 +1817,36 @@
 
     def near(j):
         net.twin_near(j)
+        if j == n_planes - 1:
+            rest.twin_across(j)
         load_unit(2 * j)
 
     def far(j):
         net.twin_far(j)
         rest.twin_corner(j)
-        if j == n_planes - 1:
+        if j >= n_planes - 2:
             rest.twin_side(j)
         load_unit(2 * j + 1)
 
     def over(j):
+        if j >= n_planes - 2:
+            rest.from_side(j)
         if j == n_planes - 1:
-            rest.from_side(j)
+            rest.from_across(j)
         rest.over_x(j)
         rest.over_y(j)
 
     plan = {
         (0, 0): [(net.onward, 1)],
         (0, 2): [(net.corner, 0), (rest.corner, 0), (far, 0), (over, 1)],
-        (0, 3): [(net.relay_of, 2, 0), (net.relay_of, 3, 1)],
-        (1, 0): [(net.sides, 1), (net.onward, 2), (rest.onward_y, 3)],
+        (0, 3): [(net.relay_of, 2, 0), (net.relay_of, 3, 1), (rest.onward_y, 2), (rest.onward_x, 3)],
+        (1, 0): [(net.sides, 1), (net.onward, 2)],
         (1, 2): [(near, 1)],
         (1, 3): [(net.corner, 1), (net.corner_of, 2, 1), (rest.corner, 1)],
-        (2, 0): [(far, 1), (over, 2)],
+        (2, 0): [(far, 1), (over, 2), (rest.onward_y, 3)],
         (2, 3): [(net.sides, 2), (net.relay_of, 3, 0), (net.onward, 3), (net.corner_of, 3, 1)],
-        (3, 0): [(near, 2), (over, 3)],
-        (3, 2): [(net.corner_of, 2, 0), (rest.corner, 2)],
+        (3, 0): [(near, 2)],
+        (3, 2): [(net.corner_of, 2, 0), (rest.corner, 2), (over, 3)],
         (4, 0): [(net.sides, 3), (far, 2)],
         (4, 3): [(net.corner_of, 3, 0), (rest.corner, 3)],
         (5, 0): [(near, 3)],
@@ -1887,7 +1903,7 @@
 def expert_call(own, own_gates, grads, w_gate, w_up, w_down, shared, n_dp, capacity, collective_id):
     own_rows, model = own.shape
     blocks = 2 * n_dp
-    width = w_gate.shape[1]
+    width = w_down.shape[0]
     bf16 = jnp.bfloat16
     rows = n_dp * capacity
     n_planes = n_dp // 4
@@ -2007,7 +2023,7 @@
         shared_hidden,
     ) = (
         expert_call(
-            normed_two, gates_t, cotangent_all, expert_gate_matrix[0], expert_up_matrix[0], expert_down_matrix[0],
+            normed_two, gates_t, cotangent_all, expert_gate_matrix[0].T, expert_up_matrix[0].T, expert_down_matrix[0],
             shared_rows, n_dp, capacity, 2,
         )
     )
@@ -2058,8 +2074,8 @@
         returned[0].T,
         returned[1].T,
         returned[2],
-        expert_gate_gradient[None],
-        expert_up_gradient[None],
+        expert_gate_gradient.T[None],
+        expert_up_gradient.T[None],
         expert_down_gradient[None],
     )
 

time: 613 us -> 583 us (0.951)
  Pallas kernels: 533 us -> 517 us
  local copies, waits for them, and re-layouts: 44.9 us -> 30.1 us
    pallas_call x1, Pallas kernels: 142 us -> 125 us  [front(): pl.pallas_call(functools.partial(front_kernel, n_planes, axes), out_shape...]
    unnamed x61, local copies, waits for them, and re-layouts: 36.9 us -> 20.6 us
    pallas_call x1, Pallas kernels: 133 us -> 143 us  [expert_call(): pl.pallas_call(functools.partial(expert_kernel, n_dp), out_shape=[everyon...]
    pallas_call x1, Pallas kernels: 178 us -> 169 us  [backward(): pl.pallas_call(functools.partial(back_kernel, n_planes, axes), out_shape=...]
  transfers between devices with their start and end apart: 2 -> 2, of which waited for: 0 -> 0; matrix products, arithmetic and copies ran while one was open for 6% -> 2% of each run, Pallas kernels for 53% -> 51%
where the time goes in v5:
time: 583 us; the launch traced here: 574 us
  Pallas kernels  517 us (89%)
  local copies, waits for them, and re-layouts  30.1 us (5%)
  starting transfers between devices  12.8 us (2%)
  other arithmetic  12.2 us (2%)
    pallas_call x1, Pallas kernels, backward(): pl.pallas_call(functools.partial(back_kernel, n_planes, axes), out_shape=...  169 us
    pallas_call x1, Pallas kernels, expert_call(): pl.pallas_call(functools.partial(expert_kernel, n_dp), out_shape=[everyon...  143 us
    pallas_call x1, Pallas kernels, front(): pl.pallas_call(functools.partial(front_kernel, n_planes, axes), out_shape...  125 us
    pallas_call x1, Pallas kernels, sum_everywhere(): pl.pallas_call(functools.partial(sum_kernel, n_planes, n), out_shape=[jax...  80.3 us
    unnamed x61, local copies, waits for them, and re-layouts  20.6 us
  transfers between devices with their start and end apart: 2, of which 0 were waited for; matrix products, arithmetic and copies ran while one was open for 2% of the time, Pallas kernels for 51%

profile of v5, /device:TPU:24, one launch (start us, length us, event | category | flops | bytes accessed | tf_op | source)
XLA Modules:
  0.0 574.2 jit_solution(13128224628701893429)
XLA Ops:
  0.7 1.2 copy.72
  1.9 1.2 copy.71
  3.4 1.1 copy.73
  4.5 6.2 %all-to-all-start = ((bf16[16,3,96,128]{3,2,1,0:T(8,128)(2,1)}), bf16[16,3,96,128]{3,2,1,0:T(8,128)(2,1)S(1)}, u32[]{:S(2)}, u32[]{:S(2)}) async-start(bf16[16,3,96,128]{3,2,1,0:T(8,128)(2,1)} %copy.73), calls=%async_computation | async-start | bytes 2359296 | tf_op jit(solution)/shard_map/all_to_all | solution.py:2017
  12.5 0.8 pad_maximum_fusion.1
  13.3 0.8 fusion.1.refs_10_
  14.1 125.2 %shard_map.280 = (bf16[2048,1024]{1,0:T(8,128)(2,1)}, bf16[2048,256]{1,0:T(8,128)(2,1)}, bf16[2048,256]{1,0:T(8,128)(2,1)}, bf16[1024,2048]{1,0:T(8,128)(2,1)}, ...) custom-call(bf16[128,1024]{1,0:T(8,128)(2,1)} %refs_0_.1, ...), custom_call_target="tpu_custom_call" | custom-call | flops 3221225472 | bytes 67108864 | tf_op jit(solution)/shard_map/pallas_call | solution.py:914
  139.4 1.4 multiply_reduce_fusion.2
  140.7 1.4 slice_convert_fusion
  142.3 1.3 pad.20
  143.7 142.9 %shard_map.281 = (bf16[32,128,2048]{2,1,0:T(8,128)(2,1)}, bf16[32,128,2048]{2,1,0:T(8,128)(2,1)}, bf16[32,128,2048]{2,1,0:T(8,128)(2,1)}, bf16[32,128,2048]{2,1,...) custom-call(bf16[128,2048]{1,0:T(8,128)(2,1)} %get-tuple-element.65., ...), custom_call_target="tpu_custom_call", output_to_operand_aliasing={{1}: (2, {})} | custom-call | tf_op jit(solution)/shard_map/pallas_call | solution.py:1913
  286.6 80.3 %shard_map.282 = (f32[128,2048]{1,0:T(8,128)}, f32[16,128]{1,0:T(8,128)}, f32[704,2048]{1,0:T(8,128)}, f32[704,2048]{1,0:T(8,128)}, f32[704,2048]{1,0:T(8,128)}, /*index=5*/bf16[384,2048]{1,0:T(8,128)(2,1)}) custom-call(bf16[32,128,2048]{2,1,0:T(8,128)(2,1)} %get-tuple-element.68.refs_0_, f32[32,16,128]{2,1,0:T(8,128)} %get-tuple-element.69.refs_1_, ...), custom_call_target="tpu_custom_call" | custom-call | tf_op jit(solution)/shard_map/pallas_call | solution.py:1314
  366.9 1.4 slice.61
  368.8 1.3 copy.75
  370.1 6.6 %all-to-all-start.1 = ((bf16[16,3,96,128]{3,2,1,0:T(8,128)(2,1)}), bf16[16,3,96,128]{3,2,1,0:T(8,128)(2,1)}, u32[]{:S(2)}, u32[]{:S(2)}) async-start(bf16[16,3,96,128]{3,2,1,0:T(8,128)(2,1)} %copy.75), calls=%async_computation.1 | async-start | bytes 2359296 | tf_op jit(solution)/shard_map/all_to_all | solution.py:2062
  377.5 0.7 select_maximum_fusion.refs_16_
  378.2 1.5 fusion.10
  379.7 168.9 %shard_map.283 = (f32[128,1024]{1,0:T(8,128)}, f32[128,256]{1,0:T(8,128)}, f32[128,256]{1,0:T(8,128)}, f32[1024,128]{1,0:T(8,128)}, f32[128,2048]{1,0:T(8,128)}, /*index=5*/f32[24,128]{1,0:T(8,128)}, f32[128,2048]{1,0:T(8,128)}) custom-call(bf16[128,2048]{1,0:T(8,128)(2,1)} %get-tuple-element.178.refs_0_, bf16[256,1024]{1,0:T(8,128)(2,1)} %get-tuple-element.79.refs_1_, ...), custom_call_target="tpu_custom_call" | custom-call | flops 6442450944 | bytes 67108864 | tf_op jit(solution)/shard_map/pallas_call | solution.py:1543
  548.6 1.4 dynamic-slice_bitcast_fusion.1
  550.0 1.4 dynamic-slice_bitcast_fusion
  551.3 2.5 add_convert_fusion
  553.8 1.4 convert_bitcast_fusion
  555.2 1.0 fusion.11
  556.2 1.1 copy.77
  557.3 1.1 copy.78
  558.6 1.0 copy.94
  559.6 0.8 copy.95
  560.4 0.7 copy.96
  561.7 0.8 copy.98
  562.5 6.5 %copy.99 = f32[1,2048,704]{1,2,0:T(8,128)} copy(f32[1,2048,704]{1,2,0:T(8,128)} %bitcast.91) | data formatting | bytes 11534336
  569.0 2.5 copy.100
  571.5 2.5 copy.101
  (77 shorter events, 4.2 us)
Async XLA Ops:
  0.6 10.1 %copy-start = (s32[256,6]{0,1:T(8,128)S(1)}, s32[256,6]{0,1:T(8,128)}, u32[]{:S(2)}) copy-start(s32[256,6]{0,1:T(8,128)} %param.34) | copy-start | bytes 18436
  0.7 2.5 copy-start.9
  4.5 6.9 %copy-start.19 = (s32[1,4]{1,0:T(1,128)S(1)}, s32[1,4]{1,0:T(1,128)}, u32[]{:S(2)}) copy-start(s32[1,4]{1,0:T(1,128)} %param.33) | copy-start | bytes 52
  4.5 7.1 %copy-start.16 = (bf16[64,16]{0,1:T(8,128)(2,1)S(1)}, bf16[64,16]{0,1:T(8,128)(2,1)}, u32[]{:S(2)}) copy-start(bf16[64,16]{0,1:T(8,128)(2,1)} %param.26) | copy-start | bytes 6148
  4.5 7.1 %copy-start.17 = (bf16[64]{0:T(256)(128)(2,1)S(1)}, bf16[64]{0:T(256)(128)(2,1)}, u32[]{:S(2)}) copy-start(bf16[64]{0:T(256)(128)(2,1)} %param.21) | copy-start | bytes 388
  4.5 7.1 %copy-start.18 = (bf16[64]{0:T(256)(128)(2,1)S(1)}, bf16[64]{0:T(256)(128)(2,1)}, u32[]{:S(2)}) copy-start(bf16[64]{0:T(256)(128)(2,1)} %param.20) | copy-start | bytes 388
  4.5 137.7 %all-to-all-start = ((bf16[16,3,96,128]{3,2,1,0:T(8,128)(2,1)}), bf16[16,3,96,128]{3,2,1,0:T(8,128)(2,1)S(1)}, u32[]{:S(2)}, u32[]{:S(2)}) async-start(bf16[16,3,96,128]{3,2,1,0:T(8,128)(2,1)} %copy.73), calls=%async_computation | async-start | bytes 2359296 | tf_op jit(solution)/shard_map/all_to_all | solution.py:2017
  11.8 2.3 copy-start.15
  368.8 7.9 %copy-start.12 = (f32[16,128]{1,0:T(8,128)S(1)}, f32[16,128]{1,0:T(8,128)}, u32[]{:S(2)}) copy-start(f32[16,128]{1,0:T(8,128)} %get-tuple-element.66.refs_1_) | copy-start | bytes 24580
  368.8 7.9 %copy-start.14 = (f32[16,128]{1,0:T(8,128)S(1)}, f32[16,128]{1,0:T(8,128)}, u32[]{:S(2)}) copy-start(f32[16,128]{1,0:T(8,128)} %get-tuple-element.77) | copy-start | bytes 24580
  370.1 6.6 %copy-start.3 = (bf16[128,2048]{1,0:T(8,128)(2,1)S(1)}, bf16[128,2048]{1,0:T(8,128)(2,1)}, u32[]{:S(2)}) copy-start(bf16[128,2048]{1,0:T(8,128)(2,1)} %get-tuple-element.65.refs_0_) | copy-start | bytes 1572868
  370.1 6.8 %copy-start.2 = (f32[128,2048]{1,0:T(8,128)S(1)}, f32[128,2048]{1,0:T(8,128)}, u32[]{:S(2)}) copy-start(f32[128,2048]{1,0:T(8,128)} %get-tuple-element.64) | copy-start | bytes 3145732
  370.1 6.8 %copy-start.4 = (f32[128,2048]{1,0:T(8,128)S(1)}, f32[128,2048]{1,0:T(8,128)}, u32[]{:S(2)}) copy-start(f32[128,2048]{1,0:T(8,128)} %get-tuple-element.76) | copy-start | bytes 3145732
  370.1 6.8 %copy-start.13 = (bf16[32,2048]{1,0:T(8,128)(2,1)S(1)}, bf16[32,2048]{1,0:T(8,128)(2,1)}, u32[]{:S(2)}) copy-start(bf16[32,2048]{1,0:T(8,128)(2,1)} %get-tuple-element.78) | copy-start | bytes 393220
  370.1 183.7 %all-to-all-start.1 = ((bf16[16,3,96,128]{3,2,1,0:T(8,128)(2,1)}), bf16[16,3,96,128]{3,2,1,0:T(8,128)(2,1)}, u32[]{:S(2)}, u32[]{:S(2)}) async-start(bf16[16,3,96,128]{3,2,1,0:T(8,128)(2,1)} %copy.75), calls=%async_computation.1 | async-start | bytes 2359296 | tf_op jit(solution)/shard_map/all_to_all | solution.py:2062
  376.9 1.3 copy-start.6
  555.2 13.8 %slice-start.2 = ((s8[5767168]{0:T(1024)(128)(4,1)}), s8[1572864]{0:T(1024)(128)(4,1)S(1)}, s32[]{:S(2)}) async-start(s8[5767168]{0:T(1024)(128)(4,1)} %bitcast.88), calls=%async_computation.4 | async-start | bytes 3145728
  557.3 1.3 copy-start.5
  558.4 1.1 copy-start.8
  558.6 1.8 copy-start.11
  558.6 2.4 copy-start.10
  558.6 3.1 copy-start.7
  561.7 7.3 %slice-start.3 = ((s8[5767168]{0:T(1024)(128)(4,1)}), s8[4194304]{0:T(1024)(128)(4,1)S(1)}, s32[]{:S(2)}) async-start(s8[5767168]{0:T(1024)(128)(4,1)} %bitcast.88), calls=%async_computation.5 | async-start | bytes 8388608
  561.7 9.8 %slice-start = ((s8[5767168]{0:T(1024)(128)(4,1)}), s8[4194304]{0:T(1024)(128)(4,1)S(1)}, s32[]{:S(2)}) async-start(s8[5767168]{0:T(1024)(128)(4,1)} %bitcast.85), calls=%async_computation.2 | async-start | bytes 8388608
  562.5 9.0 %slice-start.1 = ((s8[5767168]{0:T(1024)(128)(4,1)}), s8[1572864]{0:T(1024)(128)(4,1)S(1)}, s32[]{:S(2)}) async-start(s8[5767168]{0:T(1024)(128)(4,1)} %bitcast.85), calls=%async_computation.3 | async-start | bytes 3145728
  571.5 2.5 copy-start.1

commit v6 on v5

--- a/solution.py
+++ b/solution.py
@@ -485,8 +485,18 @@
             low, high = low + take_low, high - (1 - take_low)
         return order
 
-    def greet(self):
+    def plane(self, k):
+        s = (self.z + k) % self.n_planes
+        return s, (s * 4 + self.dp % 4, self.x)
+
+    def greet(self, all_planes=False):
         barrier = pltpu.get_barrier_semaphore()
+        if all_planes:
+            peers = [self.side, self.twin, self.across] + [self.plane(k)[1] for k in range(1, self.n_planes)]
+            for device in peers:
+                pl.semaphore_signal(barrier, inc=1, device_id=device, device_id_type=MESH)
+            pl.semaphore_wait(barrier, len(peers))
+            return
         fixed = [self.side, self.twin, self.across]
         for device in fixed:
             pl.semaphore_signal(barrier, inc=1, device_id=device, device_id_type=MESH)
@@ -1341,9 +1351,10 @@
     outs, grad_tokens, small_out, out_sum = refs[18 : 18 + n], *refs[18 + n : 21 + n]
     (
         grad_attn, grad_mixed, grad_query, grad_key, grad_value, gq, gk, gv, go, some_p, some_o, some_q, some_k,
-        some_v, sent, received, terms, small_sum, small_in, load, x_send, x_recv,
-    ) = refs[21 + n : 43 + n]
-    scratch = refs[43 + n : -len(inputs) - 1]
+        some_v, sent, received, terms, from_twin, from_side, from_across, quarter, from_planes, load, x_send, x_recv,
+        p_send, p_recv,
+    ) = refs[21 + n : 48 + n]
+    scratch = refs[48 + n : -len(inputs) - 1]
     spot = Spot(n_planes)
     x = spot.x
     bf16, f32 = jnp.bfloat16, jnp.float32
@@ -1359,17 +1370,12 @@
             places.append(a.at[span] if axis == 0 else a.at[:, span])
         return places
 
-    def small_blocks(s, yy, cc, xx):
-        size = small_sum.shape[1]
-        return [terms.at[:, pl.ds(pl.multiple_of(dp_of(s, yy, cc) * size, size), size)]]
-
     def token_blocks(s, yy, cc, xx):
         return [parts.at[dp_of(s, yy, cc) * 2 + xx]]
 
     count = 3 * n + 3
     weights = Reduce(spot, weight_blocks, outs, scratch[:count], False, direct=True)
-    params = Reduce(spot, small_blocks, [small_sum], scratch[count : count + 6], False, direct=True)
-    sums = Reduce(spot, token_blocks, [out_sum], scratch[count + 6 :], True, own_rows // 2, by_z=True)
+    sums = Reduce(spot, token_blocks, [out_sum], scratch[count:], True, own_rows // 2, by_z=True)
 
     def swap(i, src, dst):
         return pltpu.make_async_remote_copy(
@@ -1377,10 +1383,59 @@
             device_id=spot.across, device_id_type=MESH,
         )
 
+    def hop(i, src, dst, device):
+        return pltpu.make_async_remote_copy(
+            src_ref=src, dst_ref=dst, send_sem=p_send.at[i], recv_sem=p_recv.at[i],
+            device_id=device, device_id_type=MESH,
+        )
+
+    lanes = terms.shape[1]
+
+    def of_core(c):
+        return terms.at[:, pl.ds(pl.multiple_of(c * (lanes // 2), lanes // 2), lanes // 2)]
+
+    def of_side(y):
+        start = spot.core * (lanes // 2) + y * (lanes // 4)
+        return terms.at[:, pl.ds(pl.multiple_of(start, lanes // 4), lanes // 4)]
+
+    def of_plane(s):
+        size = lanes // 4 // n_planes
+        return quarter.at[:, pl.ds(pl.multiple_of(s * size, size), size)]
+
+    hops = [
+        hop(0, of_core(1 - spot.core), from_twin, spot.twin),
+        hop(1, of_side(1 - spot.y), from_side, spot.side),
+        hop(2, of_side(spot.y), from_across, spot.across),
+    ]
+    for k in range(1, n_planes):
+        s, device = spot.plane(k)
+        hops.append(hop(2 + k, of_plane(s), from_planes.at[k - 1], device))
+
+    def small_step(i):
+        if i > 0:
+            for h in hops[i - 1 : i] if i < 4 else hops[3:]:
+                h.wait_recv()
+        if i == 1:
+            mine = of_core(spot.core)
+            mine[...] = mine[...] + from_twin[...]
+        if i == 2:
+            mine = of_side(spot.y)
+            mine[...] = mine[...] + from_side[...]
+        if i == 3:
+            quarter[...] = of_side(spot.y)[...] + from_across[...]
+        if i == 4:
+            total = of_plane(spot.z)[...]
+            for k in range(n_planes - 1):
+                total = total + from_planes[k]
+            small_out[...] = total
+            return
+        for h in hops[i : i + 1] if i < 3 else hops[3:]:
+            h.start()
+
     own = pltpu.make_async_copy(grad_own, grad_attn.at[x], load.at[4, 0])
     own.start()
     sums.start_loads()
-    spot.greet()
+    spot.greet(True)
     swap(0, grad_own, grad_attn.at[x]).start()
     sums.start_twins()
     fetched = [pltpu.make_async_copy(a, b, held_load.at[i]) for i, (a, b) in enumerate(zip(inputs, held))]
@@ -1495,26 +1550,27 @@
         total = total + jnp.sum(grad * rows_in * size, axis=0, keepdims=True)
         grad_tokens[span, :] = size * weighted - rows_in * (size * size * size) * inner + grad_residual[span, :]
     place = small.shape[0] - 8
-    terms[pl.ds(place, 1), :] = total
-    params.start_twins()
+    size = lanes // 4 // n_planes
+    for i in range(4 * n_planes):
+        at = (i % 2 * 2 + i // 2 % 2) * n_planes + i // 4
+        terms[pl.ds(place, 1), pl.ds(at * size, size)] = total[:, i * size : (i + 1) * size]
+    small_step(0)
     weights.column(0)
+    small_step(1)
     weights.sides(2)
-    params.sides(0)
+    small_step(2)
     weights.column(1)
+    small_step(3)
     weights.sides(3)
     sums.column(3)
-    for j in range(1, n_planes):
-        params.sides(j)
-        params.column(j - 1)
     weights.column(2)
-    params.column(n_planes - 1)
+    small_step(4)
     weights.column(3)
-    swap(2, small_sum, small_in).start()
-    swap(2, small_sum, small_in).wait()
-    small_out[...] = small_sum[...] + small_in[...]
+    for h in hops:
+        h.wait_send()
     swap(0, grad_own, grad_attn.at[x]).wait_send()
     swap(1, sent, received).wait_send()
-    for each in (weights, params, sums):
+    for each in (weights, sums):
         each.close()
 
 
@@ -1562,14 +1618,18 @@
             vmem_ref((own_rows, model), bf16),
             vmem_ref((own_rows, model), bf16),
             vmem_ref(small.shape, f32),
-            vmem_ref(tile, f32),
-            vmem_ref(tile, f32),
+            vmem_ref((small.shape[0], model // 2), f32),
+            vmem_ref((small.shape[0], model // 4), f32),
+            vmem_ref((small.shape[0], model // 4), f32),
+            vmem_ref((small.shape[0], model // 4), f32),
+            vmem_ref((n_planes - 1,) + tile, f32),
             dma((5, 2)),
             dma((3,)),
             dma((3,)),
+            dma((2 + n_planes,)),
+            dma((2 + n_planes,)),
         ]
         + Reduce.scratch(shapes, [bf16] * n, n_planes, False, direct=True)
-        + Reduce.scratch([tile], [f32], n_planes, False, direct=True)
         + Reduce.scratch([block], [parts.dtype], n_planes, True, block[0] // 2, by_z=True)
         + [
             vmem_ref(a.shape, a.dtype)
@@ -1755,7 +1815,10 @@
         b = dp_of(s, yy, cc) * 2 + xx
         if part == ALL:
             return [grads.at[b]]
-        return [grads.at[b, pl.ds(0 if part == FIRST else half, half)]]
+        some = 5 * own.shape[0] // 8
+        if part == FIRST:
+            return [grads.at[b, pl.ds(0, some)]]
+        return [grads.at[b, pl.ds(some, own.shape[0] - some)]]
 
     kept = [
         pltpu.make_async_copy(a, v, local.at[i])
@@ -2051,6 +2114,8 @@
     grad_residual, grad_gain_two = rms_back(grad_normed_two, residual, scale_two, second_gain)
     grad_residual = grad_residual + cotangent.astype(f32)
     small_grads = jnp.concatenate([grad_router_part.T, jnp.zeros((8, model_dim), f32).at[1].set(grad_gain_two)])
+    by_place = small_grads.reshape(-1, n_dp // 4, 2, 2, 2 * width).transpose(0, 3, 2, 1, 4)
+    small_grads = by_place.reshape(small_grads.shape)
     *weight_grads, grad_inputs, small_sums, ffn_own = backward(
         grad_residual.astype(bf16), mixed_heads, full_one, rows_of_query, key_rows, rows_of_value, attn_probs,
         [query_all, key_all, value_all, out_all], axes, cosine, sine, tokens, grad_residual, first_gain[None],

time: 583 us -> 559 us (0.959)
  Pallas kernels: 517 us -> 493 us
    pallas_call x1, Pallas kernels: 169 us -> 149 us  [backward(): pl.pallas_call(functools.partial(back_kernel, n_planes, axes), out_shape=...]
  transfers between devices with their start and end apart: 2 -> 2, of which waited for: 0 -> 0; matrix products, arithmetic and copies ran while one was open for 2% -> 3% of each run, Pallas kernels for 51% -> 50%
where the time goes in v6:
time: 559 us; the launch traced here: 550 us
  Pallas kernels  493 us (88%)
  local copies, waits for them, and re-layouts  31.1 us (6%)
  starting transfers between devices  12.5 us (2%)
  other arithmetic  11.5 us (2%)
    pallas_call x1, Pallas kernels, backward(): pl.pallas_call(functools.partial(back_kernel, n_planes, axes), out_shape=...  149 us
    pallas_call x1, Pallas kernels, expert_call(): pl.pallas_call(functools.partial(expert_kernel, n_dp), out_shape=[everyon...  138 us
    pallas_call x1, Pallas kernels, front(): pl.pallas_call(functools.partial(front_kernel, n_planes, axes), out_shape...  125 us
    pallas_call x1, Pallas kernels, sum_everywhere(): pl.pallas_call(functools.partial(sum_kernel, n_planes, n), out_shape=[jax...  80.2 us
    unnamed x61, local copies, waits for them, and re-layouts  20.6 us
  transfers between devices with their start and end apart: 2, of which 0 were waited for; matrix products, arithmetic and copies ran while one was open for 3% of the time, Pallas kernels for 50%

profile of v6, /device:TPU:24, one launch (start us, length us, event | category | flops | bytes accessed | tf_op | source)
XLA Modules:
  0.0 550.1 jit_solution(8383030410465851513)
XLA Ops:
  0.7 1.2 copy.77
  1.9 1.2 copy.76
  3.4 1.1 copy.78
  4.5 6.2 %all-to-all-start = ((bf16[16,3,96,128]{3,2,1,0:T(8,128)(2,1)}), bf16[16,3,96,128]{3,2,1,0:T(8,128)(2,1)S(1)}, u32[]{:S(2)}, u32[]{:S(2)}) async-start(bf16[16,3,96,128]{3,2,1,0:T(8,128)(2,1)} %copy.78), calls=%async_computation | async-start | bytes 2359296 | tf_op jit(solution)/shard_map/all_to_all | solution.py:2080
  12.5 0.8 pad_maximum_fusion.1
  13.3 0.8 fusion.1.refs_10_
  14.1 125.2 %shard_map.280 = (bf16[2048,1024]{1,0:T(8,128)(2,1)}, bf16[2048,256]{1,0:T(8,128)(2,1)}, bf16[2048,256]{1,0:T(8,128)(2,1)}, bf16[1024,2048]{1,0:T(8,128)(2,1)}, ...) custom-call(bf16[128,1024]{1,0:T(8,128)(2,1)} %refs_0_.1, ...), custom_call_target="tpu_custom_call" | custom-call | flops 3221225472 | bytes 67108864 | tf_op jit(solution)/shard_map/pallas_call | solution.py:924
  139.4 1.4 multiply_reduce_fusion.2
  140.7 1.4 slice_convert_fusion
  142.3 1.3 pad.20
  143.7 138.5 %shard_map.281 = (bf16[32,128,2048]{2,1,0:T(8,128)(2,1)}, bf16[32,128,2048]{2,1,0:T(8,128)(2,1)}, bf16[32,128,2048]{2,1,0:T(8,128)(2,1)}, bf16[32,128,2048]{2,1,...) custom-call(bf16[128,2048]{1,0:T(8,128)(2,1)} %get-tuple-element.65., ...), custom_call_target="tpu_custom_call", output_to_operand_aliasing={{1}: (2, {})} | custom-call | tf_op jit(solution)/shard_map/pallas_call | solution.py:1976
  282.1 80.2 %shard_map.282 = (f32[128,2048]{1,0:T(8,128)}, f32[16,128]{1,0:T(8,128)}, f32[704,2048]{1,0:T(8,128)}, f32[704,2048]{1,0:T(8,128)}, f32[704,2048]{1,0:T(8,128)}, /*index=5*/bf16[384,2048]{1,0:T(8,128)(2,1)}) custom-call(bf16[32,128,2048]{2,1,0:T(8,128)(2,1)} %get-tuple-element.68.refs_0_, f32[32,16,128]{2,1,0:T(8,128)} %get-tuple-element.69.refs_1_, ...), custom_call_target="tpu_custom_call" | custom-call | tf_op jit(solution)/shard_map/pallas_call | solution.py:1324
  362.3 1.4 slice.61
  364.2 1.3 copy.81
  365.5 6.2 %all-to-all-start.1 = ((bf16[16,3,96,128]{3,2,1,0:T(8,128)(2,1)}), bf16[16,3,96,128]{3,2,1,0:T(8,128)(2,1)}, u32[]{:S(2)}, u32[]{:S(2)}) async-start(bf16[16,3,96,128]{3,2,1,0:T(8,128)(2,1)} %copy.81), calls=%async_computation.1 | async-start | bytes 2359296 | tf_op jit(solution)/shard_map/all_to_all | solution.py:2127
  372.9 0.8 reshape.161.refs_16_
  373.6 1.5 fusion.10
  375.2 149.3 %shard_map.283 = (f32[128,1024]{1,0:T(8,128)}, f32[128,256]{1,0:T(8,128)}, f32[128,256]{1,0:T(8,128)}, f32[1024,128]{1,0:T(8,128)}, f32[128,2048]{1,0:T(8,128)}, /*index=5*/f32[24,128]{1,0:T(8,128)}, f32[128,2048]{1,0:T(8,128)}) custom-call(bf16[128,2048]{1,0:T(8,128)(2,1)} %get-tuple-element.178.refs_0_, bf16[256,1024]{1,0:T(8,128)(2,1)} %get-tuple-element.79.refs_1_, ...), custom_call_target="tpu_custom_call" | custom-call | flops 6442450944 | bytes 67108864 | tf_op jit(solution)/shard_map/pallas_call | solution.py:1599
  524.5 1.4 dynamic-slice_bitcast_fusion.1
  525.9 1.4 dynamic-slice_bitcast_fusion
  527.2 2.5 add_convert_fusion
  529.7 1.4 convert_bitcast_fusion
  531.1 1.0 fusion.11
  532.1 1.1 copy.83
  533.2 1.1 copy.84
  534.5 1.0 copy.102
  535.5 0.8 copy.103
  536.3 0.7 copy.104
  537.6 0.8 copy.106
  538.4 6.5 %copy.107 = f32[1,2048,704]{1,2,0:T(8,128)} copy(f32[1,2048,704]{1,2,0:T(8,128)} %bitcast.94) | data formatting | bytes 11534336
  544.9 2.5 copy.108
  547.4 2.5 copy.109
  (80 shorter events, 4.5 us)
Async XLA Ops:
  0.6 10.1 %copy-start = (s32[256,6]{0,1:T(8,128)S(1)}, s32[256,6]{0,1:T(8,128)}, u32[]{:S(2)}) copy-start(s32[256,6]{0,1:T(8,128)} %param.34) | copy-start | bytes 18436
  0.7 2.5 copy-start.9
  4.5 6.9 %copy-start.19 = (s32[1,4]{1,0:T(1,128)S(1)}, s32[1,4]{1,0:T(1,128)}, u32[]{:S(2)}) copy-start(s32[1,4]{1,0:T(1,128)} %param.33) | copy-start | bytes 52
  4.5 7.1 %copy-start.16 = (bf16[64,16]{0,1:T(8,128)(2,1)S(1)}, bf16[64,16]{0,1:T(8,128)(2,1)}, u32[]{:S(2)}) copy-start(bf16[64,16]{0,1:T(8,128)(2,1)} %param.26) | copy-start | bytes 6148
  4.5 7.1 %copy-start.17 = (bf16[64]{0:T(256)(128)(2,1)S(1)}, bf16[64]{0:T(256)(128)(2,1)}, u32[]{:S(2)}) copy-start(bf16[64]{0:T(256)(128)(2,1)} %param.21) | copy-start | bytes 388
  4.5 7.1 %copy-start.18 = (bf16[64]{0:T(256)(128)(2,1)S(1)}, bf16[64]{0:T(256)(128)(2,1)}, u32[]{:S(2)}) copy-start(bf16[64]{0:T(256)(128)(2,1)} %param.20) | copy-start | bytes 388
  4.5 137.7 %all-to-all-start = ((bf16[16,3,96,128]{3,2,1,0:T(8,128)(2,1)}), bf16[16,3,96,128]{3,2,1,0:T(8,128)(2,1)S(1)}, u32[]{:S(2)}, u32[]{:S(2)}) async-start(bf16[16,3,96,128]{3,2,1,0:T(8,128)(2,1)} %copy.78), calls=%async_computation | async-start | bytes 2359296 | tf_op jit(solution)/shard_map/all_to_all | solution.py:2080
  11.8 2.3 copy-start.15
  364.2 7.6 %copy-start.12 = (f32[16,128]{1,0:T(8,128)S(1)}, f32[16,128]{1,0:T(8,128)}, u32[]{:S(2)}) copy-start(f32[16,128]{1,0:T(8,128)} %get-tuple-element.66.refs_1_) | copy-start | bytes 24580
  364.2 7.6 %copy-start.14 = (f32[16,128]{1,0:T(8,128)S(1)}, f32[16,128]{1,0:T(8,128)}, u32[]{:S(2)}) copy-start(f32[16,128]{1,0:T(8,128)} %get-tuple-element.77) | copy-start | bytes 24580
  365.5 6.3 %copy-start.3 = (bf16[128,2048]{1,0:T(8,128)(2,1)S(1)}, bf16[128,2048]{1,0:T(8,128)(2,1)}, u32[]{:S(2)}) copy-start(bf16[128,2048]{1,0:T(8,128)(2,1)} %get-tuple-element.65.refs_0_) | copy-start | bytes 1572868
  365.5 6.5 %copy-start.2 = (f32[128,2048]{1,0:T(8,128)S(1)}, f32[128,2048]{1,0:T(8,128)}, u32[]{:S(2)}) copy-start(f32[128,2048]{1,0:T(8,128)} %get-tuple-element.64) | copy-start | bytes 3145732
  365.5 6.5 %copy-start.4 = (f32[128,2048]{1,0:T(8,128)S(1)}, f32[128,2048]{1,0:T(8,128)}, u32[]{:S(2)}) copy-start(f32[128,2048]{1,0:T(8,128)} %get-tuple-element.76) | copy-start | bytes 3145732
  365.5 6.5 %copy-start.13 = (bf16[32,2048]{1,0:T(8,128)(2,1)S(1)}, bf16[32,2048]{1,0:T(8,128)(2,1)}, u32[]{:S(2)}) copy-start(bf16[32,2048]{1,0:T(8,128)(2,1)} %get-tuple-element.78) | copy-start | bytes 393220
  365.5 164.2 %all-to-all-start.1 = ((bf16[16,3,96,128]{3,2,1,0:T(8,128)(2,1)}), bf16[16,3,96,128]{3,2,1,0:T(8,128)(2,1)}, u32[]{:S(2)}, u32[]{:S(2)}) async-start(bf16[16,3,96,128]{3,2,1,0:T(8,128)(2,1)} %copy.81), calls=%async_computation.1 | async-start | bytes 2359296 | tf_op jit(solution)/shard_map/all_to_all | solution.py:2127
  372.6 1.0 copy-start.6
  531.1 13.8 %slice-start.2 = ((s8[5767168]{0:T(1024)(128)(4,1)}), s8[1572864]{0:T(1024)(128)(4,1)S(1)}, s32[]{:S(2)}) async-start(s8[5767168]{0:T(1024)(128)(4,1)} %bitcast.91), calls=%async_computation.4 | async-start | bytes 3145728
  533.2 1.3 copy-start.5
  534.3 1.1 copy-start.8
  534.5 1.8 copy-start.11
  534.5 2.4 copy-start.10
  534.5 3.1 copy-start.7
  537.6 7.3 %slice-start.3 = ((s8[5767168]{0:T(1024)(128)(4,1)}), s8[4194304]{0:T(1024)(128)(4,1)S(1)}, s32[]{:S(2)}) async-start(s8[5767168]{0:T(1024)(128)(4,1)} %bitcast.91), calls=%async_computation.5 | async-start | bytes 8388608
  537.6 9.8 %slice-start = ((s8[5767168]{0:T(1024)(128)(4,1)}), s8[4194304]{0:T(1024)(128)(4,1)S(1)}, s32[]{:S(2)}) async-start(s8[5767168]{0:T(1024)(128)(4,1)} %bitcast.88), calls=%async_computation.2 | async-start | bytes 8388608
  538.4 9.0 %slice-start.1 = ((s8[5767168]{0:T(1024)(128)(4,1)}), s8[1572864]{0:T(1024)(128)(4,1)S(1)}, s32[]{:S(2)}) async-start(s8[5767168]{0:T(1024)(128)(4,1)} %bitcast.88), calls=%async_computation.3 | async-start | bytes 3145728
  547.4 2.5 copy-start.1

commit v7 on v6

--- a/solution.py
+++ b/solution.py
@@ -851,7 +851,6 @@
     net.onward_y(1)
     net.relay_of(2, 0)
     net.relay_of(3, 1)
-    net.onward_x(2)
     net.onward_twin(2)
     net.from_across(1)
     may = allowed[...] > 0.0
@@ -874,7 +873,6 @@
     net.relay_of(3, 0)
     net.onward_twin(3)
     net.from_side(1)
-    net.from_across(2)
     swap(2, received, received).wait_recv()
     second_gain = params[experts + 1 : experts + 2, :].astype(f32)
     for r in range(own_rows // step):
@@ -891,7 +889,7 @@
 
     for j in range(n_planes):
         net.twin_own(j)
-        if j < n_planes - 1:
+        if j < n_planes - 2:
             net.twin_across(j)
         if j < n_planes - 2:
             net.twin_side(j)
@@ -1815,7 +1813,7 @@
         b = dp_of(s, yy, cc) * 2 + xx
         if part == ALL:
             return [grads.at[b]]
-        some = 5 * own.shape[0] // 8
+        some = own.shape[0] // 2
         if part == FIRST:
             return [grads.at[b, pl.ds(0, some)]]
         return [grads.at[b, pl.ds(some, own.shape[0] - some)]]
@@ -1880,7 +1878,7 @@
 
     def near(j):
         net.twin_near(j)
-        if j == n_planes - 1:
+        if j >= n_planes - 2:
             rest.twin_across(j)
         load_unit(2 * j)
 
@@ -1894,16 +1892,15 @@
     def over(j):
         if j >= n_planes - 2:
             rest.from_side(j)
-        if j == n_planes - 1:
             rest.from_across(j)
         rest.over_x(j)
         rest.over_y(j)
 
     plan = {
         (0, 0): [(net.onward, 1)],
-        (0, 2): [(net.corner, 0), (rest.corner, 0), (far, 0), (over, 1)],
-        (0, 3): [(net.relay_of, 2, 0), (net.relay_of, 3, 1), (rest.onward_y, 2), (rest.onward_x, 3)],
-        (1, 0): [(net.sides, 1), (net.onward, 2)],
+        (0, 2): [(net.corner, 0), (rest.corner, 0), (far, 0), (over, 1), (rest.onward_x, 2)],
+        (0, 3): [(net.relay_of, 2, 0), (net.relay_of, 3, 1), (rest.onward_y, 2)],
+        (1, 0): [(net.sides, 1), (net.onward, 2), (rest.onward_x, 3)],
         (1, 2): [(near, 1)],
         (1, 3): [(net.corner, 1), (net.corner_of, 2, 1), (rest.corner, 1)],
         (2, 0): [(far, 1), (over, 2), (rest.onward_y, 3)],

time: 559 us -> 555 us (level)
    pallas_call x1, Pallas kernels: 125 us -> 116 us  [front(): pl.pallas_call(functools.partial(front_kernel, n_planes, axes), out_shape...]
  transfers between devices with their start and end apart: 2 -> 2, of which waited for: 0 -> 0; matrix products, arithmetic and copies ran while one was open for 3% -> 3% of each run, Pallas kernels for 50% -> 49%
where the time goes in v7:
time: 555 us; the launch traced here: 547 us
  Pallas kernels  490 us (88%)
  local copies, waits for them, and re-layouts  31.1 us (6%)
  starting transfers between devices  12.6 us (2%)
  other arithmetic  11.5 us (2%)
    pallas_call x1, Pallas kernels, backward(): pl.pallas_call(functools.partial(back_kernel, n_planes, axes), out_shape=...  150 us
    pallas_call x1, Pallas kernels, expert_call(): pl.pallas_call(functools.partial(expert_kernel, n_dp), out_shape=[everyon...  144 us
    pallas_call x1, Pallas kernels, front(): pl.pallas_call(functools.partial(front_kernel, n_planes, axes), out_shape...  116 us
    pallas_call x1, Pallas kernels, sum_everywhere(): pl.pallas_call(functools.partial(sum_kernel, n_planes, n), out_shape=[jax...  79.7 us
    unnamed x61, local copies, waits for them, and re-layouts  20.6 us
  transfers between devices with their start and end apart: 2, of which 0 were waited for; matrix products, arithmetic and copies ran while one was open for 3% of the time, Pallas kernels for 49%

profile of v7, /device:TPU:24, one launch (start us, length us, event | category | flops | bytes accessed | tf_op | source)
XLA Modules:
  0.0 546.7 jit_solution(126827139257187202)
XLA Ops:
  0.7 1.2 copy.77
  1.9 1.2 copy.76
  3.4 1.1 copy.78
  4.5 6.2 %all-to-all-start = ((bf16[16,3,96,128]{3,2,1,0:T(8,128)(2,1)}), bf16[16,3,96,128]{3,2,1,0:T(8,128)(2,1)S(1)}, u32[]{:S(2)}, u32[]{:S(2)}) async-start(bf16[16,3,96,128]{3,2,1,0:T(8,128)(2,1)} %copy.78), calls=%async_computation | async-start | bytes 2359296 | tf_op jit(solution)/shard_map/all_to_all | solution.py:2077
  12.5 0.8 pad_maximum_fusion.1
  13.3 0.8 fusion.1.refs_10_
  14.1 116.0 %shard_map.280 = (bf16[2048,1024]{1,0:T(8,128)(2,1)}, bf16[2048,256]{1,0:T(8,128)(2,1)}, bf16[2048,256]{1,0:T(8,128)(2,1)}, bf16[1024,2048]{1,0:T(8,128)(2,1)}, ...) custom-call(bf16[128,1024]{1,0:T(8,128)(2,1)} %refs_0_.1, ...), custom_call_target="tpu_custom_call" | custom-call | flops 3221225472 | bytes 67108864 | tf_op jit(solution)/shard_map/pallas_call | solution.py:922
  130.1 1.4 multiply_reduce_fusion.2
  131.5 1.4 slice_convert_fusion
  133.1 1.3 pad.20
  134.4 144.0 %shard_map.281 = (bf16[32,128,2048]{2,1,0:T(8,128)(2,1)}, bf16[32,128,2048]{2,1,0:T(8,128)(2,1)}, bf16[32,128,2048]{2,1,0:T(8,128)(2,1)}, bf16[32,128,2048]{2,1,...) custom-call(bf16[128,2048]{1,0:T(8,128)(2,1)} %get-tuple-element.65., ...), custom_call_target="tpu_custom_call", output_to_operand_aliasing={{1}: (2, {})} | custom-call | tf_op jit(solution)/shard_map/pallas_call | solution.py:1973
  278.4 79.7 %shard_map.282 = (f32[128,2048]{1,0:T(8,128)}, f32[16,128]{1,0:T(8,128)}, f32[704,2048]{1,0:T(8,128)}, f32[704,2048]{1,0:T(8,128)}, f32[704,2048]{1,0:T(8,128)}, /*index=5*/bf16[384,2048]{1,0:T(8,128)(2,1)}) custom-call(bf16[32,128,2048]{2,1,0:T(8,128)(2,1)} %get-tuple-element.68.refs_0_, f32[32,16,128]{2,1,0:T(8,128)} %get-tuple-element.69.refs_1_, ...), custom_call_target="tpu_custom_call" | custom-call | tf_op jit(solution)/shard_map/pallas_call | solution.py:1322
  358.1 1.4 slice.61
  360.0 1.3 copy.81
  361.3 6.4 %all-to-all-start.1 = ((bf16[16,3,96,128]{3,2,1,0:T(8,128)(2,1)}), bf16[16,3,96,128]{3,2,1,0:T(8,128)(2,1)}, u32[]{:S(2)}, u32[]{:S(2)}) async-start(bf16[16,3,96,128]{3,2,1,0:T(8,128)(2,1)} %copy.81), calls=%async_computation.1 | async-start | bytes 2359296 | tf_op jit(solution)/shard_map/all_to_all | solution.py:2124
  368.8 0.8 reshape.161.refs_16_
  369.6 1.5 fusion.10
  371.1 150.0 %shard_map.283 = (f32[128,1024]{1,0:T(8,128)}, f32[128,256]{1,0:T(8,128)}, f32[128,256]{1,0:T(8,128)}, f32[1024,128]{1,0:T(8,128)}, f32[128,2048]{1,0:T(8,128)}, /*index=5*/f32[24,128]{1,0:T(8,128)}, f32[128,2048]{1,0:T(8,128)}) custom-call(bf16[128,2048]{1,0:T(8,128)(2,1)} %get-tuple-element.178.refs_0_, bf16[256,1024]{1,0:T(8,128)(2,1)} %get-tuple-element.79.refs_1_, ...), custom_call_target="tpu_custom_call" | custom-call | flops 6442450944 | bytes 67108864 | tf_op jit(solution)/shard_map/pallas_call | solution.py:1597
  521.1 1.4 dynamic-slice_bitcast_fusion.1
  522.4 1.4 dynamic-slice_bitcast_fusion
  523.8 2.5 add_convert_fusion
  526.3 1.4 convert_bitcast_fusion
  527.7 1.0 fusion.11
  528.7 1.1 copy.83
  529.8 1.1 copy.84
  531.1 1.0 copy.102
  532.1 0.8 copy.103
  532.9 0.7 copy.104
  534.2 0.8 copy.106
  535.0 6.5 %copy.107 = f32[1,2048,704]{1,2,0:T(8,128)} copy(f32[1,2048,704]{1,2,0:T(8,128)} %bitcast.94) | data formatting | bytes 11534336
  541.4 2.5 copy.108
  544.0 2.5 copy.109
  (80 shorter events, 4.5 us)
Async XLA Ops:
  0.6 10.1 %copy-start = (s32[256,6]{0,1:T(8,128)S(1)}, s32[256,6]{0,1:T(8,128)}, u32[]{:S(2)}) copy-start(s32[256,6]{0,1:T(8,128)} %param.34) | copy-start | bytes 18436
  0.7 2.5 copy-start.9
  4.5 6.9 %copy-start.19 = (s32[1,4]{1,0:T(1,128)S(1)}, s32[1,4]{1,0:T(1,128)}, u32[]{:S(2)}) copy-start(s32[1,4]{1,0:T(1,128)} %param.33) | copy-start | bytes 52
  4.5 7.1 %copy-start.16 = (bf16[64,16]{0,1:T(8,128)(2,1)S(1)}, bf16[64,16]{0,1:T(8,128)(2,1)}, u32[]{:S(2)}) copy-start(bf16[64,16]{0,1:T(8,128)(2,1)} %param.26) | copy-start | bytes 6148
  4.5 7.1 %copy-start.17 = (bf16[64]{0:T(256)(128)(2,1)S(1)}, bf16[64]{0:T(256)(128)(2,1)}, u32[]{:S(2)}) copy-start(bf16[64]{0:T(256)(128)(2,1)} %param.21) | copy-start | bytes 388
  4.5 7.1 %copy-start.18 = (bf16[64]{0:T(256)(128)(2,1)S(1)}, bf16[64]{0:T(256)(128)(2,1)}, u32[]{:S(2)}) copy-start(bf16[64]{0:T(256)(128)(2,1)} %param.20) | copy-start | bytes 388
  4.5 128.5 %all-to-all-start = ((bf16[16,3,96,128]{3,2,1,0:T(8,128)(2,1)}), bf16[16,3,96,128]{3,2,1,0:T(8,128)(2,1)S(1)}, u32[]{:S(2)}, u32[]{:S(2)}) async-start(bf16[16,3,96,128]{3,2,1,0:T(8,128)(2,1)} %copy.78), calls=%async_computation | async-start | bytes 2359296 | tf_op jit(solution)/shard_map/all_to_all | solution.py:2077
  11.8 2.3 copy-start.15
  360.0 7.7 %copy-start.12 = (f32[16,128]{1,0:T(8,128)S(1)}, f32[16,128]{1,0:T(8,128)}, u32[]{:S(2)}) copy-start(f32[16,128]{1,0:T(8,128)} %get-tuple-element.66.refs_1_) | copy-start | bytes 24580
  360.0 7.7 %copy-start.14 = (f32[16,128]{1,0:T(8,128)S(1)}, f32[16,128]{1,0:T(8,128)}, u32[]{:S(2)}) copy-start(f32[16,128]{1,0:T(8,128)} %get-tuple-element.77) | copy-start | bytes 24580
  361.3 6.5 %copy-start.3 = (bf16[128,2048]{1,0:T(8,128)(2,1)S(1)}, bf16[128,2048]{1,0:T(8,128)(2,1)}, u32[]{:S(2)}) copy-start(bf16[128,2048]{1,0:T(8,128)(2,1)} %get-tuple-element.65.refs_0_) | copy-start | bytes 1572868
  361.3 6.6 %copy-start.2 = (f32[128,2048]{1,0:T(8,128)S(1)}, f32[128,2048]{1,0:T(8,128)}, u32[]{:S(2)}) copy-start(f32[128,2048]{1,0:T(8,128)} %get-tuple-element.64) | copy-start | bytes 3145732
  361.3 6.6 %copy-start.4 = (f32[128,2048]{1,0:T(8,128)S(1)}, f32[128,2048]{1,0:T(8,128)}, u32[]{:S(2)}) copy-start(f32[128,2048]{1,0:T(8,128)} %get-tuple-element.76) | copy-start | bytes 3145732
  361.3 6.6 %copy-start.13 = (bf16[32,2048]{1,0:T(8,128)(2,1)S(1)}, bf16[32,2048]{1,0:T(8,128)(2,1)}, u32[]{:S(2)}) copy-start(bf16[32,2048]{1,0:T(8,128)(2,1)} %get-tuple-element.78) | copy-start | bytes 393220
  361.3 164.9 %all-to-all-start.1 = ((bf16[16,3,96,128]{3,2,1,0:T(8,128)(2,1)}), bf16[16,3,96,128]{3,2,1,0:T(8,128)(2,1)}, u32[]{:S(2)}, u32[]{:S(2)}) async-start(bf16[16,3,96,128]{3,2,1,0:T(8,128)(2,1)} %copy.81), calls=%async_computation.1 | async-start | bytes 2359296 | tf_op jit(solution)/shard_map/all_to_all | solution.py:2124
  368.5 1.0 copy-start.6
  527.6 13.8 %slice-start.2 = ((s8[5767168]{0:T(1024)(128)(4,1)}), s8[1572864]{0:T(1024)(128)(4,1)S(1)}, s32[]{:S(2)}) async-start(s8[5767168]{0:T(1024)(128)(4,1)} %bitcast.91), calls=%async_computation.4 | async-start | bytes 3145728
  529.8 1.3 copy-start.5
  530.9 1.1 copy-start.8
  531.1 1.8 copy-start.11
  531.1 2.4 copy-start.10
  531.1 3.1 copy-start.7
  534.2 7.3 %slice-start.3 = ((s8[5767168]{0:T(1024)(128)(4,1)}), s8[4194304]{0:T(1024)(128)(4,1)S(1)}, s32[]{:S(2)}) async-start(s8[5767168]{0:T(1024)(128)(4,1)} %bitcast.91), calls=%async_computation.5 | async-start | bytes 8388608
  534.2 9.8 %slice-start = ((s8[5767168]{0:T(1024)(128)(4,1)}), s8[4194304]{0:T(1024)(128)(4,1)S(1)}, s32[]{:S(2)}) async-start(s8[5767168]{0:T(1024)(128)(4,1)} %bitcast.88), calls=%async_computation.2 | async-start | bytes 8388608
  535.0 9.0 %slice-start.1 = ((s8[5767168]{0:T(1024)(128)(4,1)}), s8[1572864]{0:T(1024)(128)(4,1)S(1)}, s32[]{:S(2)}) async-start(s8[5767168]{0:T(1024)(128)(4,1)} %bitcast.88), calls=%async_computation.3 | async-start | bytes 3145728
  544.0 2.5 copy-start.1
